TPU v7x, 32 devices: a whole 2x2x4 slice. The times are simulated.
32 devices in a mesh: row: 4 (over y, core), col: 4 (over z), depth: 2 (over x).
Axes of the slice: x: 2, y: 2, z: 4, core: 2. Of those that a mesh axis runs over, the one named last changes fastest.
Arguments:
- x_blocks: bfloat16 [64, 8, 128, 128], P(('row', 'col'), 'depth'), may hold values from -2 to 2
- col_slot: int32 [64, 8], P(('row', 'col'), 'depth'), may hold values from 0 to 3
- out_pos: int32 [4, 4, 192, 2], P('row', 'col'), may hold values from 0 to 15, as said below
- out_count: int32 [4, 4], P('row', 'col'), may hold values from 48 to 192, as said below
Outputs:
- product_blocks: bfloat16 [4, 4, 192, 128, 128], P('row', 'col', 'depth')
Inputs may be any that keep to these rules, and one draw needn't show every extreme that they name: `out_pos`: within a tile the listed positions are distinct, local rows below 16 and local columns below 16. Some tile uses all 192 slots; only the first out_count slots of a tile are in use.
All inputs are finite; a program needn't handle non-finite values.
Results may differ from a plain program's by a relative error of at most 0.0048.
Values may be sent and summed in bfloat16 or wider, within the bound.
No kernel may reach another device: no remote copies, remote signals or barrier semaphores. Data moves between devices by JAX's collectives and lax.ppermute only.
A program may use at most 128 MiB of HBM per device.

v0:
```python
import jax
import jax.numpy as jnp
from jax import lax
from jax.sharding import PartitionSpec as P


def spread(value, axis, source):
    kept = jnp.where(lax.axis_index(axis) == source, value, 0).astype(value.dtype)
    return lax.psum(kept, axis)


def block_terms(panel_rows, panel_keys, column_rows, column_keys, row_slots, col_slots, live_mask):
    left_blocks = panel_rows[row_slots]
    right_blocks = column_rows[col_slots]
    same_slot = (panel_keys[row_slots] == column_keys[col_slots]).astype(jnp.bfloat16)
    right_masked = right_blocks * same_slot[:, :, None, None]
    summed = jnp.einsum(
        "sgab,sgcb->sac", left_blocks, right_masked, preferred_element_type=jnp.float32
    )
    return summed * live_mask[:, None, None]


def body(x_blocks, col_slot, out_pos, out_count):
    column_rows, column_keys = (
        lax.all_gather(x_blocks, "row", axis=0, tiled=True),
        lax.all_gather(col_slot, "row", axis=0, tiled=True),
    )
    repeats = lax.axis_size("col") // lax.axis_size("row")
    root_here = lax.axis_index("row") * repeats + 0
    panel_parts = [(spread(column_rows, "col", root_here), spread(column_keys, "col", root_here))]
    panel_rows = jnp.concatenate([piece_pair[0] for piece_pair in panel_parts], 0)
    panel_keys = jnp.concatenate([piece_pair[1] for piece_pair in panel_parts], 0)
    positions = out_pos[0, 0]
    row_index = positions[:, 0]
    col_index = positions[:, 1]
    capacity = positions.shape[0]
    share = capacity // lax.axis_size("depth")
    live_all = (jnp.arange(capacity, dtype=jnp.int32) < out_count[0, 0]).astype(jnp.float32)
    first_slot = jnp.int32(0)
    blocks_out = []
    for block_idx in range(share * lax.axis_size("depth") // share):
        begin = first_slot + block_idx * share
        rows_here = lax.dynamic_slice_in_dim(row_index, begin, share)
        cols_here = lax.dynamic_slice_in_dim(col_index, begin, share)
        live_here = lax.dynamic_slice_in_dim(live_all, begin, share)
        blocks_out.append(
            block_terms(
                panel_rows, panel_keys, column_rows, column_keys, rows_here, cols_here, live_here
            )
        )
    summed = lax.psum_scatter(
        jnp.concatenate(blocks_out, 0).astype(jnp.bfloat16),
        "depth",
        scatter_dimension=0,
        tiled=True,
    )
    return summed[None, None]


def solution(mesh):
    in_specs = (
        P(("row", "col"), "depth", None, None),
        P(("row", "col"), "depth"),
        P("row", "col", None, None),
        P("row", "col"),
    )
    out_specs = P("row", "col", "depth", None, None)
    return jax.shard_map(body, mesh=mesh, in_specs=in_specs, out_specs=out_specs, check_vma=False)
```

profile of v0, /device:TPU:0, one launch (start us, length us, event | category | flops | bytes accessed | tf_op | source)
XLA Modules:
  0.0 247.8 jit_solution(15371230426668067330)
XLA Ops:
  6.5 0.0 all-gather.3.cloned.1.call-start
  6.5 0.7 all-gather.3.cloned.1.call-update
  7.3 0.0 all-reduce.2.cloned.1.call-start
  7.3 26.9 %all-gather.3.cloned.1.call-done = bf16[16,4,128,128]{3,2,1,0:T(8,128)(2,1)} async-done(((bf16[4,4,128,128]{3,2,1,0:T(8,128)(2,1)}), bf16[16,4,128,128]{3,2,1,0:T(8,128)(2,1)}) %all-gather.3.cloned.1.call-update) | async-done | bytes 2097168 | tf_op jit(solution)/shard_map/all_gather | solution.py:25
  34.2 0.0 copy-start
  34.2 3.2 %broadcast_select_fusion = bf16[16,4,128,128]{3,2,1,0:T(8,128)(2,1)} fusion(bf16[16,4,128,128]{3,2,1,0:T(8,128)(2,1)} %all-gather.3.cloned.1.call-done, pred[]{:T(512)S(6)} %eq.18), kind=kLoop, calls=%fused_computation.19 | loop fusion | flops 1048576 | bytes 4194305 | tf_op jit(solution)/shard_map/jit(_where)/select_n | solution.py:8
  37.4 0.0 all-reduce.2.cloned.1.call-update
  37.5 0.0 reduce-scatter.2.cloned.1.call-start
  38.2 5.3 %all-gather = s32[4,4,4]{2,1,0:T(4,128)S(1)} all-gather(s32[1,4,4]{2,1,0:T(4,128)} %bitcast.29), channel_id=1, replica_groups=mesh['row'=4,'col'=4,'depth'=2] {'row'}, dimensions={0}, use_global_device_ids=true | all-gather | bytes 320 | tf_op jit(solution)/shard_map/all_gather | solution.py:26
  43.5 0.9 fusion.13
  44.4 0.6 gather_fusion.3
  45.0 7.4 %psum.15 = s32[16,4]{1,0:T(8,128)S(1)} all-reduce(s32[16,4]{1,0:T(8,128)S(1)} %broadcast_select_fusion.1), channel_id=1, replica_groups=mesh['row'=4,'col'=4,'depth'=2] {'col'}, use_global_device_ids=true, to_apply=%region_1.2 | all-reduce | flops 64 | bytes 512 | tf_op jit(solution)/shard_map/psum | solution.py:9
  52.4 0.6 gather_fusion.2
  53.0 0.6 gather_fusion.6
  53.6 0.6 gather_fusion.7
  54.3 0.1 fusion.16
  54.4 0.0 copy-done
  54.4 6.8 %gather_fusion.1 = bf16[96,4,128,128]{3,2,1,0:T(8,128)(2,1)} fusion(bf16[16,4,128,128]{3,2,1,0:T(8,128)(2,1)S(1)} %copy-done, s32[1024]{0:T(1024)S(1)} %get-tuple-element.13), kind=kCustom, calls=%fused_computation.1 | custom fusion | bytes 25166208 | tf_op jit(solution)/shard_map/gather | solution.py:14
  61.2 6.9 %gather_fusion.5 = bf16[96,4,128,128]{3,2,1,0:T(8,128)(2,1)} fusion(bf16[16,4,128,128]{3,2,1,0:T(8,128)(2,1)S(1)} %copy-done, s32[1024]{0:T(1024)S(1)} %get-tuple-element.11), kind=kCustom, calls=%fused_computation.5 | custom fusion | bytes 25166208 | tf_op jit(solution)/shard_map/gather | solution.py:14
  68.1 56.3 %all-reduce.2.cloned.1.call-done = bf16[16,4,128,128]{3,2,1,0:T(8,128)(2,1)} async-done(((bf16[16,4,128,128]{3,2,1,0:T(8,128)(2,1)}), bf16[16,4,128,128]{3,2,1,0:T(8,128)(2,1)}) %all-reduce.2.cloned.1.call-update) | async-done | bytes 2097168 | tf_op jit(solution)/shard_map/psum | solution.py:9
  124.3 8.5 %gather_fusion = bf16[96,4,128,128]{3,2,1,0:T(8,128)(2,1)} fusion(bf16[16,4,128,128]{3,2,1,0:T(8,128)(2,1)} %all-reduce.2.cloned.1.call-done, s32[1024]{0:T(1024)S(1)} %get-tuple-element.14), kind=kCustom, calls=%fused_computation | custom fusion | bytes 25166208 | tf_op jit(solution)/shard_map/gather | solution.py:13
  132.8 0.0 copy-start.1
  132.8 11.9 %fusion.5 = bf16[96,128,128]{2,1,0:T(8,128)(2,1)} fusion(f32[96]{0:T(128)S(1)} %get-tuple-element.9, bf16[96,4,128,128]{3,2,1,0:T(8,128)(2,1)} %gather_fusion, bf16[96,4,128,128]{3,2,1,0:T(8,128)(2,1)} %gather_fusion.1, bf16[96,4]{1,0:T(8,128)(2,1)S(1)} %compare_convert_fusion.1), kind=kOutput, calls=%fused_computation.16 | convolution fusion | flops 1620049920 | bytes 28312704 | tf_op jit(solution)/shard_map/sgab,sgcb->sac/dot_general | solution.py:17
  144.8 0.0 copy-done.1
  144.8 6.8 %gather_fusion.4 = bf16[96,4,128,128]{3,2,1,0:T(8,128)(2,1)} fusion(bf16[16,4,128,128]{3,2,1,0:T(8,128)(2,1)S(1)} %copy-done.1, s32[1024]{0:T(1024)S(1)} %get-tuple-element.12), kind=kCustom, calls=%fused_computation.4 | custom fusion | bytes 25166208 | tf_op jit(solution)/shard_map/gather | solution.py:13
  151.6 0.0 copy-start.2
  151.6 10.2 %fusion.4 = bf16[96,128,128]{2,1,0:T(8,128)(2,1)S(1)} fusion(f32[96]{0:T(128)S(1)} %get-tuple-element.10, bf16[96,4,128,128]{3,2,1,0:T(8,128)(2,1)} %gather_fusion.4, bf16[96,4,128,128]{3,2,1,0:T(8,128)(2,1)} %gather_fusion.5, bf16[96,4]{1,0:T(8,128)(2,1)S(1)} %compare_convert_fusion), kind=kOutput, calls=%fused_computation.14 | convolution fusion | flops 1620049920 | bytes 28312704 | tf_op jit(solution)/shard_map/sgab,sgcb->sac/dot_general | solution.py:17
  161.8 0.0 copy-done.2
  161.8 3.2 %pad_maximum_fusion = bf16[192,128,128]{2,1,0:T(8,128)(2,1)} fusion(bf16[96,128,128]{2,1,0:T(8,128)(2,1)S(1)} %fusion.4, bf16[96,128,128]{2,1,0:T(8,128)(2,1)S(1)} %copy-done.2), kind=kLoop, calls=%fused_computation.12 | loop fusion | flops 3145728 | bytes 12582912 | tf_op jit(solution)/shard_map/concatenate | solution.py:52
  165.0 0.0 reduce-scatter.2.cloned.1.call-update
  165.1 76.2 %reduce-scatter.2.cloned.1.call-done = bf16[96,128,128]{2,1,0:T(8,128)(2,1)} async-done(((bf16[192,128,128]{2,1,0:T(8,128)(2,1)}), bf16[96,128,128]{2,1,0:T(8,128)(2,1)}) %reduce-scatter.2.cloned.1.call-update) | async-done | bytes 3145744 | tf_op jit(solution)/shard_map/reduce_scatter | solution.py:51
  (6 shorter events, 0.0 us)
Async XLA Ops:
  6.5 27.7 %all-gather.3.cloned.1.call-start = ((), (), s32[]{:S(2)}) async-start(), calls=%async_computation.1 | async-start | bytes 2621440 | tf_op jit(solution)/shard_map/all_gather | solution.py:25
  7.3 117.1 %all-reduce.2.cloned.1.call-start = ((), (), s32[]{:S(2)}) async-start(), calls=%async_computation.2 | async-start | bytes 4194304 | tf_op jit(solution)/shard_map/psum | solution.py:9
  34.2 20.1 %copy-start = (bf16[16,4,128,128]{3,2,1,0:T(8,128)(2,1)S(1)}, bf16[16,4,128,128]{3,2,1,0:T(8,128)(2,1)}, u32[]{:S(2)}) copy-start(bf16[16,4,128,128]{3,2,1,0:T(8,128)(2,1)} %all-gather.3.cloned.1.call-done) | copy-start | bytes 6291460
  37.5 203.8 %reduce-scatter.2.cloned.1.call-start = ((), (), s32[]{:S(2)}) async-start(), calls=%async_computation.3 | async-start | bytes 9437184 | tf_op jit(solution)/shard_map/reduce_scatter | solution.py:51
  132.8 11.9 %copy-start.1 = (bf16[16,4,128,128]{3,2,1,0:T(8,128)(2,1)S(1)}, bf16[16,4,128,128]{3,2,1,0:T(8,128)(2,1)}, u32[]{:S(2)}) copy-start(bf16[16,4,128,128]{3,2,1,0:T(8,128)(2,1)} %all-reduce.2.cloned.1.call-done) | copy-start | bytes 6291460
  151.6 10.3 %copy-start.2 = (bf16[96,128,128]{2,1,0:T(8,128)(2,1)S(1)}, bf16[96,128,128]{2,1,0:T(8,128)(2,1)}, u32[]{:S(2)}) copy-start(bf16[96,128,128]{2,1,0:T(8,128)(2,1)} %fusion.5) | copy-start | bytes 9437188
Sparse Core Ops, SparseCore 0:
  8.9 25.2 all-gather.2
  37.6 86.7 all-reduce.1
  165.2 76.0 reduce-scatter.1
where the time goes:
time: 248 us
  waiting for transfers between devices  160 us (65%)
  local copies, waits for them, and re-layouts  31.5 us (13%)
  matrix products  22.2 us (9%)
  between operations  13.8 us (6%)
  blocking collectives  12.7 us (5%)
  other arithmetic  7.33 us (3%)
    reduce_scatter x1, waiting for transfers between devices, body(): lax.psum_scatter(jnp.concatenate(blocks_out, 0).astype(jnp.bfloat16), 'de...  76.2 us
    psum x1, waiting for transfers between devices, spread(): return lax.psum(kept, axis)  56.3 us
    all_gather x1, waiting for transfers between devices, body(): lax.all_gather(x_blocks, 'row', axis=0, tiled=True)  26.9 us
    dot_general x2, matrix products, block_terms(): jnp.einsum('sgab,sgcb->sac', left_blocks, right_masked, preferred_element...  22.2 us
    gather x2, local copies, waits for them, and re-layouts, block_terms(): left_blocks = panel_rows[row_slots]  15.3 us
    gather x2, local copies, waits for them, and re-layouts, block_terms(): right_blocks = column_rows[col_slots]  13.7 us
    psum x1, blocking collectives, spread(): return lax.psum(kept, axis)  7.38 us
    all_gather x1, blocking collectives, body(): lax.all_gather(col_slot, 'row', axis=0, tiled=True)  5.3 us
  transfers between devices with their start and end apart: 3, of which 3 were waited for; matrix products, arithmetic and copies ran while one was open for 7% of the time, Pallas kernels for 0%

commit v1 on v0

v1 whole, which is shorter than its diff:
```python
import functools

import jax
import jax.numpy as jnp
from jax import lax
from jax.experimental import pallas as pl
from jax.experimental.pallas import tpu as pltpu
from jax.sharding import PartitionSpec as P

KEY_ROWS = 16
SLOTS = 16


def product_kernel(
    n_row, n_depth, n_rows, share, first, last, info, pos, *refs
):
    n = n_row * n_depth
    left_in, right_in = refs[:n], refs[n : 2 * n]
    refs = refs[2 * n :]
    if first:
        total_in = None
    else:
        total_in, refs = refs[0], refs[1:]
    out, left, right, left_keys, right_keys, sems = refs
    block = left.shape[-1]
    count, row, depth = info[0], info[1], info[2]

    @pl.when(pl.program_id(0) == 0)
    def _():
        copies = []
        for e in range(n_depth):
            for t in range(n_row):
                at = e * n_row + t
                for side, (src, dst) in enumerate(((left_in, left), (right_in, right))):
                    copies.append(
                        pltpu.make_async_copy(
                            src[at], dst.at[e, row ^ t], sems.at[side * n + at]
                        )
                    )
        for copy in copies:
            copy.start()
        for copy in copies:
            copy.wait()
        for e in range(n_depth):
            for t in range(n_row):
                for src, dst in ((left, left_keys), (right, right_keys)):
                    dst[e, t] = src[e, t, n_rows * block :, :].astype(jnp.float32)

    for i in range(SLOTS):
        slot = depth * share + pl.program_id(0) * SLOTS + i
        u, v = pos[2 * slot], pos[2 * slot + 1]
        u_at, u_in = lax.div(u, n_rows), lax.rem(u, n_rows)
        v_at, v_in = lax.div(v, n_rows), lax.rem(v, n_rows)
        u_rows = pl.ds(pl.multiple_of(u_in * block, block), block)
        v_rows = pl.ds(pl.multiple_of(v_in * block, block), block)
        lefts, rights = [], []
        for e in range(n_depth):
            same = left_keys[e, u_at, pl.ds(u_in, 1), :] == right_keys[e, v_at, pl.ds(v_in, 1), :]
            same = same.astype(jnp.float32).astype(jnp.bfloat16)
            lefts.append(left[e, u_at, u_rows, :])
            rights.append(right[e, v_at, v_rows, :] * same)
        total = lax.dot_general(
            jnp.concatenate(lefts, 1),
            jnp.concatenate(rights, 1),
            (((1,), (1,)), ((), ())),
            preferred_element_type=jnp.float32,
        )
        if total_in is not None:
            total = total + total_in[i]
        if last:
            total = jnp.where(slot < count, total, 0.0)
        out[i] = total.astype(out.dtype)


def add_products(sizes, n_rows, share, first, last, info, pos, left, right, total):
    n_row, n_depth = sizes
    n = n_row * n_depth
    rows, block = left[0].shape
    slots = pl.BlockSpec((SLOTS, block, block), lambda i: (i, 0, 0))
    in_specs = [pl.BlockSpec(memory_space=pltpu.SMEM)] * 2 + [pl.BlockSpec(memory_space=pl.ANY)] * (2 * n)
    args = [info, pos, *left, *right]
    if not first:
        in_specs.append(slots)
        args.append(total)
    return pl.pallas_call(
        functools.partial(product_kernel, n_row, n_depth, n_rows, share, first, last),
        grid=(share // SLOTS,),
        in_specs=in_specs,
        out_specs=slots,
        out_shape=jax.ShapeDtypeStruct((share, block, block), jnp.bfloat16 if last else jnp.float32),
        scratch_shapes=[
            pltpu.VMEM((n_depth, n_row, rows, block), jnp.bfloat16),
            pltpu.VMEM((n_depth, n_row, rows, block), jnp.bfloat16),
            pltpu.VMEM((n_depth, n_row, KEY_ROWS, block), jnp.float32),
            pltpu.VMEM((n_depth, n_row, KEY_ROWS, block), jnp.float32),
            pltpu.SemaphoreType.DMA((2 * n,)),
        ],
        compiler_params=pltpu.CompilerParams(vmem_limit_bytes=40 * 1024 * 1024),
        cost_estimate=pl.CostEstimate(
            flops=2 * share * n_depth * block**3,
            bytes_accessed=2 * n * rows * block * 2 + share * block * block * 8,
            transcendentals=0,
        ),
    )(*args)


def body(sizes, x_blocks, col_slot, out_pos, out_count):
    n_row, n_col, n_depth = sizes
    n_rows, n_groups, block, _ = x_blocks.shape
    capacity = out_pos.shape[2]
    share = capacity // n_depth
    row, col, depth = lax.axis_index("row"), lax.axis_index("col"), lax.axis_index("depth")
    info = jnp.stack([out_count[0, 0], row, depth]).astype(jnp.int32)
    pos = out_pos[0, 0].reshape(-1)

    def swap_row(value, t):
        return lax.ppermute(value, "row", [(i, i ^ t) for i in range(n_row)])

    def from_depth(value, e):
        return lax.ppermute(value, "depth", [((i + e) % n_depth, i) for i in range(n_depth)])

    def from_both(value, t, e):
        pairs = [
            ((i ^ t) * n_depth + (j + e) % n_depth, i * n_depth + j)
            for i in range(n_row)
            for j in range(n_depth)
        ]
        return lax.ppermute(value, ("row", "depth"), pairs)

    total = None
    for g in range(n_groups):
        keys = jnp.pad(col_slot[:, g].astype(jnp.bfloat16), (0, KEY_ROWS - n_rows))
        own = jnp.concatenate(
            [
                x_blocks[:, g].reshape(n_rows * block, block),
                jnp.broadcast_to(keys[:, None], (KEY_ROWS, block)),
            ]
        )
        right = {(0, 0): own}
        for t in range(0, n_row, 2):
            if t:
                right[t, 0] = swap_row(own, t)
        for e in range(1, n_depth):
            right[0, e] = from_depth(own, e)
        for e in range(1, n_depth):
            for t in range(2, n_row, 2):
                right[t, e] = from_depth(right[t, 0], e) if g % 2 else swap_row(right[0, e], t)
        for t in range(1, n_row, 2):
            for e in range(n_depth):
                right[t, e] = swap_row(right[t - 1, e], 1)
        up, down = [own], [own]
        for k in range(1, n_col):
            up.append(lax.ppermute(up[-1], "col", [(i, i + 1) for i in range(k - 1, n_col - 1)]))
            down.append(lax.ppermute(down[-1], "col", [(i + 1, i) for i in range(n_col - k)]))
        left = {}
        for t in range(n_row):
            far = col - (row ^ t)
            value = own
            for k in range(1, n_col):
                value = jnp.where(far == k, up[k], value)
                value = jnp.where(far == -k, down[k], value)
            left[t, 0] = swap_row(value, t) if t else value
            for e in range(1, n_depth):
                if t >= 2 and (t + g) % 2:
                    left[t, e] = from_both(value, t, e)
                else:
                    left[t, e] = from_depth(left[t, 0], e)
        order = [(t, e) for e in range(n_depth) for t in range(n_row)]
        total = add_products(
            (n_row, n_depth),
            n_rows,
            share,
            g == 0,
            g == n_groups - 1,
            info,
            pos,
            [left[at] for at in order],
            [right[at] for at in order],
            total,
        )
    return total[None, None]


def solution(mesh):
    sizes = tuple(mesh.shape[axis] for axis in ("row", "col", "depth"))
    in_specs = (
        P(("row", "col"), "depth", None, None),
        P(("row", "col"), "depth"),
        P("row", "col", None, None),
        P("row", "col"),
    )
    out_specs = P("row", "col", "depth", None, None)
    return jax.shard_map(
        functools.partial(body, sizes), mesh=mesh, in_specs=in_specs, out_specs=out_specs, check_vma=False
    )
```

time: 248 us -> 177 us (0.71)
  waiting for transfers between devices: 160 us -> 45 us
  starting transfers between devices: 0.08 us -> 82.5 us
  Pallas kernels: 0 us -> 34.3 us
  local copies, waits for them, and re-layouts: 31.5 us -> 7.5 us
  matrix products: 22.2 us -> 0 us
  blocking collectives: 12.7 us -> 0 us
  between operations: 13.8 us -> 1.61 us
    ppermute x0 -> x80, starting transfers between devices: none -> 82.5 us  [the longest x12 24.8 us: body(): lax.ppermute(up[-1], 'col', [(i, i + 1) for i in range(k - 1, n_col - 1)])]
    reduce_scatter x1 -> x0, waiting for transfers between devices: 76.2 us -> none  [body(): lax.psum_scatter(jnp.concatenate(blocks_out, 0).astype(jnp.bfloat16), 'de...]
    psum x1 -> x0, waiting for transfers between devices: 56.3 us -> none  [spread(): return lax.psum(kept, axis)]
    ppermute x0 -> x80, waiting for transfers between devices: none -> 45 us  [the longest x12 28 us: body(): lax.ppermute(down[-1], 'col', [(i + 1, i) for i in range(n_col - k)])]
    pallas_call x0 -> x4, Pallas kernels: none -> 34.3 us  [add_products(): pl.pallas_call(functools.partial(product_kernel, n_row, n_depth, n_rows,...]
    gather x8 -> x0, local copies, waits for them, and re-layouts: 31.5 us -> none  [the longest x2 15.3 us: block_terms(): left_blocks = panel_rows[row_slots]]
    all_gather x1 -> x0, waiting for transfers between devices: 26.9 us -> none  [body(): lax.all_gather(x_blocks, 'row', axis=0, tiled=True)]
    dot_general x2 -> x0, matrix products: 22.2 us -> none  [block_terms(): jnp.einsum('sgab,sgcb->sac', left_blocks, right_masked, preferred_element...]
  transfers between devices with their start and end apart: 3 -> 80, of which waited for: 3 -> 15; matrix products, arithmetic and copies ran while one was open for 7% -> 3% of each run, Pallas kernels for 0% -> 15%
where the time goes in v1:
time: 177 us; the launch traced here: 176 us
  starting transfers between devices  82.5 us (47%)
  waiting for transfers between devices  45 us (25%)
  Pallas kernels  34.3 us (19%)
  local copies, waits for them, and re-layouts  7.5 us (4%)
  other arithmetic  5.5 us (3%)
    pallas_call x4, Pallas kernels, add_products(): pl.pallas_call(functools.partial(product_kernel, n_row, n_depth, n_rows,...  34.3 us
    ppermute x12, waiting for transfers between devices, body(): lax.ppermute(down[-1], 'col', [(i + 1, i) for i in range(n_col - k)])  28 us
    ppermute x12, starting transfers between devices, body(): lax.ppermute(up[-1], 'col', [(i, i + 1) for i in range(k - 1, n_col - 1)])  24.8 us
    ppermute x18, starting transfers between devices, from_depth(): lax.ppermute(value, 'depth', [((i + e) % n_depth, i) for i in range(n_dep...  21.7 us
    ppermute x12, starting transfers between devices, body(): lax.ppermute(down[-1], 'col', [(i + 1, i) for i in range(n_col - k)])  15.4 us
    ppermute x34, waiting for transfers between devices, swap_row(): return lax.ppermute(value, 'row', [(i, i ^ t) for i in range(n_row)])  13.3 us
    ppermute x34, starting transfers between devices, swap_row(): return lax.ppermute(value, 'row', [(i, i ^ t) for i in range(n_row)])  12.4 us
    ppermute x4, starting transfers between devices, from_both(): return lax.ppermute(value, ('row', 'depth'), pairs)  8.22 us
  transfers between devices with their start and end apart: 80, of which 15 were waited for; matrix products, arithmetic and copies ran while one was open for 3% of the time, Pallas kernels for 15%

profile of v1, /device:TPU:0, one launch (start us, length us, event | category | flops | bytes accessed | tf_op | source)
XLA Modules:
  0.0 176.4 jit_solution(4141451012505299618)
XLA Ops:
  0.0 1.1 fusion.4
  1.1 0.7 convert.6
  2.2 1.3 collective-permute-start.60
  3.5 5.6 %collective-permute-start.63 = (bf16[528,128]{1,0:T(8,128)(2,1)S(1)}, bf16[528,128]{1,0:T(8,128)(2,1)S(1)}, u32[]{:S(2)}, u32[]{:S(2)}) collective-permute-start(bf16[528,128]{1,0:T(8,128)(2,1)S(1)} %pad_maximum_fusion.3.refs_8_), channel_id=1, source_target_pairs={{0,2},{2,4},{4,6},{1,3},{3,5},{5,7},{8,10},{10,12},{12,14},{9,11},... | collective-permute-start | bytes 405512 | tf_op jit(solution)/shard_map/ppermute | solution.py:153
  9.0 2.0 %collective-permute-start.76 = (bf16[528,128]{1,0:T(8,128)(2,1)S(1)}, bf16[528,128]{1,0:T(8,128)(2,1)S(1)}, u32[]{:S(2)}, u32[]{:S(2)}) collective-permute-start(bf16[528,128]{1,0:T(8,128)(2,1)S(1)} %pad_maximum_fusion.3.refs_8_), channel_id=1, source_target_pairs={{1,0},{0,1},{3,2},{2,3},{5,4},{4,5},{7,6},{6,7},{9,8},{8,9},{11,10... | collective-permute-start | bytes 405512 | tf_op jit(solution)/shard_map/ppermute | solution.py:120
  11.2 1.3 collective-permute-start.40
  12.5 4.6 %collective-permute-start.43 = (bf16[528,128]{1,0:T(8,128)(2,1)S(1)}, bf16[528,128]{1,0:T(8,128)(2,1)S(1)}, u32[]{:S(2)}, u32[]{:S(2)}) collective-permute-start(bf16[528,128]{1,0:T(8,128)(2,1)S(1)} %pad_maximum_fusion.2.refs_8_), channel_id=1, source_target_pairs={{0,2},{2,4},{4,6},{1,3},{3,5},{5,7},{8,10},{10,12},{12,14},{9,11},... | collective-permute-start | bytes 405512 | tf_op jit(solution)/shard_map/ppermute | solution.py:153
  17.1 1.3 collective-permute-start.61
  18.4 0.7 collective-permute-start.64
  19.2 1.3 collective-permute-start.41
  20.5 0.7 collective-permute-start.44
  21.2 2.8 %collective-permute-done.61 = bf16[528,128]{1,0:T(8,128)(2,1)S(1)} collective-permute-done((bf16[528,128]{1,0:T(8,128)(2,1)S(1)}, bf16[528,128]{1,0:T(8,128)(2,1)S(1)}, u32[]{:S(2)}, u32[]{:S(2)}) %collective-permute-start.61) | collective-permute-done | bytes 135200 | tf_op jit(solution)/shard_map/ppermute | solution.py:154
  24.0 1.3 collective-permute-start.62
  25.3 0.7 collective-permute-start.65
  26.8 0.8 copy.5
  27.8 1.7 collective-permute-done.41
  29.6 1.5 collective-permute-start.74
  31.1 3.7 %collective-permute-done.62 = bf16[528,128]{1,0:T(8,128)(2,1)S(1)} collective-permute-done((bf16[528,128]{1,0:T(8,128)(2,1)S(1)}, bf16[528,128]{1,0:T(8,128)(2,1)S(1)}, u32[]{:S(2)}, u32[]{:S(2)}) %collective-permute-start.62) | collective-permute-done | bytes 135200 | tf_op jit(solution)/shard_map/ppermute | solution.py:154
  34.8 1.3 collective-permute-start.42
  37.1 4.6 %collective-permute-done.42 = bf16[528,128]{1,0:T(8,128)(2,1)S(1)} collective-permute-done((bf16[528,128]{1,0:T(8,128)(2,1)S(1)}, bf16[528,128]{1,0:T(8,128)(2,1)S(1)}, u32[]{:S(2)}, u32[]{:S(2)}) %collective-permute-start.42) | collective-permute-done | bytes 135200 | tf_op jit(solution)/shard_map/ppermute | solution.py:154
  41.7 1.5 collective-permute-start.54
  44.7 1.3 collective-permute-start.20
  46.0 4.6 %collective-permute-start.23 = (bf16[528,128]{1,0:T(8,128)(2,1)S(1)}, bf16[528,128]{1,0:T(8,128)(2,1)S(1)}, u32[]{:S(2)}, u32[]{:S(2)}) collective-permute-start(bf16[528,128]{1,0:T(8,128)(2,1)S(1)} %pad_maximum_fusion.1.refs_8_), channel_id=1, source_target_pairs={{0,2},{2,4},{4,6},{1,3},{3,5},{5,7},{8,10},{10,12},{12,14},{9,11},... | collective-permute-start | bytes 405512 | tf_op jit(solution)/shard_map/ppermute | solution.py:153
  50.8 1.6 collective-permute-start.36
  52.9 1.3 collective-permute-start
  54.2 4.6 %collective-permute-start.3 = (bf16[528,128]{1,0:T(8,128)(2,1)S(1)}, bf16[528,128]{1,0:T(8,128)(2,1)S(1)}, u32[]{:S(2)}, u32[]{:S(2)}) collective-permute-start(bf16[528,128]{1,0:T(8,128)(2,1)S(1)} %pad_maximum_fusion.refs_8_), channel_id=1, source_target_pairs={{0,2},{2,4},{4,6},{1,3},{3,5},{5,7},{8,10},{10,12},{12,14},{9,11},... | collective-permute-start | bytes 405512 | tf_op jit(solution)/shard_map/ppermute | solution.py:153
  59.1 1.6 collective-permute-start.14
  61.2 1.3 collective-permute-start.21
  63.5 1.1 collective-permute-done.14.refs_10_
  64.6 1.5 collective-permute-start.78
  66.6 2.5 %collective-permute-done.21 = bf16[528,128]{1,0:T(8,128)(2,1)S(1)} collective-permute-done((bf16[528,128]{1,0:T(8,128)(2,1)S(1)}, bf16[528,128]{1,0:T(8,128)(2,1)S(1)}, u32[]{:S(2)}, u32[]{:S(2)}) %collective-permute-start.21) | collective-permute-done | bytes 135200 | tf_op jit(solution)/shard_map/ppermute | solution.py:154
  69.1 1.3 collective-permute-start.22
  71.3 1.6 collective-permute-start.58
  73.5 2.7 %collective-permute-done.22 = bf16[528,128]{1,0:T(8,128)(2,1)S(1)} collective-permute-done((bf16[528,128]{1,0:T(8,128)(2,1)S(1)}, bf16[528,128]{1,0:T(8,128)(2,1)S(1)}, u32[]{:S(2)}, u32[]{:S(2)}) %collective-permute-start.22) | collective-permute-done | bytes 135200 | tf_op jit(solution)/shard_map/ppermute | solution.py:154
  77.0 1.6 collective-permute-start.18
  79.0 1.3 collective-permute-start.1
  81.4 5.4 %collective-permute-done.1 = bf16[528,128]{1,0:T(8,128)(2,1)S(1)} collective-permute-done((bf16[528,128]{1,0:T(8,128)(2,1)S(1)}, bf16[528,128]{1,0:T(8,128)(2,1)S(1)}, u32[]{:S(2)}, u32[]{:S(2)}) %collective-permute-start.1) | collective-permute-done | bytes 135200 | tf_op jit(solution)/shard_map/ppermute | solution.py:154
  87.4 1.3 collective-permute-start.2
  89.0 0.8 collective-permute-start.5
  91.0 4.5 %collective-permute-done.2 = bf16[528,128]{1,0:T(8,128)(2,1)S(1)} collective-permute-done((bf16[528,128]{1,0:T(8,128)(2,1)S(1)}, bf16[528,128]{1,0:T(8,128)(2,1)S(1)}, u32[]{:S(2)}, u32[]{:S(2)}) %collective-permute-start.2) | collective-permute-done | bytes 135200 | tf_op jit(solution)/shard_map/ppermute | solution.py:154
  95.8 1.8 %collective-permute-start.72 = (bf16[528,128]{1,0:T(8,128)(2,1)S(1)}, bf16[528,128]{1,0:T(8,128)(2,1)S(1)}, u32[]{:S(2)}, u32[]{:S(2)}) collective-permute-start(bf16[528,128]{1,0:T(8,128)(2,1)S(1)} %select_select_fusion), channel_id=1, source_target_pairs={{25,0},{24,1},{17,8},{16,9},{9,16},{8,17},{1,24},{0,25},{27,2},{26... | collective-permute-start | bytes 405512 | tf_op jit(solution)/shard_map/ppermute | solution.py:128
  97.5 1.5 collective-permute-start.69
  99.7 4.6 %collective-permute-done.68.refs_3_ = bf16[528,128]{1,0:T(8,128)(2,1)S(1)} collective-permute-done((bf16[528,128]{1,0:T(8,128)(2,1)S(1)}, bf16[528,128]{1,0:T(8,128)(2,1)S(1)}, u32[]{:S(2)}, u32[]{:S(2)}) %collective-permute-start.68) | collective-permute-done | bytes 135200 | tf_op jit(solution)/shard_map/ppermute | solution.py:117
  104.7 1.9 %collective-permute-start.51 = (bf16[528,128]{1,0:T(8,128)(2,1)S(1)}, bf16[528,128]{1,0:T(8,128)(2,1)S(1)}, u32[]{:S(2)}, u32[]{:S(2)}) collective-permute-start(bf16[528,128]{1,0:T(8,128)(2,1)S(1)} %select_select_fusion.5), channel_id=1, source_target_pairs={{17,0},{16,1},{25,8},{24,9},{1,16},{0,17},{9,24},{8,25},{19,2},{18... | collective-permute-start | bytes 405512 | tf_op jit(solution)/shard_map/ppermute | solution.py:128
  106.6 2.7 %collective-permute-start.32 = (bf16[528,128]{1,0:T(8,128)(2,1)S(1)}, bf16[528,128]{1,0:T(8,128)(2,1)S(1)}, u32[]{:S(2)}, u32[]{:S(2)}) collective-permute-start(bf16[528,128]{1,0:T(8,128)(2,1)S(1)} %select_select_fusion.8), channel_id=1, source_target_pairs={{25,0},{24,1},{17,8},{16,9},{9,16},{8,17},{1,24},{0,25},{27,2},{26... | collective-permute-start | bytes 405512 | tf_op jit(solution)/shard_map/ppermute | solution.py:128
  109.8 6.8 %collective-permute-done.47.refs_2_ = bf16[528,128]{1,0:T(8,128)(2,1)S(1)} collective-permute-done((bf16[528,128]{1,0:T(8,128)(2,1)S(1)}, bf16[528,128]{1,0:T(8,128)(2,1)S(1)}, u32[]{:S(2)}, u32[]{:S(2)}) %collective-permute-start.47) | collective-permute-done | bytes 135200 | tf_op jit(solution)/shard_map/ppermute | solution.py:117
  117.1 1.5 collective-permute-start.29
  119.2 1.7 collective-permute-start.70
  120.8 0.8 collective-permute-done.27.refs_2_
  122.3 1.3 collective-permute-done.29.refs_4_
  123.6 1.4 collective-permute-start.50
  125.6 0.9 collective-permute-done.70.refs_5_
  126.5 1.4 collective-permute-start.31
  127.9 1.5 collective-permute-done.71.refs_6_
  129.4 1.4 collective-permute-start.30
  131.1 6.9 %shard_map.46.refs_16_ = f32[96,128,128]{2,1,0:T(8,128)S(1)} custom-call(s32[3]{0:T(128)S(1)} %pad_add_fusion.info, s32[384]{0:T(512)S(1)} %reshape_squeeze.15.pos, bf16[528,128]{1,0:T(8,128)(2,1)S(1)} %select_select_fusion.3.refs_0_, bf16[528,128]{1,0:T(8,128)(2,1)S(1)} %collective-permute-done.66.refs_1_, ...), custom_call_target="tpu_custom_call" | custom-call | flops 805306368 | bytes 14745600 | tf_op jit(solution)/shard_map/pallas_call | solution.py:85
  138.0 2.6 %copy-done = f32[96,128,128]{2,1,0:T(8,128)} copy-done((f32[96,128,128]{2,1,0:T(8,128)}, f32[96,128,128]{2,1,0:T(8,128)S(1)}, u32[]{:S(2)}) %copy-start) | copy-done | bytes 6291480
  140.6 1.9 %collective-permute-start.11 = (bf16[528,128]{1,0:T(8,128)(2,1)S(1)}, bf16[528,128]{1,0:T(8,128)(2,1)S(1)}, u32[]{:S(2)}, u32[]{:S(2)}) collective-permute-start(bf16[528,128]{1,0:T(8,128)(2,1)S(1)} %select_select_fusion.13), channel_id=1, source_target_pairs={{17,0},{16,1},{25,8},{24,9},{1,16},{0,17},{9,24},{8,25},{19,2},{18... | collective-permute-start | bytes 405512 | tf_op jit(solution)/shard_map/ppermute | solution.py:128
  142.7 1.5 collective-permute-start.9
  144.7 1.5 collective-permute-start.10
  146.2 9.4 %shard_map.47.refs_16_ = f32[96,128,128]{2,1,0:T(8,128)S(1)} custom-call(s32[3]{0:T(128)S(1)} %pad_add_fusion.info, s32[384]{0:T(512)S(1)} %reshape_squeeze.15.pos, bf16[528,128]{1,0:T(8,128)(2,1)S(1)} %select_select_fusion.7.refs_0_, bf16[528,128]{1,0:T(8,128)(2,1)S(1)} %collective-permute-done.46.refs_1_, ...), custom_call_target="tpu_custom_call" | custom-call | flops 805306368 | bytes 14745600 | tf_op jit(solution)/shard_map/pallas_call | solution.py:85
  155.6 2.6 %copy-done.1 = f32[96,128,128]{2,1,0:T(8,128)} copy-done((f32[96,128,128]{2,1,0:T(8,128)}, f32[96,128,128]{2,1,0:T(8,128)S(1)}, u32[]{:S(2)}) %copy-start.1) | copy-done | bytes 6291480
  158.3 9.4 %shard_map.48.refs_16_ = f32[96,128,128]{2,1,0:T(8,128)S(1)} custom-call(s32[3]{0:T(128)S(1)} %pad_add_fusion.info, s32[384]{0:T(512)S(1)} %reshape_squeeze.15.pos, bf16[528,128]{1,0:T(8,128)(2,1)S(1)} %select_select_fusion.11.refs_0_, bf16[528,128]{1,0:T(8,128)(2,1)S(1)} %collective-permute-done.26.refs_1_, ...), custom_call_target="tpu_custom_call" | custom-call | flops 805306368 | bytes 14745600 | tf_op jit(solution)/shard_map/pallas_call | solution.py:85
  167.8 8.5 %shard_map.49 = bf16[96,128,128]{2,1,0:T(8,128)(2,1)} custom-call(s32[3]{0:T(128)S(1)} %pad_add_fusion.info, s32[384]{0:T(512)S(1)} %reshape_squeeze.15.pos, bf16[528,128]{1,0:T(8,128)(2,1)S(1)} %select_select_fusion.15.refs_0_, bf16[528,128]{1,0:T(8,128)(2,1)S(1)} %collective-permute-done.6.refs_1_, bf16[528,128]{1,0:T(8,128)(2,1)S(1)} %collective-permute-done.7.refs_2_, ...), custom_call_target="tpu_custom_call" | custom-call | flops 805306368 | bytes 14745600 | tf_op jit(solution)/shard_map/pallas_call | solution.py:85
  (134 shorter events, 17.4 us)
Async XLA Ops:
  2.2 14.9 %collective-permute-start.60 = (bf16[528,128]{1,0:T(8,128)(2,1)S(1)}, bf16[528,128]{1,0:T(8,128)(2,1)S(1)}, u32[]{:S(2)}, u32[]{:S(2)}) collective-permute-start(bf16[528,128]{1,0:T(8,128)(2,1)S(1)} %pad_maximum_fusion.3.refs_8_), channel_id=1, source_target_pairs={{2,0},{4,2},{6,4},{3,1},{5,3},{7,5},{10,8},{12,10},{14,12},{11,9},... | collective-permute-start | bytes 405512 | tf_op jit(solution)/shard_map/ppermute | solution.py:154
  3.5 14.9 %collective-permute-start.63 = (bf16[528,128]{1,0:T(8,128)(2,1)S(1)}, bf16[528,128]{1,0:T(8,128)(2,1)S(1)}, u32[]{:S(2)}, u32[]{:S(2)}) collective-permute-start(bf16[528,128]{1,0:T(8,128)(2,1)S(1)} %pad_maximum_fusion.3.refs_8_), channel_id=1, source_target_pairs={{0,2},{2,4},{4,6},{1,3},{3,5},{5,7},{8,10},{10,12},{12,14},{9,11},... | collective-permute-start | bytes 405512 | tf_op jit(solution)/shard_map/ppermute | solution.py:153
  9.0 35.5 %collective-permute-start.76 = (bf16[528,128]{1,0:T(8,128)(2,1)S(1)}, bf16[528,128]{1,0:T(8,128)(2,1)S(1)}, u32[]{:S(2)}, u32[]{:S(2)}) collective-permute-start(bf16[528,128]{1,0:T(8,128)(2,1)S(1)} %pad_maximum_fusion.3.refs_8_), channel_id=1, source_target_pairs={{1,0},{0,1},{3,2},{2,3},{5,4},{4,5},{7,6},{6,7},{9,8},{8,9},{11,10... | collective-permute-start | bytes 405512 | tf_op jit(solution)/shard_map/ppermute | solution.py:120
  11.2 8.0 %collective-permute-start.40 = (bf16[528,128]{1,0:T(8,128)(2,1)S(1)}, bf16[528,128]{1,0:T(8,128)(2,1)S(1)}, u32[]{:S(2)}, u32[]{:S(2)}) collective-permute-start(bf16[528,128]{1,0:T(8,128)(2,1)S(1)} %pad_maximum_fusion.2.refs_8_), channel_id=1, source_target_pairs={{2,0},{4,2},{6,4},{3,1},{5,3},{7,5},{10,8},{12,10},{14,12},{11,9},... | collective-permute-start | bytes 405512 | tf_op jit(solution)/shard_map/ppermute | solution.py:154
  12.5 8.0 %collective-permute-start.43 = (bf16[528,128]{1,0:T(8,128)(2,1)S(1)}, bf16[528,128]{1,0:T(8,128)(2,1)S(1)}, u32[]{:S(2)}, u32[]{:S(2)}) collective-permute-start(bf16[528,128]{1,0:T(8,128)(2,1)S(1)} %pad_maximum_fusion.2.refs_8_), channel_id=1, source_target_pairs={{0,2},{2,4},{4,6},{1,3},{3,5},{5,7},{8,10},{10,12},{12,14},{9,11},... | collective-permute-start | bytes 405512 | tf_op jit(solution)/shard_map/ppermute | solution.py:153
  17.1 6.9 %collective-permute-start.61 = (bf16[528,128]{1,0:T(8,128)(2,1)S(1)}, bf16[528,128]{1,0:T(8,128)(2,1)S(1)}, u32[]{:S(2)}, u32[]{:S(2)}) collective-permute-start(bf16[528,128]{1,0:T(8,128)(2,1)S(1)} %collective-permute-done.60), channel_id=1, source_target_pairs={{2,0},{4,2},{3,1},{5,3},{10,8},{12,10},{11,9},{13,11},{18,16},{20,... | collective-permute-start | bytes 405512 | tf_op jit(solution)/shard_map/ppermute | solution.py:154
  18.4 6.9 %collective-permute-start.64 = (bf16[528,128]{1,0:T(8,128)(2,1)S(1)}, bf16[528,128]{1,0:T(8,128)(2,1)S(1)}, u32[]{:S(2)}, u32[]{:S(2)}) collective-permute-start(bf16[528,128]{1,0:T(8,128)(2,1)S(1)} %collective-permute-done.63), channel_id=1, source_target_pairs={{2,4},{4,6},{3,5},{5,7},{10,12},{12,14},{11,13},{13,15},{18,20},{2... | collective-permute-start | bytes 405512 | tf_op jit(solution)/shard_map/ppermute | solution.py:153
  19.2 10.3 %collective-permute-start.41 = (bf16[528,128]{1,0:T(8,128)(2,1)S(1)}, bf16[528,128]{1,0:T(8,128)(2,1)S(1)}, u32[]{:S(2)}, u32[]{:S(2)}) collective-permute-start(bf16[528,128]{1,0:T(8,128)(2,1)S(1)} %collective-permute-done.40), channel_id=1, source_target_pairs={{2,0},{4,2},{3,1},{5,3},{10,8},{12,10},{11,9},{13,11},{18,16},{20,... | collective-permute-start | bytes 405512 | tf_op jit(solution)/shard_map/ppermute | solution.py:154
  20.5 10.6 %collective-permute-start.44 = (bf16[528,128]{1,0:T(8,128)(2,1)S(1)}, bf16[528,128]{1,0:T(8,128)(2,1)S(1)}, u32[]{:S(2)}, u32[]{:S(2)}) collective-permute-start(bf16[528,128]{1,0:T(8,128)(2,1)S(1)} %collective-permute-done.43), channel_id=1, source_target_pairs={{2,4},{4,6},{3,5},{5,7},{10,12},{12,14},{11,13},{13,15},{18,20},{2... | collective-permute-start | bytes 405512 | tf_op jit(solution)/shard_map/ppermute | solution.py:153
  24.0 10.9 %collective-permute-start.62 = (bf16[528,128]{1,0:T(8,128)(2,1)S(1)}, bf16[528,128]{1,0:T(8,128)(2,1)S(1)}, u32[]{:S(2)}, u32[]{:S(2)}) collective-permute-start(bf16[528,128]{1,0:T(8,128)(2,1)S(1)} %collective-permute-done.61), channel_id=1, source_target_pairs={{2,0},{3,1},{10,8},{11,9},{18,16},{19,17},{26,24},{27,25}} | collective-permute-start | bytes 405512 | tf_op jit(solution)/shard_map/ppermute | solution.py:154
  25.3 10.8 %collective-permute-start.65 = (bf16[528,128]{1,0:T(8,128)(2,1)S(1)}, bf16[528,128]{1,0:T(8,128)(2,1)S(1)}, u32[]{:S(2)}, u32[]{:S(2)}) collective-permute-start(bf16[528,128]{1,0:T(8,128)(2,1)S(1)} %collective-permute-done.64), channel_id=1, source_target_pairs={{4,6},{5,7},{12,14},{13,15},{20,22},{21,23},{28,30},{29,31}} | collective-permute-start | bytes 405512 | tf_op jit(solution)/shard_map/ppermute | solution.py:153
  29.6 15.1 %collective-permute-start.74 = (bf16[528,128]{1,0:T(8,128)(2,1)S(1)}, bf16[528,128]{1,0:T(8,128)(2,1)S(1)}, u32[]{:S(2)}, u32[]{:S(2)}) collective-permute-start(bf16[528,128]{1,0:T(8,128)(2,1)S(1)} %pad_maximum_fusion.3.refs_8_), channel_id=1, source_target_pairs={{0,16},{8,24},{16,0},{24,8},{1,17},{9,25},{17,1},{25,9},{2,18},{10... | collective-permute-start | bytes 405512 | tf_op jit(solution)/shard_map/ppermute | solution.py:117
  31.1 14.9 %collective-permute-start.73 = (bf16[528,128]{1,0:T(8,128)(2,1)S(1)}, bf16[528,128]{1,0:T(8,128)(2,1)S(1)}, u32[]{:S(2)}, u32[]{:S(2)}) collective-permute-start(bf16[528,128]{1,0:T(8,128)(2,1)S(1)} %pad_maximum_fusion.3.refs_8_), channel_id=1, source_target_pairs={{0,8},{8,0},{16,24},{24,16},{1,9},{9,1},{17,25},{25,17},{2,10},{10... | collective-permute-start | bytes 405512 | tf_op jit(solution)/shard_map/ppermute | solution.py:117
  34.8 6.9 %collective-permute-start.42 = (bf16[528,128]{1,0:T(8,128)(2,1)S(1)}, bf16[528,128]{1,0:T(8,128)(2,1)S(1)}, u32[]{:S(2)}, u32[]{:S(2)}) collective-permute-start(bf16[528,128]{1,0:T(8,128)(2,1)S(1)} %collective-permute-done.41), channel_id=1, source_target_pairs={{2,0},{3,1},{10,8},{11,9},{18,16},{19,17},{26,24},{27,25}} | collective-permute-start | bytes 405512 | tf_op jit(solution)/shard_map/ppermute | solution.py:154
  36.1 7.1 %collective-permute-start.45 = (bf16[528,128]{1,0:T(8,128)(2,1)S(1)}, bf16[528,128]{1,0:T(8,128)(2,1)S(1)}, u32[]{:S(2)}, u32[]{:S(2)}) collective-permute-start(bf16[528,128]{1,0:T(8,128)(2,1)S(1)} %collective-permute-done.44), channel_id=1, source_target_pairs={{4,6},{5,7},{12,14},{13,15},{20,22},{21,23},{28,30},{29,31}} | collective-permute-start | bytes 405512 | tf_op jit(solution)/shard_map/ppermute | solution.py:153
  41.7 9.1 %collective-permute-start.54 = (bf16[528,128]{1,0:T(8,128)(2,1)S(1)}, bf16[528,128]{1,0:T(8,128)(2,1)S(1)}, u32[]{:S(2)}, u32[]{:S(2)}) collective-permute-start(bf16[528,128]{1,0:T(8,128)(2,1)S(1)} %pad_maximum_fusion.2.refs_8_), channel_id=1, source_target_pairs={{0,16},{8,24},{16,0},{24,8},{1,17},{9,25},{17,1},{25,9},{2,18},{10... | collective-permute-start | bytes 405512 | tf_op jit(solution)/shard_map/ppermute | solution.py:117
  43.3 9.1 %collective-permute-start.56 = (bf16[528,128]{1,0:T(8,128)(2,1)S(1)}, bf16[528,128]{1,0:T(8,128)(2,1)S(1)}, u32[]{:S(2)}, u32[]{:S(2)}) collective-permute-start(bf16[528,128]{1,0:T(8,128)(2,1)S(1)} %pad_maximum_fusion.2.refs_8_), channel_id=1, source_target_pairs={{1,0},{0,1},{3,2},{2,3},{5,4},{4,5},{7,6},{6,7},{9,8},{8,9},{11,10... | collective-permute-start | bytes 405512 | tf_op jit(solution)/shard_map/ppermute | solution.py:120
  44.6 8.3 %collective-permute-start.53 = (bf16[528,128]{1,0:T(8,128)(2,1)S(1)}, bf16[528,128]{1,0:T(8,128)(2,1)S(1)}, u32[]{:S(2)}, u32[]{:S(2)}) collective-permute-start(bf16[528,128]{1,0:T(8,128)(2,1)S(1)} %pad_maximum_fusion.2.refs_8_), channel_id=1, source_target_pairs={{0,8},{8,0},{16,24},{24,16},{1,9},{9,1},{17,25},{25,17},{2,10},{10... | collective-permute-start | bytes 405512 | tf_op jit(solution)/shard_map/ppermute | solution.py:117
  44.7 8.2 %collective-permute-start.20 = (bf16[528,128]{1,0:T(8,128)(2,1)S(1)}, bf16[528,128]{1,0:T(8,128)(2,1)S(1)}, u32[]{:S(2)}, u32[]{:S(2)}) collective-permute-start(bf16[528,128]{1,0:T(8,128)(2,1)S(1)} %pad_maximum_fusion.1.refs_8_), channel_id=1, source_target_pairs={{2,0},{4,2},{6,4},{3,1},{5,3},{7,5},{10,8},{12,10},{14,12},{11,9},... | collective-permute-start | bytes 405512 | tf_op jit(solution)/shard_map/ppermute | solution.py:154
  46.0 8.2 %collective-permute-start.23 = (bf16[528,128]{1,0:T(8,128)(2,1)S(1)}, bf16[528,128]{1,0:T(8,128)(2,1)S(1)}, u32[]{:S(2)}, u32[]{:S(2)}) collective-permute-start(bf16[528,128]{1,0:T(8,128)(2,1)S(1)} %pad_maximum_fusion.1.refs_8_), channel_id=1, source_target_pairs={{0,2},{2,4},{4,6},{1,3},{3,5},{5,7},{8,10},{10,12},{12,14},{9,11},... | collective-permute-start | bytes 405512 | tf_op jit(solution)/shard_map/ppermute | solution.py:153
  50.8 8.2 %collective-permute-start.36 = (bf16[528,128]{1,0:T(8,128)(2,1)S(1)}, bf16[528,128]{1,0:T(8,128)(2,1)S(1)}, u32[]{:S(2)}, u32[]{:S(2)}) collective-permute-start(bf16[528,128]{1,0:T(8,128)(2,1)S(1)} %pad_maximum_fusion.1.refs_8_), channel_id=1, source_target_pairs={{1,0},{0,1},{3,2},{2,3},{5,4},{4,5},{7,6},{6,7},{9,8},{8,9},{11,10... | collective-permute-start | bytes 405512 | tf_op jit(solution)/shard_map/ppermute | solution.py:120
  52.4 8.3 %collective-permute-start.34 = (bf16[528,128]{1,0:T(8,128)(2,1)S(1)}, bf16[528,128]{1,0:T(8,128)(2,1)S(1)}, u32[]{:S(2)}, u32[]{:S(2)}) collective-permute-start(bf16[528,128]{1,0:T(8,128)(2,1)S(1)} %pad_maximum_fusion.1.refs_8_), channel_id=1, source_target_pairs={{0,16},{8,24},{16,0},{24,8},{1,17},{9,25},{17,1},{25,9},{2,18},{10... | collective-permute-start | bytes 405512 | tf_op jit(solution)/shard_map/ppermute | solution.py:117
  52.9 8.3 %collective-permute-start.33 = (bf16[528,128]{1,0:T(8,128)(2,1)S(1)}, bf16[528,128]{1,0:T(8,128)(2,1)S(1)}, u32[]{:S(2)}, u32[]{:S(2)}) collective-permute-start(bf16[528,128]{1,0:T(8,128)(2,1)S(1)} %pad_maximum_fusion.1.refs_8_), channel_id=1, source_target_pairs={{0,8},{8,0},{16,24},{24,16},{1,9},{9,1},{17,25},{25,17},{2,10},{10... | collective-permute-start | bytes 405512 | tf_op jit(solution)/shard_map/ppermute | solution.py:117
  52.9 8.3 %collective-permute-start = (bf16[528,128]{1,0:T(8,128)(2,1)S(1)}, bf16[528,128]{1,0:T(8,128)(2,1)S(1)}, u32[]{:S(2)}, u32[]{:S(2)}) collective-permute-start(bf16[528,128]{1,0:T(8,128)(2,1)S(1)} %pad_maximum_fusion.refs_8_), channel_id=1, source_target_pairs={{2,0},{4,2},{6,4},{3,1},{5,3},{7,5},{10,8},{12,10},{14,12},{11,9},... | collective-permute-start | bytes 405512 | tf_op jit(solution)/shard_map/ppermute | solution.py:154
  54.2 8.3 %collective-permute-start.3 = (bf16[528,128]{1,0:T(8,128)(2,1)S(1)}, bf16[528,128]{1,0:T(8,128)(2,1)S(1)}, u32[]{:S(2)}, u32[]{:S(2)}) collective-permute-start(bf16[528,128]{1,0:T(8,128)(2,1)S(1)} %pad_maximum_fusion.refs_8_), channel_id=1, source_target_pairs={{0,2},{2,4},{4,6},{1,3},{3,5},{5,7},{8,10},{10,12},{12,14},{9,11},... | collective-permute-start | bytes 405512 | tf_op jit(solution)/shard_map/ppermute | solution.py:153
  61.2 7.9 %collective-permute-start.21 = (bf16[528,128]{1,0:T(8,128)(2,1)S(1)}, bf16[528,128]{1,0:T(8,128)(2,1)S(1)}, u32[]{:S(2)}, u32[]{:S(2)}) collective-permute-start(bf16[528,128]{1,0:T(8,128)(2,1)S(1)} %collective-permute-done.20), channel_id=1, source_target_pairs={{2,0},{4,2},{3,1},{5,3},{10,8},{12,10},{11,9},{13,11},{18,16},{20,... | collective-permute-start | bytes 405512 | tf_op jit(solution)/shard_map/ppermute | solution.py:154
  62.5 7.9 %collective-permute-start.24 = (bf16[528,128]{1,0:T(8,128)(2,1)S(1)}, bf16[528,128]{1,0:T(8,128)(2,1)S(1)}, u32[]{:S(2)}, u32[]{:S(2)}) collective-permute-start(bf16[528,128]{1,0:T(8,128)(2,1)S(1)} %collective-permute-done.23), channel_id=1, source_target_pairs={{2,4},{4,6},{3,5},{5,7},{10,12},{12,14},{11,13},{13,15},{18,20},{2... | collective-permute-start | bytes 405512 | tf_op jit(solution)/shard_map/ppermute | solution.py:153
  64.6 6.8 %collective-permute-start.78 = (bf16[528,128]{1,0:T(8,128)(2,1)S(1)}, bf16[528,128]{1,0:T(8,128)(2,1)S(1)}, u32[]{:S(2)}, u32[]{:S(2)}) collective-permute-start(bf16[528,128]{1,0:T(8,128)(2,1)S(1)} %collective-permute-done.76.refs_12_), channel_id=1, source_target_pairs={{0,16},{8,24},{16,0},{24,8},{1,17},{9,25},{17,1},{25,9},{2,18},{10... | collective-permute-start | bytes 405512 | tf_op jit(solution)/shard_map/ppermute | solution.py:117
  66.1 6.8 %collective-permute-start.77 = (bf16[528,128]{1,0:T(8,128)(2,1)S(1)}, bf16[528,128]{1,0:T(8,128)(2,1)S(1)}, u32[]{:S(2)}, u32[]{:S(2)}) collective-permute-start(bf16[528,128]{1,0:T(8,128)(2,1)S(1)} %collective-permute-done.76.refs_12_), channel_id=1, source_target_pairs={{0,8},{8,0},{16,24},{24,16},{1,9},{9,1},{17,25},{25,17},{2,10},{10... | collective-permute-start | bytes 405512 | tf_op jit(solution)/shard_map/ppermute | solution.py:117
  66.1 6.8 %collective-permute-start.75 = (bf16[528,128]{1,0:T(8,128)(2,1)S(1)}, bf16[528,128]{1,0:T(8,128)(2,1)S(1)}, u32[]{:S(2)}, u32[]{:S(2)}) collective-permute-start(bf16[528,128]{1,0:T(8,128)(2,1)S(1)} %collective-permute-done.74.refs_10_), channel_id=1, source_target_pairs={{0,8},{8,0},{16,24},{24,16},{1,9},{9,1},{17,25},{25,17},{2,10},{10... | collective-permute-start | bytes 405512 | tf_op jit(solution)/shard_map/ppermute | solution.py:117
  69.1 7.1 %collective-permute-start.22 = (bf16[528,128]{1,0:T(8,128)(2,1)S(1)}, bf16[528,128]{1,0:T(8,128)(2,1)S(1)}, u32[]{:S(2)}, u32[]{:S(2)}) collective-permute-start(bf16[528,128]{1,0:T(8,128)(2,1)S(1)} %collective-permute-done.21), channel_id=1, source_target_pairs={{2,0},{3,1},{10,8},{11,9},{18,16},{19,17},{26,24},{27,25}} | collective-permute-start | bytes 405512 | tf_op jit(solution)/shard_map/ppermute | solution.py:154
  77.0 10.4 %collective-permute-start.18 = (bf16[528,128]{1,0:T(8,128)(2,1)S(1)}, bf16[528,128]{1,0:T(8,128)(2,1)S(1)}, u32[]{:S(2)}, u32[]{:S(2)}) collective-permute-start(bf16[528,128]{1,0:T(8,128)(2,1)S(1)} %collective-permute-done.14.refs_10_), channel_id=1, source_target_pairs={{1,0},{0,1},{3,2},{2,3},{5,4},{4,5},{7,6},{6,7},{9,8},{8,9},{11,10... | collective-permute-start | bytes 405512 | tf_op jit(solution)/shard_map/ppermute | solution.py:120
  78.5 8.9 %collective-permute-start.15 = (bf16[528,128]{1,0:T(8,128)(2,1)S(1)}, bf16[528,128]{1,0:T(8,128)(2,1)S(1)}, u32[]{:S(2)}, u32[]{:S(2)}) collective-permute-start(bf16[528,128]{1,0:T(8,128)(2,1)S(1)} %collective-permute-done.14.refs_10_), channel_id=1, source_target_pairs={{0,8},{8,0},{16,24},{24,16},{1,9},{9,1},{17,25},{25,17},{2,10},{10... | collective-permute-start | bytes 405512 | tf_op jit(solution)/shard_map/ppermute | solution.py:117
  79.0 7.8 %collective-permute-start.1 = (bf16[528,128]{1,0:T(8,128)(2,1)S(1)}, bf16[528,128]{1,0:T(8,128)(2,1)S(1)}, u32[]{:S(2)}, u32[]{:S(2)}) collective-permute-start(bf16[528,128]{1,0:T(8,128)(2,1)S(1)} %collective-permute-done), channel_id=1, source_target_pairs={{2,0},{4,2},{3,1},{5,3},{10,8},{12,10},{11,9},{13,11},{18,16},{20,... | collective-permute-start | bytes 405512 | tf_op jit(solution)/shard_map/ppermute | solution.py:154
  80.3 6.5 %collective-permute-start.4 = (bf16[528,128]{1,0:T(8,128)(2,1)S(1)}, bf16[528,128]{1,0:T(8,128)(2,1)S(1)}, u32[]{:S(2)}, u32[]{:S(2)}) collective-permute-start(bf16[528,128]{1,0:T(8,128)(2,1)S(1)} %collective-permute-done.3), channel_id=1, source_target_pairs={{2,4},{4,6},{3,5},{5,7},{10,12},{12,14},{11,13},{13,15},{18,20},{2... | collective-permute-start | bytes 405512 | tf_op jit(solution)/shard_map/ppermute | solution.py:153
  81.3 7.7 %collective-permute-start.17 = (bf16[528,128]{1,0:T(8,128)(2,1)S(1)}, bf16[528,128]{1,0:T(8,128)(2,1)S(1)}, u32[]{:S(2)}, u32[]{:S(2)}) collective-permute-start(bf16[528,128]{1,0:T(8,128)(2,1)S(1)} %collective-permute-done.16.refs_12_), channel_id=1, source_target_pairs={{0,8},{8,0},{16,24},{24,16},{1,9},{9,1},{17,25},{25,17},{2,10},{10... | collective-permute-start | bytes 405512 | tf_op jit(solution)/shard_map/ppermute | solution.py:117
  87.4 8.1 %collective-permute-start.2 = (bf16[528,128]{1,0:T(8,128)(2,1)S(1)}, bf16[528,128]{1,0:T(8,128)(2,1)S(1)}, u32[]{:S(2)}, u32[]{:S(2)}) collective-permute-start(bf16[528,128]{1,0:T(8,128)(2,1)S(1)} %collective-permute-done.1), channel_id=1, source_target_pairs={{2,0},{3,1},{10,8},{11,9},{18,16},{19,17},{26,24},{27,25}} | collective-permute-start | bytes 405512 | tf_op jit(solution)/shard_map/ppermute | solution.py:154
  89.0 6.8 %collective-permute-start.5 = (bf16[528,128]{1,0:T(8,128)(2,1)S(1)}, bf16[528,128]{1,0:T(8,128)(2,1)S(1)}, u32[]{:S(2)}, u32[]{:S(2)}) collective-permute-start(bf16[528,128]{1,0:T(8,128)(2,1)S(1)} %collective-permute-done.4), channel_id=1, source_target_pairs={{4,6},{5,7},{12,14},{13,15},{20,22},{21,23},{28,30},{29,31}} | collective-permute-start | bytes 405512 | tf_op jit(solution)/shard_map/ppermute | solution.py:153
  89.9 7.7 %collective-permute-start.19 = (bf16[528,128]{1,0:T(8,128)(2,1)S(1)}, bf16[528,128]{1,0:T(8,128)(2,1)S(1)}, u32[]{:S(2)}, u32[]{:S(2)}) collective-permute-start(bf16[528,128]{1,0:T(8,128)(2,1)S(1)} %collective-permute-done.18.refs_14_), channel_id=1, source_target_pairs={{0,8},{8,0},{16,24},{24,16},{1,9},{9,1},{17,25},{25,17},{2,10},{10... | collective-permute-start | bytes 405512 | tf_op jit(solution)/shard_map/ppermute | solution.py:117
  90.4 8.7 %collective-permute-start.66 = (bf16[528,128]{1,0:T(8,128)(2,1)S(1)}, bf16[528,128]{1,0:T(8,128)(2,1)S(1)}, u32[]{:S(2)}, u32[]{:S(2)}) collective-permute-start(bf16[528,128]{1,0:T(8,128)(2,1)S(1)} %select_select_fusion.2), channel_id=1, source_target_pairs={{0,8},{8,0},{16,24},{24,16},{1,9},{9,1},{17,25},{25,17},{2,10},{10... | collective-permute-start | bytes 405512 | tf_op jit(solution)/shard_map/ppermute | solution.py:117
  90.5 8.6 %collective-permute-start.67 = (bf16[528,128]{1,0:T(8,128)(2,1)S(1)}, bf16[528,128]{1,0:T(8,128)(2,1)S(1)}, u32[]{:S(2)}, u32[]{:S(2)}) collective-permute-start(bf16[528,128]{1,0:T(8,128)(2,1)S(1)} %select_select_fusion.1), channel_id=1, source_target_pairs={{0,16},{8,24},{16,0},{24,8},{1,17},{9,25},{17,1},{25,9},{2,18},{10... | collective-permute-start | bytes 405512 | tf_op jit(solution)/shard_map/ppermute | solution.py:117
  95.5 8.8 %collective-permute-start.68 = (bf16[528,128]{1,0:T(8,128)(2,1)S(1)}, bf16[528,128]{1,0:T(8,128)(2,1)S(1)}, u32[]{:S(2)}, u32[]{:S(2)}) collective-permute-start(bf16[528,128]{1,0:T(8,128)(2,1)S(1)} %select_select_fusion), channel_id=1, source_target_pairs={{0,24},{8,16},{16,8},{24,0},{1,25},{9,17},{17,9},{25,1},{2,26},{10... | collective-permute-start | bytes 405512 | tf_op jit(solution)/shard_map/ppermute | solution.py:117
  95.8 8.9 %collective-permute-start.72 = (bf16[528,128]{1,0:T(8,128)(2,1)S(1)}, bf16[528,128]{1,0:T(8,128)(2,1)S(1)}, u32[]{:S(2)}, u32[]{:S(2)}) collective-permute-start(bf16[528,128]{1,0:T(8,128)(2,1)S(1)} %select_select_fusion), channel_id=1, source_target_pairs={{25,0},{24,1},{17,8},{16,9},{9,16},{8,17},{1,24},{0,25},{27,2},{26... | collective-permute-start | bytes 405512 | tf_op jit(solution)/shard_map/ppermute | solution.py:128
  97.5 9.1 %collective-permute-start.69 = (bf16[528,128]{1,0:T(8,128)(2,1)S(1)}, bf16[528,128]{1,0:T(8,128)(2,1)S(1)}, u32[]{:S(2)}, u32[]{:S(2)}) collective-permute-start(bf16[528,128]{1,0:T(8,128)(2,1)S(1)} %select_select_fusion.3.refs_0_), channel_id=1, source_target_pairs={{1,0},{0,1},{3,2},{2,3},{5,4},{4,5},{7,6},{6,7},{9,8},{8,9},{11,10... | collective-permute-start | bytes 405512 | tf_op jit(solution)/shard_map/ppermute | solution.py:120
  99.0 7.6 %collective-permute-start.46 = (bf16[528,128]{1,0:T(8,128)(2,1)S(1)}, bf16[528,128]{1,0:T(8,128)(2,1)S(1)}, u32[]{:S(2)}, u32[]{:S(2)}) collective-permute-start(bf16[528,128]{1,0:T(8,128)(2,1)S(1)} %select_select_fusion.6), channel_id=1, source_target_pairs={{0,8},{8,0},{16,24},{24,16},{1,9},{9,1},{17,25},{25,17},{2,10},{10... | collective-permute-start | bytes 405512 | tf_op jit(solution)/shard_map/ppermute | solution.py:117
  99.1 10.2 %collective-permute-start.48 = (bf16[528,128]{1,0:T(8,128)(2,1)S(1)}, bf16[528,128]{1,0:T(8,128)(2,1)S(1)}, u32[]{:S(2)}, u32[]{:S(2)}) collective-permute-start(bf16[528,128]{1,0:T(8,128)(2,1)S(1)} %select_select_fusion.4), channel_id=1, source_target_pairs={{0,24},{8,16},{16,8},{24,0},{1,25},{9,17},{17,9},{25,1},{2,26},{10... | collective-permute-start | bytes 405512 | tf_op jit(solution)/shard_map/ppermute | solution.py:117
  104.3 12.3 %collective-permute-start.47 = (bf16[528,128]{1,0:T(8,128)(2,1)S(1)}, bf16[528,128]{1,0:T(8,128)(2,1)S(1)}, u32[]{:S(2)}, u32[]{:S(2)}) collective-permute-start(bf16[528,128]{1,0:T(8,128)(2,1)S(1)} %select_select_fusion.5), channel_id=1, source_target_pairs={{0,16},{8,24},{16,0},{24,8},{1,17},{9,25},{17,1},{25,9},{2,18},{10... | collective-permute-start | bytes 405512 | tf_op jit(solution)/shard_map/ppermute | solution.py:117
  104.7 12.3 %collective-permute-start.51 = (bf16[528,128]{1,0:T(8,128)(2,1)S(1)}, bf16[528,128]{1,0:T(8,128)(2,1)S(1)}, u32[]{:S(2)}, u32[]{:S(2)}) collective-permute-start(bf16[528,128]{1,0:T(8,128)(2,1)S(1)} %select_select_fusion.5), channel_id=1, source_target_pairs={{17,0},{16,1},{25,8},{24,9},{1,16},{0,17},{9,24},{8,25},{19,2},{18... | collective-permute-start | bytes 405512 | tf_op jit(solution)/shard_map/ppermute | solution.py:128
  106.6 12.0 %collective-permute-start.28 = (bf16[528,128]{1,0:T(8,128)(2,1)S(1)}, bf16[528,128]{1,0:T(8,128)(2,1)S(1)}, u32[]{:S(2)}, u32[]{:S(2)}) collective-permute-start(bf16[528,128]{1,0:T(8,128)(2,1)S(1)} %select_select_fusion.8), channel_id=1, source_target_pairs={{0,24},{8,16},{16,8},{24,0},{1,25},{9,17},{17,9},{25,1},{2,26},{10... | collective-permute-start | bytes 405512 | tf_op jit(solution)/shard_map/ppermute | solution.py:117
  106.6 12.5 %collective-permute-start.32 = (bf16[528,128]{1,0:T(8,128)(2,1)S(1)}, bf16[528,128]{1,0:T(8,128)(2,1)S(1)}, u32[]{:S(2)}, u32[]{:S(2)}) collective-permute-start(bf16[528,128]{1,0:T(8,128)(2,1)S(1)} %select_select_fusion.8), channel_id=1, source_target_pairs={{25,0},{24,1},{17,8},{16,9},{9,16},{8,17},{1,24},{0,25},{27,2},{26... | collective-permute-start | bytes 405512 | tf_op jit(solution)/shard_map/ppermute | solution.py:128
  109.3 7.8 %collective-permute-start.49 = (bf16[528,128]{1,0:T(8,128)(2,1)S(1)}, bf16[528,128]{1,0:T(8,128)(2,1)S(1)}, u32[]{:S(2)}, u32[]{:S(2)}) collective-permute-start(bf16[528,128]{1,0:T(8,128)(2,1)S(1)} %select_select_fusion.7.refs_0_), channel_id=1, source_target_pairs={{1,0},{0,1},{3,2},{2,3},{5,4},{4,5},{7,6},{6,7},{9,8},{8,9},{11,10... | collective-permute-start | bytes 405512 | tf_op jit(solution)/shard_map/ppermute | solution.py:120
  117.1 6.5 %collective-permute-start.29 = (bf16[528,128]{1,0:T(8,128)(2,1)S(1)}, bf16[528,128]{1,0:T(8,128)(2,1)S(1)}, u32[]{:S(2)}, u32[]{:S(2)}) collective-permute-start(bf16[528,128]{1,0:T(8,128)(2,1)S(1)} %select_select_fusion.11.refs_0_), channel_id=1, source_target_pairs={{1,0},{0,1},{3,2},{2,3},{5,4},{4,5},{7,6},{6,7},{9,8},{8,9},{11,10... | collective-permute-start | bytes 405512 | tf_op jit(solution)/shard_map/ppermute | solution.py:120
  119.2 7.3 %collective-permute-start.70 = (bf16[528,128]{1,0:T(8,128)(2,1)S(1)}, bf16[528,128]{1,0:T(8,128)(2,1)S(1)}, u32[]{:S(2)}, u32[]{:S(2)}) collective-permute-start(bf16[528,128]{1,0:T(8,128)(2,1)S(1)} %collective-permute-done.66.refs_1_), channel_id=1, source_target_pairs={{1,0},{0,1},{3,2},{2,3},{5,4},{4,5},{7,6},{6,7},{9,8},{8,9},{11,10... | collective-permute-start | bytes 405512 | tf_op jit(solution)/shard_map/ppermute | solution.py:120
  121.6 7.8 %collective-permute-start.71 = (bf16[528,128]{1,0:T(8,128)(2,1)S(1)}, bf16[528,128]{1,0:T(8,128)(2,1)S(1)}, u32[]{:S(2)}, u32[]{:S(2)}) collective-permute-start(bf16[528,128]{1,0:T(8,128)(2,1)S(1)} %collective-permute-done.67.refs_2_), channel_id=1, source_target_pairs={{1,0},{0,1},{3,2},{2,3},{5,4},{4,5},{7,6},{6,7},{9,8},{8,9},{11,10... | collective-permute-start | bytes 405512 | tf_op jit(solution)/shard_map/ppermute | solution.py:120
  122.2 18.4 %collective-permute-start.6 = (bf16[528,128]{1,0:T(8,128)(2,1)S(1)}, bf16[528,128]{1,0:T(8,128)(2,1)S(1)}, u32[]{:S(2)}, u32[]{:S(2)}) collective-permute-start(bf16[528,128]{1,0:T(8,128)(2,1)S(1)} %select_select_fusion.14), channel_id=1, source_target_pairs={{0,8},{8,0},{16,24},{24,16},{1,9},{9,1},{17,25},{25,17},{2,10},{10... | collective-permute-start | bytes 405512 | tf_op jit(solution)/shard_map/ppermute | solution.py:117
  123.6 18.9 %collective-permute-start.50 = (bf16[528,128]{1,0:T(8,128)(2,1)S(1)}, bf16[528,128]{1,0:T(8,128)(2,1)S(1)}, u32[]{:S(2)}, u32[]{:S(2)}) collective-permute-start(bf16[528,128]{1,0:T(8,128)(2,1)S(1)} %collective-permute-done.46.refs_1_), channel_id=1, source_target_pairs={{1,0},{0,1},{3,2},{2,3},{5,4},{4,5},{7,6},{6,7},{9,8},{8,9},{11,10... | collective-permute-start | bytes 405512 | tf_op jit(solution)/shard_map/ppermute | solution.py:120
  125.0 17.7 %collective-permute-start.52 = (bf16[528,128]{1,0:T(8,128)(2,1)S(1)}, bf16[528,128]{1,0:T(8,128)(2,1)S(1)}, u32[]{:S(2)}, u32[]{:S(2)}) collective-permute-start(bf16[528,128]{1,0:T(8,128)(2,1)S(1)} %collective-permute-done.48.refs_3_), channel_id=1, source_target_pairs={{1,0},{0,1},{3,2},{2,3},{5,4},{4,5},{7,6},{6,7},{9,8},{8,9},{11,10... | collective-permute-start | bytes 405512 | tf_op jit(solution)/shard_map/ppermute | solution.py:120
  126.5 17.7 %collective-permute-start.31 = (bf16[528,128]{1,0:T(8,128)(2,1)S(1)}, bf16[528,128]{1,0:T(8,128)(2,1)S(1)}, u32[]{:S(2)}, u32[]{:S(2)}) collective-permute-start(bf16[528,128]{1,0:T(8,128)(2,1)S(1)} %collective-permute-done.27.refs_2_), channel_id=1, source_target_pairs={{1,0},{0,1},{3,2},{2,3},{5,4},{4,5},{7,6},{6,7},{9,8},{8,9},{11,10... | collective-permute-start | bytes 405512 | tf_op jit(solution)/shard_map/ppermute | solution.py:120
  129.4 15.3 %collective-permute-start.30 = (bf16[528,128]{1,0:T(8,128)(2,1)S(1)}, bf16[528,128]{1,0:T(8,128)(2,1)S(1)}, u32[]{:S(2)}, u32[]{:S(2)}) collective-permute-start(bf16[528,128]{1,0:T(8,128)(2,1)S(1)} %collective-permute-done.26.refs_1_), channel_id=1, source_target_pairs={{1,0},{0,1},{3,2},{2,3},{5,4},{4,5},{7,6},{6,7},{9,8},{8,9},{11,10... | collective-permute-start | bytes 405512 | tf_op jit(solution)/shard_map/ppermute | solution.py:120
  140.6 27.1 %collective-permute-start.11 = (bf16[528,128]{1,0:T(8,128)(2,1)S(1)}, bf16[528,128]{1,0:T(8,128)(2,1)S(1)}, u32[]{:S(2)}, u32[]{:S(2)}) collective-permute-start(bf16[528,128]{1,0:T(8,128)(2,1)S(1)} %select_select_fusion.13), channel_id=1, source_target_pairs={{17,0},{16,1},{25,8},{24,9},{1,16},{0,17},{9,24},{8,25},{19,2},{18... | collective-permute-start | bytes 405512 | tf_op jit(solution)/shard_map/ppermute | solution.py:128
  142.5 25.2 %collective-permute-start.7 = (bf16[528,128]{1,0:T(8,128)(2,1)S(1)}, bf16[528,128]{1,0:T(8,128)(2,1)S(1)}, u32[]{:S(2)}, u32[]{:S(2)}) collective-permute-start(bf16[528,128]{1,0:T(8,128)(2,1)S(1)} %select_select_fusion.13), channel_id=1, source_target_pairs={{0,16},{8,24},{16,0},{24,8},{1,17},{9,25},{17,1},{25,9},{2,18},{10... | collective-permute-start | bytes 405512 | tf_op jit(solution)/shard_map/ppermute | solution.py:117
  142.7 25.1 %collective-permute-start.9 = (bf16[528,128]{1,0:T(8,128)(2,1)S(1)}, bf16[528,128]{1,0:T(8,128)(2,1)S(1)}, u32[]{:S(2)}, u32[]{:S(2)}) collective-permute-start(bf16[528,128]{1,0:T(8,128)(2,1)S(1)} %select_select_fusion.15.refs_0_), channel_id=1, source_target_pairs={{1,0},{0,1},{3,2},{2,3},{5,4},{4,5},{7,6},{6,7},{9,8},{8,9},{11,10... | collective-permute-start | bytes 405512 | tf_op jit(solution)/shard_map/ppermute | solution.py:120
  144.1 23.6 %collective-permute-start.12 = (bf16[528,128]{1,0:T(8,128)(2,1)S(1)}, bf16[528,128]{1,0:T(8,128)(2,1)S(1)}, u32[]{:S(2)}, u32[]{:S(2)}) collective-permute-start(bf16[528,128]{1,0:T(8,128)(2,1)S(1)} %collective-permute-done.8.refs_3_), channel_id=1, source_target_pairs={{1,0},{0,1},{3,2},{2,3},{5,4},{4,5},{7,6},{6,7},{9,8},{8,9},{11,10... | collective-permute-start | bytes 405512 | tf_op jit(solution)/shard_map/ppermute | solution.py:120
  144.7 23.0 %collective-permute-start.10 = (bf16[528,128]{1,0:T(8,128)(2,1)S(1)}, bf16[528,128]{1,0:T(8,128)(2,1)S(1)}, u32[]{:S(2)}, u32[]{:S(2)}) collective-permute-start(bf16[528,128]{1,0:T(8,128)(2,1)S(1)} %collective-permute-done.6.refs_1_), channel_id=1, source_target_pairs={{1,0},{0,1},{3,2},{2,3},{5,4},{4,5},{7,6},{6,7},{9,8},{8,9},{11,10... | collective-permute-start | bytes 405512 | tf_op jit(solution)/shard_map/ppermute | solution.py:120
  (18 other events, 79.7 us)

commit v2 on v0

v2 whole, which is shorter than its diff:
```python
import functools

import jax
import jax.numpy as jnp
from jax import lax
from jax.experimental import pallas as pl
from jax.experimental.pallas import tpu as pltpu
from jax.sharding import PartitionSpec as P

SLOTS = 48
KEY_ROWS = 16


def product_kernel(plan, places, info, pos, *refs):
    n_row, n_depth, n_rows, share, slots, n_chunks, per = plan
    given, out, refs = refs[: len(places)], refs[len(places)], refs[len(places) + 1 :]
    panels, tails, keys, sums, sems, tail_sems = refs
    block = out.shape[-1]
    size = per * n_rows * block
    n_keys = tails.shape[3]
    count, row, depth, kind = info[0], info[1], info[2], info[3]
    chunk, step = pl.program_id(0), pl.program_id(1)

    def start(side, c, src, place):
        d, r = lax.rem(depth + place[1], n_depth), row ^ place[0]
        rows = src.at[pl.ds(c * size, size)]
        pltpu.make_async_copy(rows, panels.at[side, c, d, r], sems.at[side, c]).start()
        if c == 0:
            rows = src.at[pl.ds(n_chunks * size, n_keys)]
            pltpu.make_async_copy(rows, tails.at[side, d, r], tail_sems.at[side]).start()

    @pl.when((chunk == 0) & (step == 0))
    def _():
        for c in range(n_chunks):
            for side, which in ((1, 0), (0, 0), (0, 1), (0, 2)):

                @pl.when((kind == which) | (side == 1))
                def _():
                    for src, (place, use) in zip(given, places):
                        if use == which:
                            start(side, c, src, place)

    for c in range(n_chunks):

        @pl.when((chunk == c) & (step == 0))
        def _(c=c):
            for side in (0, 1):
                pltpu.make_async_copy(panels.at[side, c], panels.at[side, c], sems.at[side, c]).wait()
                if c == 0:
                    pltpu.make_async_copy(tails.at[side], tails.at[side], tail_sems.at[side]).wait()
                    for d in range(n_depth):
                        for r in range(n_row):
                            rows = tails[side, d, r].astype(jnp.float32)
                            for g in range(n_chunks * per):
                                for i in range(n_rows):
                                    at = g * n_rows + i
                                    keys[side, r * n_rows + i, pl.ds(g * n_depth + d, 1), :] = rows[at : at + 1]

        @pl.when(chunk == c)
        def _(c=c):
            for k in range(slots):
                slot = step * slots + k
                u, v, u_row, v_row = [pos[4 * slot + i] for i in range(4)]
                same = (keys[0, u] == keys[1, v]).astype(jnp.float32).astype(jnp.bfloat16)
                lefts, rights = [], []
                for g in range(per):
                    for d in range(n_depth):
                        at = g * n_rows * block
                        key = (c * per + g) * n_depth + d
                        lefts.append(block_of(panels, 0, c, d, u_row + at))
                        rights.append(block_of(panels, 1, c, d, v_row + at) * same[key : key + 1])
                total = lax.dot_general(
                    jnp.concatenate(lefts, 1),
                    jnp.concatenate(rights, 1),
                    (((1,), (1,)), ((), ())),
                    preferred_element_type=jnp.float32,
                )
                if c:
                    total = total + sums[slot]
                if c < n_chunks - 1:
                    sums[slot] = total
                else:
                    out[k] = jnp.where(depth * share + slot < count, total, 0.0).astype(out.dtype)


def block_of(panels, side, c, d, start):
    n_row, size, block = panels.shape[3:]
    flat = panels.reshape(*panels.shape[:3], n_row * size, block)
    return flat[side, c, d, pl.ds(pl.multiple_of(start, block), block), :]


def products(plan, info, pos, pieces):
    n_row, n_depth, n_rows, share, slots, n_chunks, per = plan
    block = pieces[0][0].shape[-1]
    size = per * n_rows * block
    n_keys = -(-n_chunks * per * n_rows // KEY_ROWS) * KEY_ROWS
    places = [(place, use) for _, place, use in pieces]
    args = [pltpu.with_memory_space_constraint(value, pltpu.HBM) for value, _, _ in pieces]
    panel_bytes = 2 * n_chunks * n_depth * n_row * size * block * 2
    held = panel_bytes + 2 * slots * block * block * 2 + share * block * block * 4
    return pl.pallas_call(
        functools.partial(product_kernel, plan, places),
        grid=(n_chunks, share // slots),
        in_specs=[pl.BlockSpec(memory_space=pltpu.SMEM)] * 2 + [pl.BlockSpec(memory_space=pl.ANY)] * len(args),
        out_specs=pl.BlockSpec((slots, block, block), lambda c, i: (jnp.where(c == n_chunks - 1, i, 0), 0, 0)),
        out_shape=jax.ShapeDtypeStruct((share, block, block), jnp.bfloat16),
        scratch_shapes=[
            pltpu.VMEM((2, n_chunks, n_depth, n_row, size, block), jnp.bfloat16),
            pltpu.VMEM((2, n_depth, n_row, n_keys, block), jnp.bfloat16),
            pltpu.VMEM((2, n_row * n_rows, -(-n_chunks * per * n_depth // 8) * 8, block), jnp.float32),
            pltpu.VMEM((share, block, block), jnp.float32),
            pltpu.SemaphoreType.DMA((2, n_chunks)),
            pltpu.SemaphoreType.DMA((2,)),
        ],
        compiler_params=pltpu.CompilerParams(vmem_limit_bytes=held + 4 * 1024 * 1024),
        cost_estimate=pl.CostEstimate(
            flops=2 * share * n_depth * n_chunks * per * block**3,
            bytes_accessed=panel_bytes + share * block * block * 2,
            transcendentals=0,
        ),
    )(info, pos, *args)


def after(value, *others):
    return lax.optimization_barrier((value, *others))[0]


def payload(x_blocks, col_slot):
    n_rows, n_groups, block, _ = x_blocks.shape
    n = n_rows * n_groups
    rows = jnp.swapaxes(x_blocks, 0, 1).reshape(n * block, block)
    keys = jnp.pad(jnp.swapaxes(col_slot, 0, 1).reshape(n).astype(x_blocks.dtype), (0, -n % KEY_ROWS))
    return jnp.concatenate([rows, jnp.broadcast_to(keys[:, None], (keys.shape[0], block))])


def body(sizes, x_blocks, col_slot, out_pos, out_count):
    n_row, n_col, n_depth = sizes
    n_rows, n_groups, block, _ = x_blocks.shape
    share = out_pos.shape[2] // n_depth
    slots = max(k for k in range(1, SLOTS + 1) if share % k == 0)
    n_chunks = 2 if n_groups % 2 == 0 else 1
    per = n_groups // n_chunks
    row, col, depth = lax.axis_index("row"), lax.axis_index("col"), lax.axis_index("depth")
    hops = lax.rem(col - row + n_col, n_col)
    kind = jnp.where(hops == 0, 0, 2 - hops % 2)
    info = jnp.stack([out_count[0, 0], row, depth, kind]).astype(jnp.int32)
    listed = lax.dynamic_slice_in_dim(out_pos[0, 0], depth * share, share)
    starts = listed // n_rows * (per * n_rows * block) + listed % n_rows * block
    pos = jnp.concatenate([listed, starts], 1).reshape(-1)
    evens, others = range(2, n_row, 2), range(1, n_depth)

    def hops_to(i, k, odd):
        ahead = (k - i // 2 * 2 + n_col) % n_col
        return lax.rem(ahead - (ahead + odd) % 2 + n_col, n_col)

    def next_col(value, step):
        return lax.ppermute(value, "col", [(i, (i + step) % n_col) for i in range(n_col)])

    def move(value, t, e, some=False):
        pairs = [
            (((i ^ t) * n_col + k) * n_depth + (j + e) % n_depth, (i * n_col + k) * n_depth + j)
            for i in range(n_row)
            for k in range(n_col)
            for j in range(n_depth)
            if not some or (k - i // 2 * 2) % n_col // 2
        ]
        return lax.ppermute(value, ("row", "col", "depth"), pairs)

    def choose(ring, t, odd):
        away = hops_to(row ^ t, col, odd)
        among = [k for k in range(1, n_col) if k % 2 == odd]
        value = ring[among[0]]
        for k in among[1:]:
            value = jnp.where(away == k, ring[k], value)
        return value

    def between_cores(pieces):
        for (t, e), value in list(pieces.items()):
            pieces[t + 1, e] = move(value, 1, 0)

    own = payload(x_blocks, col_slot)
    ring = {1: next_col(own, 1), n_col - 1: next_col(own, -1)}
    right = {(0, 0): own}
    for e in others:
        right[0, e] = move(own, 0, e)
    for t in evens:
        right[t, 0] = move(own, t, 0)
    for t in evens:
        for e in others:
            right[t, e] = move(right[0, e], t, 0)
    waited = [*ring.values(), *[right[at] for at in right if at != (0, 0)]]

    for k in range(2, n_col // 2 + 1):
        ring[k] = next_col(after(ring[k - 1], *ring.values()), 1)
    for k in range(n_col - 2, n_col // 2, -1):
        ring[k] = next_col(ring[k + 1], -1)
    first = {(0, 0): choose({**ring, 1: after(ring[1], *waited)}, 0, 1)}
    for e in others:
        first[0, e] = move(first[0, 0], 0, e)
    for t in evens:
        first[t, 0] = move(choose({**ring, 1: after(ring[1], *waited)}, t, 1), t, 0)
    waited = [*[first[at] for at in first if at != (0, 0)], *ring.values()]

    for t in evens:
        for e in others:
            first[t, e] = move(after(first[t, 0], *waited), 0, e)
    second = {}
    for t in range(0, n_row, 2):
        value = choose({**ring, 2: after(ring[2], *waited)}, t, 0)
        for e in range(n_depth):
            second[t, e] = move(value, t, e, True) if t or e else value
    for pieces in (right, first, second):
        between_cores(pieces)
    pieces = [(value, at, use) for use, part in enumerate((right, first, second)) for at, value in part.items()]
    plan = (n_row, n_depth, n_rows, share, slots, n_chunks, per)
    return products(plan, info, pos, pieces)[None, None]


def solution(mesh):
    sizes = tuple(mesh.shape[axis] for axis in ("row", "col", "depth"))
    in_specs = (
        P(("row", "col"), "depth", None, None),
        P(("row", "col"), "depth"),
        P("row", "col", None, None),
        P("row", "col"),
    )
    out_specs = P("row", "col", "depth", None, None)
    return jax.shard_map(
        functools.partial(body, sizes), mesh=mesh, in_specs=in_specs, out_specs=out_specs, check_vma=False
    )
```

time: 248 us -> 94.3 us (0.38)
  waiting for transfers between devices: 160 us -> 53.3 us
  local copies, waits for them, and re-layouts: 31.5 us -> 1.56 us
  starting transfers between devices: 0.08 us -> 22.7 us
  matrix products: 22.2 us -> 0 us
  Pallas kernels: 0 us -> 13 us
  between operations: 13.8 us -> 0.87 us
  blocking collectives: 12.7 us -> 0 us
  other arithmetic: 7.33 us -> 2.67 us
    reduce_scatter x1 -> x0, waiting for transfers between devices: 76.2 us -> none  [body(): lax.psum_scatter(jnp.concatenate(blocks_out, 0).astype(jnp.bfloat16), 'de...]
    psum x1 -> x0, waiting for transfers between devices: 56.3 us -> none  [spread(): return lax.psum(kept, axis)]
    ppermute x0 -> x24, waiting for transfers between devices: none -> 53.3 us  [the longest x21 31.9 us: move(): return lax.ppermute(value, ('row', 'col', 'depth'), pairs)]
    gather x8 -> x0, local copies, waits for them, and re-layouts: 31.5 us -> none  [the longest x2 15.3 us: block_terms(): left_blocks = panel_rows[row_slots]]
    all_gather x1 -> x0, waiting for transfers between devices: 26.9 us -> none  [body(): lax.all_gather(x_blocks, 'row', axis=0, tiled=True)]
    ppermute x0 -> x24, starting transfers between devices: none -> 22.7 us  [the longest x21 17.7 us: move(): return lax.ppermute(value, ('row', 'col', 'depth'), pairs)]
    dot_general x2 -> x0, matrix products: 22.2 us -> none  [block_terms(): jnp.einsum('sgab,sgcb->sac', left_blocks, right_masked, preferred_element...]
    pallas_call x0 -> x1, Pallas kernels: none -> 13 us  [products(): pl.pallas_call(functools.partial(product_kernel, plan, places), grid=(n_c...]
  transfers between devices with their start and end apart: 3 -> 24, of which waited for: 3 -> 12; matrix products, arithmetic and copies ran while one was open for 7% -> 2% of each run, Pallas kernels for 0% -> 0%
where the time goes in v2:
time: 94.3 us; the launch traced here: 94 us
  waiting for transfers between devices  53.3 us (57%)
  starting transfers between devices  22.7 us (24%)
  Pallas kernels  13 us (14%)
  other arithmetic  2.67 us (3%)
  local copies, waits for them, and re-layouts  1.56 us (2%)
    ppermute x21, waiting for transfers between devices, move(): return lax.ppermute(value, ('row', 'col', 'depth'), pairs)  31.9 us
    ppermute x3, waiting for transfers between devices, next_col(): lax.ppermute(value, 'col', [(i, (i + step) % n_col) for i in range(n_col)])  21.4 us
    ppermute x21, starting transfers between devices, move(): return lax.ppermute(value, ('row', 'col', 'depth'), pairs)  17.7 us
    pallas_call x1, Pallas kernels, products(): pl.pallas_call(functools.partial(product_kernel, plan, places), grid=(n_c...  13 us
    ppermute x3, starting transfers between devices, next_col(): lax.ppermute(value, 'col', [(i, (i + step) % n_col) for i in range(n_col)])  4.95 us
  transfers between devices with their start and end apart: 24, of which 12 were waited for; matrix products, arithmetic and copies ran while one was open for 2% of the time, Pallas kernels for 0%

profile of v2, /device:TPU:0, one launch (start us, length us, event | category | flops | bytes accessed | tf_op | source)
XLA Modules:
  0.0 94.0 jit_solution(2803315726560677290)
XLA Ops:
  0.0 0.7 convert_bitcast_fusion
  0.7 0.1 copy.11
  0.8 0.1 reshape.16
  0.9 1.1 %copy.10 = bf16[4,4,128,128]{3,2,1,0:T(8,128)(2,1)S(1)} copy(bf16[4,4,128,128]{3,2,0,1:T(8,128)(2,1)} %bitcast.14) | data formatting | bytes 1048576 | tf_op jit(solution)/shard_map/transpose | solution.py:131
  2.0 0.3 pad_maximum_fusion.refs_0_
  2.3 0.0 copy-start
  2.3 3.0 %collective-permute-start = (bf16[2064,128]{1,0:T(8,128)(2,1)S(1)}, bf16[2064,128]{1,0:T(8,128)(2,1)S(1)}, u32[]{:S(2)}, u32[]{:S(2)}) collective-permute-start(bf16[2064,128]{1,0:T(8,128)(2,1)S(1)} %pad_maximum_fusion.refs_0_), channel_id=1, source_target_pairs={{1,0},{0,1},{3,2},{2,3},{5,4},{4,5},{7,6},{6,7},{9,8},{8,9},{11,10... | collective-permute-start | bytes 1585160 | tf_op jit(solution)/shard_map/ppermute | solution.py:167
  5.3 1.6 %collective-permute-start.8 = (bf16[2064,128]{1,0:T(8,128)(2,1)S(1)}, bf16[2064,128]{1,0:T(8,128)(2,1)}, u32[]{:S(2)}, u32[]{:S(2)}) collective-permute-start(bf16[2064,128]{1,0:T(8,128)(2,1)S(1)} %pad_maximum_fusion.refs_0_), channel_id=1, source_target_pairs={{0,2},{2,4},{4,6},{6,0},{1,3},{3,5},{5,7},{7,1},{8,10},{10,12},{12... | collective-permute-start | bytes 1585160 | tf_op jit(solution)/shard_map/ppermute | solution.py:157
  6.9 2.2 %collective-permute-start.7 = (bf16[2064,128]{1,0:T(8,128)(2,1)S(1)}, bf16[2064,128]{1,0:T(8,128)(2,1)S(1)}, u32[]{:S(2)}, u32[]{:S(2)}) collective-permute-start(bf16[2064,128]{1,0:T(8,128)(2,1)S(1)} %pad_maximum_fusion.refs_0_), channel_id=1, source_target_pairs={{0,6},{2,0},{4,2},{6,4},{1,7},{3,1},{5,3},{7,5},{8,14},{10,8},{12,... | collective-permute-start | bytes 1585160 | tf_op jit(solution)/shard_map/ppermute | solution.py:157
  9.2 1.5 %collective-permute-start.1 = (bf16[2064,128]{1,0:T(8,128)(2,1)S(1)}, bf16[2064,128]{1,0:T(8,128)(2,1)S(1)}, u32[]{:S(2)}, u32[]{:S(2)}) collective-permute-start(bf16[2064,128]{1,0:T(8,128)(2,1)S(1)} %pad_maximum_fusion.refs_0_), channel_id=1, source_target_pairs={{16,0},{17,1},{18,2},{19,3},{20,4},{21,5},{22,6},{23,7},{24,8},{25... | collective-permute-start | bytes 1585160 | tf_op jit(solution)/shard_map/ppermute | solution.py:167
  10.7 6.7 %collective-permute-done.refs_1_ = bf16[2064,128]{1,0:T(8,128)(2,1)S(1)} collective-permute-done((bf16[2064,128]{1,0:T(8,128)(2,1)S(1)}, bf16[2064,128]{1,0:T(8,128)(2,1)S(1)}, u32[]{:S(2)}, u32[]{:S(2)}) %collective-permute-start) | collective-permute-done | bytes 528416 | tf_op jit(solution)/shard_map/ppermute | solution.py:167
  17.3 1.8 %collective-permute-start.2 = (bf16[2064,128]{1,0:T(8,128)(2,1)S(1)}, bf16[2064,128]{1,0:T(8,128)(2,1)S(1)}, u32[]{:S(2)}, u32[]{:S(2)}) collective-permute-start(bf16[2064,128]{1,0:T(8,128)(2,1)S(1)} %collective-permute-done.refs_1_), channel_id=1, source_target_pairs={{16,0},{17,1},{18,2},{19,3},{20,4},{21,5},{22,6},{23,7},{24,8},{25... | collective-permute-start | bytes 1585160 | tf_op jit(solution)/shard_map/ppermute | solution.py:167
  19.1 0.0 collective-permute-start.3
  19.1 3.1 %collective-permute-done.8 = bf16[2064,128]{1,0:T(8,128)(2,1)} collective-permute-done((bf16[2064,128]{1,0:T(8,128)(2,1)S(1)}, bf16[2064,128]{1,0:T(8,128)(2,1)}, u32[]{:S(2)}, u32[]{:S(2)}) %collective-permute-start.8) | collective-permute-done | bytes 528416 | tf_op jit(solution)/shard_map/ppermute | solution.py:157
  22.2 9.2 %collective-permute-done.7 = bf16[2064,128]{1,0:T(8,128)(2,1)S(1)} collective-permute-done((bf16[2064,128]{1,0:T(8,128)(2,1)S(1)}, bf16[2064,128]{1,0:T(8,128)(2,1)S(1)}, u32[]{:S(2)}, u32[]{:S(2)}) %collective-permute-start.7) | collective-permute-done | bytes 528416 | tf_op jit(solution)/shard_map/ppermute | solution.py:157
  31.4 1.1 %collective-permute-start.11 = (bf16[2064,128]{1,0:T(8,128)(2,1)}, bf16[2064,128]{1,0:T(8,128)(2,1)S(1)}, u32[]{:S(2)}, u32[]{:S(2)}) collective-permute-start(bf16[2064,128]{1,0:T(8,128)(2,1)} %collective-permute-done.8), channel_id=1, source_target_pairs={{0,2},{2,4},{4,6},{6,0},{1,3},{3,5},{5,7},{7,1},{8,10},{10,12},{12... | collective-permute-start | bytes 1585160 | tf_op jit(solution)/shard_map/ppermute | solution.py:157
  32.6 0.0 collective-permute-done.1.refs_2_
  32.6 0.9 collective-permute-done.2.refs_3_
  33.5 1.5 %broadcast_select_fusion = (bf16[2064,128]{1,0:T(8,128)(2,1)S(1)}, bf16[2064,128]{1,0:T(8,128)(2,1)S(1)}) fusion(bf16[2064,128]{1,0:T(8,128)(2,1)} %copy-done.16, bf16[2064,128]{1,0:T(8,128)(2,1)} %collective-permute-done.8, pred[]{:T(512)S(6)} %eq.19, pred[]{:T(512)S(6)} %eq.18), kind=kLoop, calls=%fused_computation.1 | loop fusion | flops 528384 | bytes 2113538 | tf_op jit(solution)/shard_map/jit(_where)/select_n | solution.py:174
  34.9 1.6 %collective-permute-start.10 = (bf16[2064,128]{1,0:T(8,128)(2,1)S(1)}, bf16[2064,128]{1,0:T(8,128)(2,1)S(1)}, u32[]{:S(2)}, u32[]{:S(2)}) collective-permute-start(bf16[2064,128]{1,0:T(8,128)(2,1)S(1)} %get-tuple-element.15), channel_id=1, source_target_pairs={{16,0},{17,1},{18,2},{19,3},{20,4},{21,5},{22,6},{23,7},{24,8},{25... | collective-permute-start | bytes 1585160 | tf_op jit(solution)/shard_map/ppermute | solution.py:167
  36.5 0.5 collective-permute-start.9
  37.1 0.0 collective-permute-start.5
  37.1 0.0 collective-permute-done.3.refs_4_
  37.1 0.6 collective-permute-start.4
  37.7 9.1 %collective-permute-done.11.refs_16_ = bf16[2064,128]{1,0:T(8,128)(2,1)S(1)} collective-permute-done((bf16[2064,128]{1,0:T(8,128)(2,1)}, bf16[2064,128]{1,0:T(8,128)(2,1)S(1)}, u32[]{:S(2)}, u32[]{:S(2)}) %collective-permute-start.11) | collective-permute-done | bytes 528416 | tf_op jit(solution)/shard_map/ppermute | solution.py:157
  46.7 0.0 copy-done.4
  46.7 0.0 collective-permute-start.6
  46.7 1.2 %collective-permute-done.10.refs_10_ = bf16[2064,128]{1,0:T(8,128)(2,1)S(1)} collective-permute-done((bf16[2064,128]{1,0:T(8,128)(2,1)S(1)}, bf16[2064,128]{1,0:T(8,128)(2,1)S(1)}, u32[]{:S(2)}, u32[]{:S(2)}) %collective-permute-start.10) | collective-permute-done | bytes 528416 | tf_op jit(solution)/shard_map/ppermute | solution.py:167
  48.0 0.0 collective-permute-start.13
  48.0 1.3 %collective-permute-done.9.refs_9_ = bf16[2064,128]{1,0:T(8,128)(2,1)} collective-permute-done((bf16[2064,128]{1,0:T(8,128)(2,1)S(1)}, bf16[2064,128]{1,0:T(8,128)(2,1)}, u32[]{:S(2)}, u32[]{:S(2)}) %collective-permute-start.9) | collective-permute-done | bytes 528416 | tf_op jit(solution)/shard_map/ppermute | solution.py:167
  49.3 0.0 collective-permute-start.15
  49.3 0.0 collective-permute-done.5.refs_6_
  49.3 0.6 collective-permute-start.12
  49.9 0.0 collective-permute-done.4.refs_5_
  49.9 0.2 collective-permute-start.20
  50.1 0.0 collective-permute-done.6.refs_7_
  50.1 3.4 %collective-permute-start.19 = (bf16[2064,128]{1,0:T(8,128)(2,1)S(1)}, bf16[2064,128]{1,0:T(8,128)(2,1)S(1)}, u32[]{:S(2)}, u32[]{:S(2)}) collective-permute-start(bf16[2064,128]{1,0:T(8,128)(2,1)S(1)} %collective-permute-done.11.refs_16_), channel_id=1, source_target_pairs={{21,4},{20,5},{23,6},{22,7},{29,12},{28,13},{31,14},{30,15},{1,16}... | collective-permute-start | bytes 1585160 | tf_op jit(solution)/shard_map/ppermute | solution.py:167
  53.5 0.0 collective-permute-done.13.refs_12_
  53.5 2.1 %collective-permute-start.18 = (bf16[2064,128]{1,0:T(8,128)(2,1)S(1)}, bf16[2064,128]{1,0:T(8,128)(2,1)}, u32[]{:S(2)}, u32[]{:S(2)}) collective-permute-start(bf16[2064,128]{1,0:T(8,128)(2,1)S(1)} %collective-permute-done.11.refs_16_), channel_id=1, source_target_pairs={{20,4},{21,5},{22,6},{23,7},{28,12},{29,13},{30,14},{31,15},{0,16}... | collective-permute-start | bytes 1585160 | tf_op jit(solution)/shard_map/ppermute | solution.py:167
  55.6 0.0 collective-permute-done.15.refs_14_
  55.6 1.5 %collective-permute-start.17 = (bf16[2064,128]{1,0:T(8,128)(2,1)S(1)}, bf16[2064,128]{1,0:T(8,128)(2,1)}, u32[]{:S(2)}, u32[]{:S(2)}) collective-permute-start(bf16[2064,128]{1,0:T(8,128)(2,1)S(1)} %collective-permute-done.11.refs_16_), channel_id=1, source_target_pairs={{5,4},{4,5},{7,6},{6,7},{13,12},{12,13},{15,14},{14,15},{17,16},{1... | collective-permute-start | bytes 1585160 | tf_op jit(solution)/shard_map/ppermute | solution.py:167
  57.1 7.1 %collective-permute-done.12.refs_11_ = bf16[2064,128]{1,0:T(8,128)(2,1)S(1)} collective-permute-done((bf16[2064,128]{1,0:T(8,128)(2,1)S(1)}, bf16[2064,128]{1,0:T(8,128)(2,1)S(1)}, u32[]{:S(2)}, u32[]{:S(2)}) %collective-permute-start.12) | collective-permute-done | bytes 528416 | tf_op jit(solution)/shard_map/ppermute | solution.py:167
  64.2 0.0 collective-permute-start.14
  64.2 0.0 collective-permute-done.20.refs_20_
  64.2 0.5 collective-permute-start.16
  64.7 8.4 %collective-permute-done.19.refs_19_ = bf16[2064,128]{1,0:T(8,128)(2,1)S(1)} collective-permute-done((bf16[2064,128]{1,0:T(8,128)(2,1)S(1)}, bf16[2064,128]{1,0:T(8,128)(2,1)S(1)}, u32[]{:S(2)}, u32[]{:S(2)}) %collective-permute-start.19) | collective-permute-done | bytes 528416 | tf_op jit(solution)/shard_map/ppermute | solution.py:167
  73.2 0.0 collective-permute-start.23
  73.2 4.8 %collective-permute-done.18.refs_18_ = bf16[2064,128]{1,0:T(8,128)(2,1)} collective-permute-done((bf16[2064,128]{1,0:T(8,128)(2,1)S(1)}, bf16[2064,128]{1,0:T(8,128)(2,1)}, u32[]{:S(2)}, u32[]{:S(2)}) %collective-permute-start.18) | collective-permute-done | bytes 528416 | tf_op jit(solution)/shard_map/ppermute | solution.py:167
  78.0 0.0 collective-permute-start.22
  78.0 0.0 collective-permute-done.17.refs_17_
  78.0 0.0 copy-done.8
  78.0 0.0 copy-done.10
  78.0 0.0 copy-done.11
  78.1 0.6 collective-permute-start.21
  79.3 0.1 fusion.1
  79.4 0.1 copy.9
  79.5 0.1 reshape.14.pos
  79.6 0.1 pad_add_fusion.1.info
  79.7 0.0 collective-permute-done.14.refs_13_
  79.7 0.0 collective-permute-done.16.refs_15_
  79.7 0.0 collective-permute-done.23.refs_23_
  79.7 0.6 collective-permute-done.22.refs_22_
  80.3 0.8 collective-permute-done.21.refs_21_
  81.1 13.0 %shard_map.46 = bf16[96,128,128]{2,1,0:T(8,128)(2,1)} custom-call(s32[4]{0:T(128)S(1)} %pad_add_fusion.1.info, s32[384]{0:T(512)S(1)} %reshape.14.pos, bf16[2064,128]{1,0:T(8,128)(2,1)} %copy-done, bf16[2064,128]{1,0:T(8,128)(2,1)} %copy-done.2, bf16[2064,128]{1,0:T(8,128)(2,1)} %copy-done.3, bf16[2064,128]{1,0:T(8,128)(2,1)} %copy-done.4, ...), custom_call_target="tpu_custom_call" | custom-call | flops 3221225472 | bytes 11534336 | tf_op jit(solution)/shard_map/pallas_call | solution.py:101
  (33 shorter events, 0.1 us)
Async XLA Ops:
  2.3 32.6 %copy-start = (bf16[2064,128]{1,0:T(8,128)(2,1)}, bf16[2064,128]{1,0:T(8,128)(2,1)S(1)}, u32[]{:S(2)}) copy-start(bf16[2064,128]{1,0:T(8,128)(2,1)S(1)} %pad_maximum_fusion.refs_0_) | copy-start | bytes 1585156
  2.3 15.0 %collective-permute-start = (bf16[2064,128]{1,0:T(8,128)(2,1)S(1)}, bf16[2064,128]{1,0:T(8,128)(2,1)S(1)}, u32[]{:S(2)}, u32[]{:S(2)}) collective-permute-start(bf16[2064,128]{1,0:T(8,128)(2,1)S(1)} %pad_maximum_fusion.refs_0_), channel_id=1, source_target_pairs={{1,0},{0,1},{3,2},{2,3},{5,4},{4,5},{7,6},{6,7},{9,8},{8,9},{11,10... | collective-permute-start | bytes 1585160 | tf_op jit(solution)/shard_map/ppermute | solution.py:167
  5.3 16.9 %collective-permute-start.8 = (bf16[2064,128]{1,0:T(8,128)(2,1)S(1)}, bf16[2064,128]{1,0:T(8,128)(2,1)}, u32[]{:S(2)}, u32[]{:S(2)}) collective-permute-start(bf16[2064,128]{1,0:T(8,128)(2,1)S(1)} %pad_maximum_fusion.refs_0_), channel_id=1, source_target_pairs={{0,2},{2,4},{4,6},{6,0},{1,3},{3,5},{5,7},{7,1},{8,10},{10,12},{12... | collective-permute-start | bytes 1585160 | tf_op jit(solution)/shard_map/ppermute | solution.py:157
  6.9 24.5 %collective-permute-start.7 = (bf16[2064,128]{1,0:T(8,128)(2,1)S(1)}, bf16[2064,128]{1,0:T(8,128)(2,1)S(1)}, u32[]{:S(2)}, u32[]{:S(2)}) collective-permute-start(bf16[2064,128]{1,0:T(8,128)(2,1)S(1)} %pad_maximum_fusion.refs_0_), channel_id=1, source_target_pairs={{0,6},{2,0},{4,2},{6,4},{1,7},{3,1},{5,3},{7,5},{8,14},{10,8},{12,... | collective-permute-start | bytes 1585160 | tf_op jit(solution)/shard_map/ppermute | solution.py:157
  9.2 23.4 %collective-permute-start.1 = (bf16[2064,128]{1,0:T(8,128)(2,1)S(1)}, bf16[2064,128]{1,0:T(8,128)(2,1)S(1)}, u32[]{:S(2)}, u32[]{:S(2)}) collective-permute-start(bf16[2064,128]{1,0:T(8,128)(2,1)S(1)} %pad_maximum_fusion.refs_0_), channel_id=1, source_target_pairs={{16,0},{17,1},{18,2},{19,3},{20,4},{21,5},{22,6},{23,7},{24,8},{25... | collective-permute-start | bytes 1585160 | tf_op jit(solution)/shard_map/ppermute | solution.py:167
  17.3 19.7 %copy-start.2 = (bf16[2064,128]{1,0:T(8,128)(2,1)}, bf16[2064,128]{1,0:T(8,128)(2,1)S(1)}, u32[]{:S(2)}) copy-start(bf16[2064,128]{1,0:T(8,128)(2,1)S(1)} %collective-permute-done.refs_1_) | copy-start | bytes 1585156
  17.3 16.1 %collective-permute-start.2 = (bf16[2064,128]{1,0:T(8,128)(2,1)S(1)}, bf16[2064,128]{1,0:T(8,128)(2,1)S(1)}, u32[]{:S(2)}, u32[]{:S(2)}) collective-permute-start(bf16[2064,128]{1,0:T(8,128)(2,1)S(1)} %collective-permute-done.refs_1_), channel_id=1, source_target_pairs={{16,0},{17,1},{18,2},{19,3},{20,4},{21,5},{22,6},{23,7},{24,8},{25... | collective-permute-start | bytes 1585160 | tf_op jit(solution)/shard_map/ppermute | solution.py:167
  19.1 18.0 %collective-permute-start.3 = (bf16[2064,128]{1,0:T(8,128)(2,1)S(1)}, bf16[2064,128]{1,0:T(8,128)(2,1)S(1)}, u32[]{:S(2)}, u32[]{:S(2)}) collective-permute-start(bf16[2064,128]{1,0:T(8,128)(2,1)S(1)} %pad_maximum_fusion.refs_0_), channel_id=1, source_target_pairs={{8,0},{9,1},{10,2},{11,3},{12,4},{13,5},{14,6},{15,7},{0,8},{1,9},... | collective-permute-start | bytes 1585160 | tf_op jit(solution)/shard_map/ppermute | solution.py:167
  19.1 60.2 %copy-start.17 = (s32[1,1,192,2]{2,3,1,0:T(2,128)S(1)}, s32[1,1,192,2]{2,3,1,0:T(2,128)}, u32[]{:S(2)}) copy-start(s32[1,1,192,2]{2,3,1,0:T(2,128)} %param.6) | copy-start | bytes 4612
  31.4 1.1 %copy-start.16 = (bf16[2064,128]{1,0:T(8,128)(2,1)}, bf16[2064,128]{1,0:T(8,128)(2,1)S(1)}, u32[]{:S(2)}) copy-start(bf16[2064,128]{1,0:T(8,128)(2,1)S(1)} %collective-permute-done.7) | copy-start | bytes 1585156
  31.4 15.3 %collective-permute-start.11 = (bf16[2064,128]{1,0:T(8,128)(2,1)}, bf16[2064,128]{1,0:T(8,128)(2,1)S(1)}, u32[]{:S(2)}, u32[]{:S(2)}) collective-permute-start(bf16[2064,128]{1,0:T(8,128)(2,1)} %collective-permute-done.8), channel_id=1, source_target_pairs={{0,2},{2,4},{4,6},{6,0},{1,3},{3,5},{5,7},{7,1},{8,10},{10,12},{12... | collective-permute-start | bytes 1585160 | tf_op jit(solution)/shard_map/ppermute | solution.py:157
  32.6 4.5 %copy-start.3 = (bf16[2064,128]{1,0:T(8,128)(2,1)}, bf16[2064,128]{1,0:T(8,128)(2,1)S(1)}, u32[]{:S(2)}) copy-start(bf16[2064,128]{1,0:T(8,128)(2,1)S(1)} %collective-permute-done.1.refs_2_) | copy-start | bytes 1585156
  33.5 13.3 %copy-start.4 = (bf16[2064,128]{1,0:T(8,128)(2,1)}, bf16[2064,128]{1,0:T(8,128)(2,1)S(1)}, u32[]{:S(2)}) copy-start(bf16[2064,128]{1,0:T(8,128)(2,1)S(1)} %collective-permute-done.2.refs_3_) | copy-start | bytes 1585156
  34.9 46.1 %copy-start.1 = (bf16[2064,128]{1,0:T(8,128)(2,1)}, bf16[2064,128]{1,0:T(8,128)(2,1)S(1)}, u32[]{:S(2)}) copy-start(bf16[2064,128]{1,0:T(8,128)(2,1)S(1)} %get-tuple-element.16.refs_8_) | copy-start | bytes 1585156
  34.9 13.0 %collective-permute-start.10 = (bf16[2064,128]{1,0:T(8,128)(2,1)S(1)}, bf16[2064,128]{1,0:T(8,128)(2,1)S(1)}, u32[]{:S(2)}, u32[]{:S(2)}) collective-permute-start(bf16[2064,128]{1,0:T(8,128)(2,1)S(1)} %get-tuple-element.15), channel_id=1, source_target_pairs={{16,0},{17,1},{18,2},{19,3},{20,4},{21,5},{22,6},{23,7},{24,8},{25... | collective-permute-start | bytes 1585160 | tf_op jit(solution)/shard_map/ppermute | solution.py:167
  36.5 12.8 %collective-permute-start.9 = (bf16[2064,128]{1,0:T(8,128)(2,1)S(1)}, bf16[2064,128]{1,0:T(8,128)(2,1)}, u32[]{:S(2)}, u32[]{:S(2)}) collective-permute-start(bf16[2064,128]{1,0:T(8,128)(2,1)S(1)} %get-tuple-element.16.refs_8_), channel_id=1, source_target_pairs={{1,0},{0,1},{3,2},{2,3},{5,4},{4,5},{7,6},{6,7},{9,8},{8,9},{11,10... | collective-permute-start | bytes 1585160 | tf_op jit(solution)/shard_map/ppermute | solution.py:167
  37.1 12.3 %collective-permute-start.5 = (bf16[2064,128]{1,0:T(8,128)(2,1)S(1)}, bf16[2064,128]{1,0:T(8,128)(2,1)S(1)}, u32[]{:S(2)}, u32[]{:S(2)}) collective-permute-start(bf16[2064,128]{1,0:T(8,128)(2,1)S(1)} %collective-permute-done.1.refs_2_), channel_id=1, source_target_pairs={{8,0},{9,1},{10,2},{11,3},{12,4},{13,5},{14,6},{15,7},{0,8},{1,9},... | collective-permute-start | bytes 1585160 | tf_op jit(solution)/shard_map/ppermute | solution.py:167
  37.1 43.9 %copy-start.5 = (bf16[2064,128]{1,0:T(8,128)(2,1)}, bf16[2064,128]{1,0:T(8,128)(2,1)S(1)}, u32[]{:S(2)}) copy-start(bf16[2064,128]{1,0:T(8,128)(2,1)S(1)} %collective-permute-done.3.refs_4_) | copy-start | bytes 1585156
  37.1 12.8 %collective-permute-start.4 = (bf16[2064,128]{1,0:T(8,128)(2,1)S(1)}, bf16[2064,128]{1,0:T(8,128)(2,1)S(1)}, u32[]{:S(2)}, u32[]{:S(2)}) collective-permute-start(bf16[2064,128]{1,0:T(8,128)(2,1)S(1)} %collective-permute-done.refs_1_), channel_id=1, source_target_pairs={{8,0},{9,1},{10,2},{11,3},{12,4},{13,5},{14,6},{15,7},{0,8},{1,9},... | collective-permute-start | bytes 1585160 | tf_op jit(solution)/shard_map/ppermute | solution.py:167
  46.7 8.9 %copy-start.6 = (bf16[2064,128]{1,0:T(8,128)(2,1)}, bf16[2064,128]{1,0:T(8,128)(2,1)S(1)}, u32[]{:S(2)}) copy-start(bf16[2064,128]{1,0:T(8,128)(2,1)S(1)} %collective-permute-done.11.refs_16_) | copy-start | bytes 1585156
  46.7 3.4 %collective-permute-start.6 = (bf16[2064,128]{1,0:T(8,128)(2,1)S(1)}, bf16[2064,128]{1,0:T(8,128)(2,1)S(1)}, u32[]{:S(2)}, u32[]{:S(2)}) collective-permute-start(bf16[2064,128]{1,0:T(8,128)(2,1)S(1)} %collective-permute-done.2.refs_3_), channel_id=1, source_target_pairs={{8,0},{9,1},{10,2},{11,3},{12,4},{13,5},{14,6},{15,7},{0,8},{1,9},... | collective-permute-start | bytes 1585160 | tf_op jit(solution)/shard_map/ppermute | solution.py:167
  48.0 30.0 %copy-start.7 = (bf16[2064,128]{1,0:T(8,128)(2,1)}, bf16[2064,128]{1,0:T(8,128)(2,1)S(1)}, u32[]{:S(2)}) copy-start(bf16[2064,128]{1,0:T(8,128)(2,1)S(1)} %collective-permute-done.10.refs_10_) | copy-start | bytes 1585156
  48.0 5.5 %collective-permute-start.13 = (bf16[2064,128]{1,0:T(8,128)(2,1)S(1)}, bf16[2064,128]{1,0:T(8,128)(2,1)S(1)}, u32[]{:S(2)}, u32[]{:S(2)}) collective-permute-start(bf16[2064,128]{1,0:T(8,128)(2,1)S(1)} %get-tuple-element.16.refs_8_), channel_id=1, source_target_pairs={{8,0},{9,1},{10,2},{11,3},{12,4},{13,5},{14,6},{15,7},{0,8},{1,9},... | collective-permute-start | bytes 1585160 | tf_op jit(solution)/shard_map/ppermute | solution.py:167
  49.3 6.3 %collective-permute-start.15 = (bf16[2064,128]{1,0:T(8,128)(2,1)S(1)}, bf16[2064,128]{1,0:T(8,128)(2,1)S(1)}, u32[]{:S(2)}, u32[]{:S(2)}) collective-permute-start(bf16[2064,128]{1,0:T(8,128)(2,1)S(1)} %collective-permute-done.10.refs_10_), channel_id=1, source_target_pairs={{8,0},{9,1},{10,2},{11,3},{12,4},{13,5},{14,6},{15,7},{0,8},{1,9},... | collective-permute-start | bytes 1585160 | tf_op jit(solution)/shard_map/ppermute | solution.py:167
  49.3 28.7 %copy-start.8 = (bf16[2064,128]{1,0:T(8,128)(2,1)}, bf16[2064,128]{1,0:T(8,128)(2,1)S(1)}, u32[]{:S(2)}) copy-start(bf16[2064,128]{1,0:T(8,128)(2,1)S(1)} %collective-permute-done.5.refs_6_) | copy-start | bytes 1585156
  49.3 14.9 %collective-permute-start.12 = (bf16[2064,128]{1,0:T(8,128)(2,1)S(1)}, bf16[2064,128]{1,0:T(8,128)(2,1)S(1)}, u32[]{:S(2)}, u32[]{:S(2)}) collective-permute-start(bf16[2064,128]{1,0:T(8,128)(2,1)S(1)} %collective-permute-done.10.refs_10_), channel_id=1, source_target_pairs={{1,0},{0,1},{3,2},{2,3},{5,4},{4,5},{7,6},{6,7},{9,8},{8,9},{11,10... | collective-permute-start | bytes 1585160 | tf_op jit(solution)/shard_map/ppermute | solution.py:167
  49.9 31.1 %copy-start.9 = (bf16[2064,128]{1,0:T(8,128)(2,1)}, bf16[2064,128]{1,0:T(8,128)(2,1)S(1)}, u32[]{:S(2)}) copy-start(bf16[2064,128]{1,0:T(8,128)(2,1)S(1)} %collective-permute-done.4.refs_5_) | copy-start | bytes 1585156
  49.9 14.3 %collective-permute-start.20 = (bf16[2064,128]{1,0:T(8,128)(2,1)S(1)}, bf16[2064,128]{1,0:T(8,128)(2,1)S(1)}, u32[]{:S(2)}, u32[]{:S(2)}) collective-permute-start(bf16[2064,128]{1,0:T(8,128)(2,1)S(1)} %collective-permute-done.11.refs_16_), channel_id=1, source_target_pairs={{8,0},{9,1},{10,2},{11,3},{12,4},{13,5},{14,6},{15,7},{0,8},{1,9},... | collective-permute-start | bytes 1585160 | tf_op jit(solution)/shard_map/ppermute | solution.py:167
  50.1 27.9 %copy-start.10 = (bf16[2064,128]{1,0:T(8,128)(2,1)}, bf16[2064,128]{1,0:T(8,128)(2,1)S(1)}, u32[]{:S(2)}) copy-start(bf16[2064,128]{1,0:T(8,128)(2,1)S(1)} %collective-permute-done.6.refs_7_) | copy-start | bytes 1585156
  50.1 23.1 %collective-permute-start.19 = (bf16[2064,128]{1,0:T(8,128)(2,1)S(1)}, bf16[2064,128]{1,0:T(8,128)(2,1)S(1)}, u32[]{:S(2)}, u32[]{:S(2)}) collective-permute-start(bf16[2064,128]{1,0:T(8,128)(2,1)S(1)} %collective-permute-done.11.refs_16_), channel_id=1, source_target_pairs={{21,4},{20,5},{23,6},{22,7},{29,12},{28,13},{31,14},{30,15},{1,16}... | collective-permute-start | bytes 1585160 | tf_op jit(solution)/shard_map/ppermute | solution.py:167
  53.5 24.5 %copy-start.11 = (bf16[2064,128]{1,0:T(8,128)(2,1)}, bf16[2064,128]{1,0:T(8,128)(2,1)S(1)}, u32[]{:S(2)}) copy-start(bf16[2064,128]{1,0:T(8,128)(2,1)S(1)} %collective-permute-done.13.refs_12_) | copy-start | bytes 1585156
  53.5 24.5 %collective-permute-start.18 = (bf16[2064,128]{1,0:T(8,128)(2,1)S(1)}, bf16[2064,128]{1,0:T(8,128)(2,1)}, u32[]{:S(2)}, u32[]{:S(2)}) collective-permute-start(bf16[2064,128]{1,0:T(8,128)(2,1)S(1)} %collective-permute-done.11.refs_16_), channel_id=1, source_target_pairs={{20,4},{21,5},{22,6},{23,7},{28,12},{29,13},{30,14},{31,15},{0,16}... | collective-permute-start | bytes 1585160 | tf_op jit(solution)/shard_map/ppermute | solution.py:167
  55.6 22.4 %copy-start.12 = (bf16[2064,128]{1,0:T(8,128)(2,1)}, bf16[2064,128]{1,0:T(8,128)(2,1)S(1)}, u32[]{:S(2)}) copy-start(bf16[2064,128]{1,0:T(8,128)(2,1)S(1)} %collective-permute-done.15.refs_14_) | copy-start | bytes 1585156
  55.6 22.4 %collective-permute-start.17 = (bf16[2064,128]{1,0:T(8,128)(2,1)S(1)}, bf16[2064,128]{1,0:T(8,128)(2,1)}, u32[]{:S(2)}, u32[]{:S(2)}) collective-permute-start(bf16[2064,128]{1,0:T(8,128)(2,1)S(1)} %collective-permute-done.11.refs_16_), channel_id=1, source_target_pairs={{5,4},{4,5},{7,6},{6,7},{13,12},{12,13},{15,14},{14,15},{17,16},{1... | collective-permute-start | bytes 1585160 | tf_op jit(solution)/shard_map/ppermute | solution.py:167
  64.2 16.8 %copy-start.13 = (bf16[2064,128]{1,0:T(8,128)(2,1)}, bf16[2064,128]{1,0:T(8,128)(2,1)S(1)}, u32[]{:S(2)}) copy-start(bf16[2064,128]{1,0:T(8,128)(2,1)S(1)} %collective-permute-done.12.refs_11_) | copy-start | bytes 1585156
  64.2 15.5 %collective-permute-start.14 = (bf16[2064,128]{1,0:T(8,128)(2,1)}, bf16[2064,128]{1,0:T(8,128)(2,1)}, u32[]{:S(2)}, u32[]{:S(2)}) collective-permute-start(bf16[2064,128]{1,0:T(8,128)(2,1)} %collective-permute-done.9.refs_9_), channel_id=1, source_target_pairs={{8,0},{9,1},{10,2},{11,3},{12,4},{13,5},{14,6},{15,7},{0,8},{1,9},... | collective-permute-start | bytes 1585160 | tf_op jit(solution)/shard_map/ppermute | solution.py:167
  64.2 16.8 %copy-start.14 = (bf16[2064,128]{1,0:T(8,128)(2,1)}, bf16[2064,128]{1,0:T(8,128)(2,1)S(1)}, u32[]{:S(2)}) copy-start(bf16[2064,128]{1,0:T(8,128)(2,1)S(1)} %collective-permute-done.20.refs_20_) | copy-start | bytes 1585156
  64.2 15.4 %collective-permute-start.16 = (bf16[2064,128]{1,0:T(8,128)(2,1)S(1)}, bf16[2064,128]{1,0:T(8,128)(2,1)}, u32[]{:S(2)}, u32[]{:S(2)}) collective-permute-start(bf16[2064,128]{1,0:T(8,128)(2,1)S(1)} %collective-permute-done.12.refs_11_), channel_id=1, source_target_pairs={{8,0},{9,1},{10,2},{11,3},{12,4},{13,5},{14,6},{15,7},{0,8},{1,9},... | collective-permute-start | bytes 1585160 | tf_op jit(solution)/shard_map/ppermute | solution.py:167
  73.2 7.9 %copy-start.15 = (bf16[2064,128]{1,0:T(8,128)(2,1)}, bf16[2064,128]{1,0:T(8,128)(2,1)S(1)}, u32[]{:S(2)}) copy-start(bf16[2064,128]{1,0:T(8,128)(2,1)S(1)} %collective-permute-done.19.refs_19_) | copy-start | bytes 1585156
  73.2 6.5 %collective-permute-start.23 = (bf16[2064,128]{1,0:T(8,128)(2,1)S(1)}, bf16[2064,128]{1,0:T(8,128)(2,1)}, u32[]{:S(2)}, u32[]{:S(2)}) collective-permute-start(bf16[2064,128]{1,0:T(8,128)(2,1)S(1)} %collective-permute-done.19.refs_19_), channel_id=1, source_target_pairs={{8,0},{9,1},{10,2},{11,3},{12,4},{13,5},{14,6},{15,7},{0,8},{1,9},... | collective-permute-start | bytes 1585160 | tf_op jit(solution)/shard_map/ppermute | solution.py:167
  78.0 2.3 %collective-permute-start.22 = (bf16[2064,128]{1,0:T(8,128)(2,1)}, bf16[2064,128]{1,0:T(8,128)(2,1)}, u32[]{:S(2)}, u32[]{:S(2)}) collective-permute-start(bf16[2064,128]{1,0:T(8,128)(2,1)} %collective-permute-done.18.refs_18_), channel_id=1, source_target_pairs={{8,0},{9,1},{10,2},{11,3},{12,4},{13,5},{14,6},{15,7},{0,8},{1,9},... | collective-permute-start | bytes 1585160 | tf_op jit(solution)/shard_map/ppermute | solution.py:167
  78.1 3.0 %collective-permute-start.21 = (bf16[2064,128]{1,0:T(8,128)(2,1)}, bf16[2064,128]{1,0:T(8,128)(2,1)}, u32[]{:S(2)}, u32[]{:S(2)}) collective-permute-start(bf16[2064,128]{1,0:T(8,128)(2,1)} %collective-permute-done.17.refs_17_), channel_id=1, source_target_pairs={{8,0},{9,1},{10,2},{11,3},{12,4},{13,5},{14,6},{15,7},{0,8},{1,9},... | collective-permute-start | bytes 1585160 | tf_op jit(solution)/shard_map/ppermute | solution.py:167

commit v3 on v2

v3 whole, which is shorter than its diff:
```python
import functools

import jax
import jax.numpy as jnp
import numpy as np
from jax import lax
from jax.experimental import pallas as pl
from jax.experimental.pallas import tpu as pltpu
from jax.sharding import PartitionSpec as P

KEY_ROWS = 16
SLOTS = 48
TOGETHER = 8
BITS = 8


def bit_table():
    table = np.zeros(1 << BITS, np.int32)
    for mask in range(1 << BITS):
        there = [k for k in range(BITS) if mask >> k & 1]
        table[mask] = sum(k << 3 * i for i, k in enumerate(there)) + (len(there) << 3 * BITS)
    return table


def product_kernel(plan, places, slots, info, pos, table, *refs):
    n_row, n_depth, n_rows, n_groups, share = plan
    given, out, refs = refs[: len(places)], refs[len(places)], refs[len(places) + 1 :]
    panels, sums, tails, keys, bits, known, later, sems, tail_sems, known_sem = refs
    block = out.shape[-1]
    count, row, depth, kind = info[0], info[1], info[2], info[3]
    left = (kind == 0).astype(jnp.int32)
    step = pl.program_id(0)
    n_blocks = n_rows * n_groups
    none = n_depth * n_row * n_blocks
    possible = n_depth * n_groups
    parts = -(-possible // BITS)
    n_keys = tails.shape[3]
    room = share + TOGETHER
    lanes = bits.shape[1]
    rows_of_bits = bits.shape[0] // parts

    def block_of(side, at):
        return panels[side, pl.ds(pl.multiple_of(at * block, block), block), :]

    def known_of(part, slot):
        if isinstance(slot, int):
            return known[part * rows_of_bits + slot // lanes, slot % lanes]
        return known[part * rows_of_bits + lax.div(slot, lanes), lax.rem(slot, lanes)]

    def product(which, slot, j):
        lefts, rights = [], []
        for part in which:
            code = table[known_of(part, slot)]
            n = lax.shift_right_logical(code, 3 * BITS)
            for i in range(2):
                at = 2 * j + i
                which_one = part * BITS + (lax.shift_right_logical(code, 3 * at) & 7)
                start = table[(1 << BITS) + which_one]
                lefts.append(block_of(left, start + pos[2 * slot] * n_groups))
                rights.append(block_of(1, jnp.where(n > at, start + pos[2 * slot + 1] * n_groups, none)))
        return lax.dot_general(
            jnp.concatenate(lefts, 1),
            jnp.concatenate(rights, 1),
            (((1,), (1,)), ((), ())),
            preferred_element_type=jnp.float32,
        )

    @pl.when(step == 0)
    def _():
        def start(side, src, place, tail):
            r = row ^ place[0]
            if tail:
                src = src.at[pl.ds(n_blocks * block, n_keys)]
                pltpu.make_async_copy(src, tails.at[side, place[1], r], tail_sems.at[side]).start()
            else:
                src = src.at[pl.ds(0, n_blocks * block)]
                to = pl.ds((place[1] * n_row + r) * n_blocks * block, n_blocks * block)
                pltpu.make_async_copy(src, panels.at[side, to], sems.at[side]).start()

        def start_all(side, tail):
            for which in (1, 2) if side == 0 else (0,):

                @pl.when((kind == which) | (side == 1))
                def _():
                    for src, (place, use) in zip(given, places):
                        if use == which:
                            start(side, src, place, tail)

        start_all(1, True)
        start_all(0, True)
        start_all(1, False)
        panels[1, pl.ds(none * block, block), :] = jnp.zeros((block, block), panels.dtype)
        def read_keys(side):
            pltpu.make_async_copy(tails.at[side], tails.at[side], tail_sems.at[side]).wait()
            for e in range(n_depth):
                for r in range(n_row):
                    rows = tails[side, e, r].astype(jnp.float32)
                    for i in range(n_rows):
                        for g in range(n_groups):
                            at = i * n_groups + g
                            keys[side, r * n_rows + i, pl.ds(e * n_groups + g, 1), :] = rows[at : at + 1]

        read_keys(1)

        @pl.when(kind != 0)
        def _():
            read_keys(0)

        weight = jnp.left_shift(1, lax.broadcasted_iota(jnp.int32, (BITS, lanes), 0)).astype(jnp.float32)
        lane = lax.broadcasted_iota(jnp.int32, (1, lanes), 1)
        for part in range(parts):
            for at in range(rows_of_bits):
                found = jnp.zeros((1, lanes), jnp.float32)
                for slot in range(at * lanes, min(at * lanes + lanes, share)):
                    u, v = pos[2 * slot], pos[2 * slot + 1]
                    here = pl.ds(part * BITS, min(BITS, possible - part * BITS))
                    same = keys[left, u, here, :] == keys[1, v, here, :]
                    mine = jnp.sum(jnp.where(same, weight[: same.shape[0]], 0.0), 0, keepdims=True)
                    found = jnp.where(lane == slot - at * lanes, mine, found)
                bits[pl.ds(part * rows_of_bits + at, 1), :] = found.astype(jnp.int32)
        copy = pltpu.make_async_copy(bits, known, known_sem)
        copy.start()
        start_all(0, False)

        def clear(i, _):
            sums[i] = jnp.zeros((block, block), jnp.float32)
            return 0

        lax.fori_loop(0, share + 1, clear, 0)
        copy.wait()

        rounds = [(part, j) for part in range(parts) for j in range(1, BITS // 2)]

        totals = []
        for part in range(parts):
            total = jnp.int32(0)
            at = len(totals)
            for slot in range(share):
                later[at * room + total] = jnp.int32(slot)
                n = lax.shift_right_logical(table[known_of(part, slot)], 3 * BITS)
                total = total + (n > 2).astype(jnp.int32)
            totals.append(total)
            for j in range(2, BITS // 2):

                def more(k, total, at=at + j - 1, part=part, j=j):
                    slot = later[(at - 1) * room + k]
                    later[at * room + total] = slot
                    n = lax.shift_right_logical(table[known_of(part, slot)], 3 * BITS)
                    return total + (n > 2 * j).astype(jnp.int32)

                totals.append(lax.fori_loop(0, totals[-1], more, jnp.int32(0)))
        for i in range(len(rounds)):
            for k in range(TOGETHER):
                later[i * room + totals[i] + k] = jnp.int32(share)

        def wait_panel(side):
            whole = panels.at[side, pl.ds(0, none * block)]
            pltpu.make_async_copy(whole, whole, sems.at[side]).wait()

        wait_panel(1)

        @pl.when(kind != 0)
        def _():
            wait_panel(0)

        for i, (part, j) in enumerate(rounds):

            def some(k, _, i=i, part=part, j=j):
                which = [later[i * room + k * TOGETHER + m] for m in range(TOGETHER)]
                made = [product([part], slot, j) for slot in which]
                added = [sums[slot] + value for slot, value in zip(which, made)]
                for slot, value in zip(which, added):
                    sums[slot] = value
                return 0

            lax.fori_loop(0, lax.div(totals[i] + TOGETHER - 1, TOGETHER), some, 0)

    for k in range(slots):
        slot = step * slots + k
        value = product(range(parts), slot, 0) + sums[slot]
        out[k] = jnp.where(depth * share + slot < count, value, 0.0).astype(out.dtype)


def products(plan, info, pos, pieces):
    n_row, n_depth, n_rows, n_groups, share = plan
    slots = max(k for k in range(1, SLOTS + 1) if share % k == 0)
    rows, block = pieces[0][0].shape
    n_blocks = n_rows * n_groups
    total = n_depth * n_row * n_blocks
    possible = n_depth * n_groups
    parts = -(-possible // BITS)
    n_keys = rows - n_blocks * block
    places = [(place, use) for _, place, use in pieces]
    near = len(pieces) * rows * block * 2 <= 16 * 1024 * 1024
    args = [
        pltpu.with_memory_space_constraint(value, pltpu.VMEM if near and use == 2 else pltpu.HBM)
        for value, _, use in pieces
    ]
    starts = [k // n_groups * n_row * n_blocks + k % n_groups for k in range(possible)] + [0] * (parts * BITS - possible)
    table = jnp.asarray(np.concatenate([bit_table(), np.array(starts, np.int32)]))
    held = 2 * (total + 1) * block * block * 2 + 2 * slots * block * block * 2 + (share + 1) * block * block * 4
    return pl.pallas_call(
        functools.partial(product_kernel, plan, places, slots),
        grid=(share // slots,),
        in_specs=[pl.BlockSpec(memory_space=pltpu.SMEM)] * 3 + [pl.BlockSpec(memory_space=pl.ANY)] * len(args),
        out_specs=pl.BlockSpec((slots, block, block), lambda i: (i, 0, 0)),
        out_shape=jax.ShapeDtypeStruct((share, block, block), jnp.bfloat16),
        scratch_shapes=[
            pltpu.VMEM((2, (total + 1) * block, block), jnp.bfloat16),
            pltpu.VMEM((share + 1, block, block), jnp.float32),
            pltpu.VMEM((2, n_depth, n_row, n_keys, block), jnp.bfloat16),
            pltpu.VMEM((2, n_row * n_rows, parts * BITS, block), jnp.float32),
            pltpu.VMEM((parts * (share // block + 1), block), jnp.int32),
            pltpu.SMEM((parts * (share // block + 1), block), jnp.int32),
            pltpu.SMEM((parts * (BITS // 2 - 1) * (share + TOGETHER),), jnp.int32),
            pltpu.SemaphoreType.DMA((2,)),
            pltpu.SemaphoreType.DMA((2,)),
            pltpu.SemaphoreType.DMA,
        ],
        compiler_params=pltpu.CompilerParams(vmem_limit_bytes=held + 4 * 1024 * 1024),
        cost_estimate=pl.CostEstimate(
            flops=2 * share * possible * block**3,
            bytes_accessed=2 * total * block * block * 2 + share * block * block * 2,
            transcendentals=0,
        ),
    )(info, pos, table, *args)


def after(value, *others):
    return lax.optimization_barrier((value, *others))[0]


def payload(x_blocks, col_slot):
    block = x_blocks.shape[-1]
    keys = col_slot.reshape(-1).astype(x_blocks.dtype)
    keys = jnp.pad(keys, (0, -keys.shape[0] % KEY_ROWS))
    return jnp.concatenate([x_blocks.reshape(-1, block), jnp.broadcast_to(keys[:, None], (keys.shape[0], block))])


def body(sizes, x_blocks, col_slot, out_pos, out_count):
    n_row, n_col, n_depth = sizes
    n_rows, n_groups, block, _ = x_blocks.shape
    share = out_pos.shape[2] // n_depth
    row, col, depth = lax.axis_index("row"), lax.axis_index("col"), lax.axis_index("depth")
    hops = lax.rem(col - row + n_col, n_col)
    kind = jnp.where(hops == 0, 0, 2 - hops % 2)
    info = jnp.stack([out_count[0, 0], row, depth, kind]).astype(jnp.int32)
    listed = lax.dynamic_slice_in_dim(out_pos[0, 0], depth * share, share)
    pos = jnp.pad(listed.reshape(-1), (0, 2))
    evens, others = range(2, n_row, 2), range(1, n_depth)

    def hops_to(i, k, odd):
        ahead = (k - i // 2 * 2 + n_col) % n_col
        return lax.rem(ahead - (ahead + odd) % 2 + n_col, n_col)

    def next_col(value, step):
        return lax.ppermute(value, "col", [(i, (i + step) % n_col) for i in range(n_col)])

    def move(value, t, e, some=False):
        pairs = [
            (((i ^ t) * n_col + k) * n_depth + (j + e * (not some or needs_even(i, k))) % n_depth, (i * n_col + k) * n_depth + j)
            for i in range(n_row)
            for k in range(n_col)
            for j in range(n_depth)
        ]
        return lax.ppermute(value, ("row", "col", "depth"), pairs)

    def needs_even(i, k):
        return (k - i // 2 * 2) % n_col > 1

    def choose(ring, t, odd):
        away = hops_to(row ^ t, col, odd)
        among = [k for k in range(1, n_col) if k % 2 == odd]
        value = ring[among[0]]
        for k in among[1:]:
            value = jnp.where(away == k, ring[k], value)
        return value

    def between_cores(pieces):
        for (t, e), value in list(pieces.items()):
            pieces[t + 1, e] = move(value, 1, 0)

    own = payload(x_blocks, col_slot)
    ring = {1: next_col(own, 1), n_col - 1: next_col(own, -1)}
    right = {(0, 0): own}
    for e in others:
        right[0, e] = move(own, 0, e)
    for t in evens:
        right[t, 0] = move(own, t, 0)
    for t in evens:
        for e in others:
            right[t, e] = move(right[0, e], t, 0)
    waited = [*ring.values(), *[right[at] for at in right if at != (0, 0)]]

    for k in range(2, n_col // 2 + 1):
        ring[k] = next_col(after(ring[k - 1], *ring.values()), 1)
    for k in range(n_col - 2, n_col // 2, -1):
        ring[k] = next_col(ring[k + 1], -1)
    first = {(0, 0): choose({**ring, 1: after(ring[1], *waited)}, 0, 1)}
    for e in others:
        first[0, e] = move(first[0, 0], 0, e)
    for t in evens:
        first[t, 0] = move(choose({**ring, 1: after(ring[1], *waited)}, t, 1), t, 0)
    waited = [*[first[at] for at in first if at != (0, 0)], *ring.values()]

    for t in evens:
        for e in others:
            first[t, e] = move(after(first[t, 0], *waited), 0, e)
    second = {}
    for t in range(0, n_row, 2):
        value = choose({**ring, 2: after(ring[2], *waited)}, t, 0)
        for e in range(n_depth):
            second[t, e] = move(value, t, e, True) if t or e else value
    for pieces in (right, first, second):
        between_cores(pieces)
    pieces = [(value, at, use) for use, part in enumerate((right, first, second)) for at, value in part.items()]
    plan = (n_row, n_depth, n_rows, n_groups, share)
    return products(plan, info, pos, pieces)[None, None]


def solution(mesh):
    sizes = tuple(mesh.shape[axis] for axis in ("row", "col", "depth"))
    in_specs = (
        P(("row", "col"), "depth", None, None),
        P(("row", "col"), "depth"),
        P("row", "col", None, None),
        P("row", "col"),
    )
    out_specs = P("row", "col", "depth", None, None)
    return jax.shard_map(
        functools.partial(body, sizes), mesh=mesh, in_specs=in_specs, out_specs=out_specs, check_vma=False
    )
```

time: 94.3 us -> 88.5 us (0.938)
  starting transfers between devices: 22.7 us -> 18.5 us
  Pallas kernels: 13 us -> 9.6 us
  waiting for transfers between devices: 53.3 us -> 55.1 us
  local copies, waits for them, and re-layouts: 1.56 us -> 0.46 us
  other arithmetic: 2.67 us -> 3.62 us
    ppermute x21, starting transfers between devices: 17.7 us -> 13.5 us  [move(): return lax.ppermute(value, ('row', 'col', 'depth'), pairs)]
    pallas_call x1, Pallas kernels: 13 us -> 9.6 us  [products(): pl.pallas_call(functools.partial(product_kernel, plan, places, slots), gr...]
    ppermute x21, waiting for transfers between devices: 31.9 us -> 33.4 us  [move(): return lax.ppermute(value, ('row', 'col', 'depth'), pairs)]
    transpose x1 -> x0, local copies, waits for them, and re-layouts: 1.08 us -> none  [payload(): rows = jnp.swapaxes(x_blocks, 0, 1).reshape(n * block, block)]
    concatenate x2 -> x1, other arithmetic: 0.35 us -> 1.38 us  [payload(): jnp.concatenate([x_blocks.reshape(-1, block), jnp.broadcast_to(keys[:, No...]
where the time goes in v3:
time: 88.5 us; the launch traced here: 88.1 us
  waiting for transfers between devices  55.1 us (62%)
  starting transfers between devices  18.5 us (21%)
  Pallas kernels  9.6 us (11%)
  other arithmetic  3.62 us (4%)
    ppermute x21, waiting for transfers between devices, move(): return lax.ppermute(value, ('row', 'col', 'depth'), pairs)  33.4 us
    ppermute x3, waiting for transfers between devices, next_col(): lax.ppermute(value, 'col', [(i, (i + step) % n_col) for i in range(n_col)])  21.7 us
    ppermute x21, starting transfers between devices, move(): return lax.ppermute(value, ('row', 'col', 'depth'), pairs)  13.5 us
    pallas_call x1, Pallas kernels, products(): pl.pallas_call(functools.partial(product_kernel, plan, places, slots), gr...  9.6 us
    ppermute x3, starting transfers between devices, next_col(): lax.ppermute(value, 'col', [(i, (i + step) % n_col) for i in range(n_col)])  4.95 us
  transfers between devices with their start and end apart: 24, of which 12 were waited for; matrix products, arithmetic and copies ran while one was open for 2% of the time, Pallas kernels for 0%

profile of v3, /device:TPU:0, one launch (start us, length us, event | category | flops | bytes accessed | tf_op | source)
XLA Modules:
  0.0 88.1 jit_solution(8372731586585492303)
XLA Ops:
  0.0 0.0 copy-start
  0.0 0.7 convert_element_type.10
  0.7 0.1 reshape.17
  0.8 1.4 %pad_maximum_fusion.refs_0_ = bf16[2064,128]{1,0:T(8,128)(2,1)S(1)} fusion(bf16[2048,128]{1,0:T(8,128)(2,1)} %bitcast.9, bf16[2064]{0:T(1024)(128)(2,1)S(1)} %pad.6.clone), kind=kLoop, calls=%fused_computation | loop fusion | flops 1056768 | bytes 1056800 | tf_op jit(solution)/shard_map/concatenate | solution.py:237
  2.2 0.0 copy-start.2
  2.2 3.0 %collective-permute-start = (bf16[2064,128]{1,0:T(8,128)(2,1)S(1)}, bf16[2064,128]{1,0:T(8,128)(2,1)S(1)}, u32[]{:S(2)}, u32[]{:S(2)}) collective-permute-start(bf16[2064,128]{1,0:T(8,128)(2,1)S(1)} %pad_maximum_fusion.refs_0_), channel_id=1, source_target_pairs={{1,0},{0,1},{3,2},{2,3},{5,4},{4,5},{7,6},{6,7},{9,8},{8,9},{11,10... | collective-permute-start | bytes 1585160 | tf_op jit(solution)/shard_map/ppermute | solution.py:266
  5.2 1.6 %collective-permute-start.8 = (bf16[2064,128]{1,0:T(8,128)(2,1)S(1)}, bf16[2064,128]{1,0:T(8,128)(2,1)}, u32[]{:S(2)}, u32[]{:S(2)}) collective-permute-start(bf16[2064,128]{1,0:T(8,128)(2,1)S(1)} %pad_maximum_fusion.refs_0_), channel_id=1, source_target_pairs={{0,2},{2,4},{4,6},{6,0},{1,3},{3,5},{5,7},{7,1},{8,10},{10,12},{12... | collective-permute-start | bytes 1585160 | tf_op jit(solution)/shard_map/ppermute | solution.py:257
  6.8 2.2 %collective-permute-start.7 = (bf16[2064,128]{1,0:T(8,128)(2,1)S(1)}, bf16[2064,128]{1,0:T(8,128)(2,1)}, u32[]{:S(2)}, u32[]{:S(2)}) collective-permute-start(bf16[2064,128]{1,0:T(8,128)(2,1)S(1)} %pad_maximum_fusion.refs_0_), channel_id=1, source_target_pairs={{0,6},{2,0},{4,2},{6,4},{1,7},{3,1},{5,3},{7,5},{8,14},{10,8},{12,... | collective-permute-start | bytes 1585160 | tf_op jit(solution)/shard_map/ppermute | solution.py:257
  9.0 1.5 %collective-permute-start.1 = (bf16[2064,128]{1,0:T(8,128)(2,1)S(1)}, bf16[2064,128]{1,0:T(8,128)(2,1)S(1)}, u32[]{:S(2)}, u32[]{:S(2)}) collective-permute-start(bf16[2064,128]{1,0:T(8,128)(2,1)S(1)} %pad_maximum_fusion.refs_0_), channel_id=1, source_target_pairs={{16,0},{17,1},{18,2},{19,3},{20,4},{21,5},{22,6},{23,7},{24,8},{25... | collective-permute-start | bytes 1585160 | tf_op jit(solution)/shard_map/ppermute | solution.py:266
  10.5 6.7 %collective-permute-done.refs_1_ = bf16[2064,128]{1,0:T(8,128)(2,1)S(1)} collective-permute-done((bf16[2064,128]{1,0:T(8,128)(2,1)S(1)}, bf16[2064,128]{1,0:T(8,128)(2,1)S(1)}, u32[]{:S(2)}, u32[]{:S(2)}) %collective-permute-start) | collective-permute-done | bytes 528416 | tf_op jit(solution)/shard_map/ppermute | solution.py:266
  17.2 1.8 %collective-permute-start.2 = (bf16[2064,128]{1,0:T(8,128)(2,1)S(1)}, bf16[2064,128]{1,0:T(8,128)(2,1)S(1)}, u32[]{:S(2)}, u32[]{:S(2)}) collective-permute-start(bf16[2064,128]{1,0:T(8,128)(2,1)S(1)} %collective-permute-done.refs_1_), channel_id=1, source_target_pairs={{16,0},{17,1},{18,2},{19,3},{20,4},{21,5},{22,6},{23,7},{24,8},{25... | collective-permute-start | bytes 1585160 | tf_op jit(solution)/shard_map/ppermute | solution.py:266
  19.0 0.0 collective-permute-start.3
  19.0 3.1 %collective-permute-done.8 = bf16[2064,128]{1,0:T(8,128)(2,1)} collective-permute-done((bf16[2064,128]{1,0:T(8,128)(2,1)S(1)}, bf16[2064,128]{1,0:T(8,128)(2,1)}, u32[]{:S(2)}, u32[]{:S(2)}) %collective-permute-start.8) | collective-permute-done | bytes 528416 | tf_op jit(solution)/shard_map/ppermute | solution.py:257
  22.1 9.3 %collective-permute-done.7 = bf16[2064,128]{1,0:T(8,128)(2,1)} collective-permute-done((bf16[2064,128]{1,0:T(8,128)(2,1)S(1)}, bf16[2064,128]{1,0:T(8,128)(2,1)}, u32[]{:S(2)}, u32[]{:S(2)}) %collective-permute-start.7) | collective-permute-done | bytes 528416 | tf_op jit(solution)/shard_map/ppermute | solution.py:257
  31.4 1.1 %collective-permute-start.11 = (bf16[2064,128]{1,0:T(8,128)(2,1)}, bf16[2064,128]{1,0:T(8,128)(2,1)S(1)}, u32[]{:S(2)}, u32[]{:S(2)}) collective-permute-start(bf16[2064,128]{1,0:T(8,128)(2,1)} %collective-permute-done.8), channel_id=1, source_target_pairs={{0,2},{2,4},{4,6},{6,0},{1,3},{3,5},{5,7},{7,1},{8,10},{10,12},{12... | collective-permute-start | bytes 1585160 | tf_op jit(solution)/shard_map/ppermute | solution.py:257
  32.5 0.0 collective-permute-done.1.refs_2_
  32.5 0.8 collective-permute-done.2.refs_3_
  33.3 1.5 %broadcast_select_fusion = (bf16[2064,128]{1,0:T(8,128)(2,1)S(1)}, bf16[2064,128]{1,0:T(8,128)(2,1)S(1)}) fusion(bf16[2064,128]{1,0:T(8,128)(2,1)} %collective-permute-done.7, bf16[2064,128]{1,0:T(8,128)(2,1)} %collective-permute-done.8, pred[]{:T(512)S(6)} %eq.17, pred[]{:T(512)S(6)} %eq.16), kind=kLoop, calls=%fused_computation.1 | loop fusion | flops 528384 | bytes 2113538 | tf_op jit(solution)/shard_map/jit(_where)/select_n | solution.py:276
  34.8 0.0 copy-done.2
  34.8 0.0 copy-start.3
  34.8 1.6 %collective-permute-start.10 = (bf16[2064,128]{1,0:T(8,128)(2,1)S(1)}, bf16[2064,128]{1,0:T(8,128)(2,1)S(1)}, u32[]{:S(2)}, u32[]{:S(2)}) collective-permute-start(bf16[2064,128]{1,0:T(8,128)(2,1)S(1)} %get-tuple-element.13), channel_id=1, source_target_pairs={{16,0},{17,1},{18,2},{19,3},{20,4},{21,5},{22,6},{23,7},{24,8},{25... | collective-permute-start | bytes 1585160 | tf_op jit(solution)/shard_map/ppermute | solution.py:266
  36.4 0.5 collective-permute-start.9
  36.9 0.0 copy-done.5
  36.9 0.0 collective-permute-start.5
  36.9 0.0 collective-permute-done.3.refs_4_
  36.9 0.0 copy-done.4
  37.0 0.5 collective-permute-start.4
  37.5 9.2 %collective-permute-done.11.refs_16_ = bf16[2064,128]{1,0:T(8,128)(2,1)S(1)} collective-permute-done((bf16[2064,128]{1,0:T(8,128)(2,1)}, bf16[2064,128]{1,0:T(8,128)(2,1)S(1)}, u32[]{:S(2)}, u32[]{:S(2)}) %collective-permute-start.11) | collective-permute-done | bytes 528416 | tf_op jit(solution)/shard_map/ppermute | solution.py:257
  46.7 0.0 copy-done.6
  46.7 0.0 collective-permute-start.6
  46.7 1.2 %collective-permute-done.10.refs_10_ = bf16[2064,128]{1,0:T(8,128)(2,1)S(1)} collective-permute-done((bf16[2064,128]{1,0:T(8,128)(2,1)S(1)}, bf16[2064,128]{1,0:T(8,128)(2,1)S(1)}, u32[]{:S(2)}, u32[]{:S(2)}) %collective-permute-start.10) | collective-permute-done | bytes 528416 | tf_op jit(solution)/shard_map/ppermute | solution.py:266
  47.9 0.0 collective-permute-start.13
  47.9 1.3 %collective-permute-done.9.refs_9_ = bf16[2064,128]{1,0:T(8,128)(2,1)} collective-permute-done((bf16[2064,128]{1,0:T(8,128)(2,1)S(1)}, bf16[2064,128]{1,0:T(8,128)(2,1)}, u32[]{:S(2)}, u32[]{:S(2)}) %collective-permute-start.9) | collective-permute-done | bytes 528416 | tf_op jit(solution)/shard_map/ppermute | solution.py:266
  49.3 0.0 collective-permute-start.15
  49.3 0.0 collective-permute-done.5.refs_6_
  49.3 0.6 collective-permute-start.12
  49.9 0.0 collective-permute-done.4.refs_5_
  49.9 0.2 collective-permute-start.20
  50.1 0.0 collective-permute-done.6.refs_7_
  50.1 1.5 %collective-permute-start.19 = (bf16[2064,128]{1,0:T(8,128)(2,1)S(1)}, bf16[2064,128]{1,0:T(8,128)(2,1)S(1)}, u32[]{:S(2)}, u32[]{:S(2)}) collective-permute-start(bf16[2064,128]{1,0:T(8,128)(2,1)S(1)} %collective-permute-done.11.refs_16_), channel_id=1, source_target_pairs={{16,0},{17,1},{18,2},{19,3},{21,4},{20,5},{23,6},{22,7},{24,8},{25... | collective-permute-start | bytes 1585160 | tf_op jit(solution)/shard_map/ppermute | solution.py:266
  51.5 0.0 collective-permute-done.13.refs_12_
  51.5 0.6 collective-permute-start.18
  52.2 0.0 collective-permute-done.15.refs_14_
  52.2 0.7 collective-permute-start.17
  52.9 11.4 %collective-permute-done.12.refs_11_ = bf16[2064,128]{1,0:T(8,128)(2,1)} collective-permute-done((bf16[2064,128]{1,0:T(8,128)(2,1)S(1)}, bf16[2064,128]{1,0:T(8,128)(2,1)}, u32[]{:S(2)}, u32[]{:S(2)}) %collective-permute-start.12) | collective-permute-done | bytes 528416 | tf_op jit(solution)/shard_map/ppermute | solution.py:266
  64.3 0.0 collective-permute-start.14
  64.3 0.0 collective-permute-done.20.refs_20_
  64.3 0.5 collective-permute-start.16
  64.8 8.3 %collective-permute-done.19.refs_19_ = bf16[2064,128]{1,0:T(8,128)(2,1)S(1)} collective-permute-done((bf16[2064,128]{1,0:T(8,128)(2,1)S(1)}, bf16[2064,128]{1,0:T(8,128)(2,1)S(1)}, u32[]{:S(2)}, u32[]{:S(2)}) %collective-permute-start.19) | collective-permute-done | bytes 528416 | tf_op jit(solution)/shard_map/ppermute | solution.py:266
  73.1 0.0 collective-permute-start.23
  73.1 2.5 %collective-permute-done.18.refs_18_ = bf16[2064,128]{1,0:T(8,128)(2,1)S(1)} collective-permute-done((bf16[2064,128]{1,0:T(8,128)(2,1)S(1)}, bf16[2064,128]{1,0:T(8,128)(2,1)S(1)}, u32[]{:S(2)}, u32[]{:S(2)}) %collective-permute-start.18) | collective-permute-done | bytes 528416 | tf_op jit(solution)/shard_map/ppermute | solution.py:266
  75.7 0.0 collective-permute-start.22
  75.7 0.0 collective-permute-done.17.refs_17_
  75.7 0.6 collective-permute-start.21
  76.9 0.1 constant_dynamic-slice_fusion
  77.0 0.1 copy.6
  77.1 0.1 reshape.15
  77.3 0.1 pad_add_fusion.info
  77.4 0.0 collective-permute-done.14.refs_13_
  77.4 0.0 collective-permute-done.16.refs_15_
  77.4 0.0 collective-permute-done.23.refs_23_
  77.4 0.3 collective-permute-done.22.refs_22_
  77.7 0.8 collective-permute-done.21.refs_21_
  78.5 9.6 %shard_map.55 = bf16[96,128,128]{2,1,0:T(8,128)(2,1)} custom-call(s32[4]{0:T(128)S(1)} %pad_add_fusion.info, s32[194]{0:T(256)S(1)} %pad.4.pos, s32[264]{0:T(512)S(1)} %copy-done.1, bf16[2064,128]{1,0:T(8,128)(2,1)} %copy-done.2, bf16[2064,128]{1,0:T(8,128)(2,1)} %copy-done.4, bf16[2064,128]{1,0:T(8,128)(2,1)} %copy-done.5, bf16[2064,128]{1,0:T(8,128)(2,1)} %copy-done.6, ...), custom_call_target="tpu_custom_call" | custom-call | flops 3221225472 | bytes 11534336 | tf_op jit(solution)/shard_map/pallas_call | solution.py:202
  (19 shorter events, 0.0 us)
Async XLA Ops:
  0.0 76.9 %copy-start = (s32[1,1,192,2]{2,3,1,0:T(2,128)S(1)}, s32[1,1,192,2]{2,3,1,0:T(2,128)}, u32[]{:S(2)}) copy-start(s32[1,1,192,2]{2,3,1,0:T(2,128)} %param.7) | copy-start | bytes 4612
  2.2 32.6 %copy-start.2 = (bf16[2064,128]{1,0:T(8,128)(2,1)}, bf16[2064,128]{1,0:T(8,128)(2,1)S(1)}, u32[]{:S(2)}) copy-start(bf16[2064,128]{1,0:T(8,128)(2,1)S(1)} %pad_maximum_fusion.refs_0_) | copy-start | bytes 1585156
  2.2 15.0 %collective-permute-start = (bf16[2064,128]{1,0:T(8,128)(2,1)S(1)}, bf16[2064,128]{1,0:T(8,128)(2,1)S(1)}, u32[]{:S(2)}, u32[]{:S(2)}) collective-permute-start(bf16[2064,128]{1,0:T(8,128)(2,1)S(1)} %pad_maximum_fusion.refs_0_), channel_id=1, source_target_pairs={{1,0},{0,1},{3,2},{2,3},{5,4},{4,5},{7,6},{6,7},{9,8},{8,9},{11,10... | collective-permute-start | bytes 1585160 | tf_op jit(solution)/shard_map/ppermute | solution.py:266
  5.2 16.9 %collective-permute-start.8 = (bf16[2064,128]{1,0:T(8,128)(2,1)S(1)}, bf16[2064,128]{1,0:T(8,128)(2,1)}, u32[]{:S(2)}, u32[]{:S(2)}) collective-permute-start(bf16[2064,128]{1,0:T(8,128)(2,1)S(1)} %pad_maximum_fusion.refs_0_), channel_id=1, source_target_pairs={{0,2},{2,4},{4,6},{6,0},{1,3},{3,5},{5,7},{7,1},{8,10},{10,12},{12... | collective-permute-start | bytes 1585160 | tf_op jit(solution)/shard_map/ppermute | solution.py:257
  6.8 24.6 %collective-permute-start.7 = (bf16[2064,128]{1,0:T(8,128)(2,1)S(1)}, bf16[2064,128]{1,0:T(8,128)(2,1)}, u32[]{:S(2)}, u32[]{:S(2)}) collective-permute-start(bf16[2064,128]{1,0:T(8,128)(2,1)S(1)} %pad_maximum_fusion.refs_0_), channel_id=1, source_target_pairs={{0,6},{2,0},{4,2},{6,4},{1,7},{3,1},{5,3},{7,5},{8,14},{10,8},{12,... | collective-permute-start | bytes 1585160 | tf_op jit(solution)/shard_map/ppermute | solution.py:257
  9.0 23.5 %collective-permute-start.1 = (bf16[2064,128]{1,0:T(8,128)(2,1)S(1)}, bf16[2064,128]{1,0:T(8,128)(2,1)S(1)}, u32[]{:S(2)}, u32[]{:S(2)}) collective-permute-start(bf16[2064,128]{1,0:T(8,128)(2,1)S(1)} %pad_maximum_fusion.refs_0_), channel_id=1, source_target_pairs={{16,0},{17,1},{18,2},{19,3},{20,4},{21,5},{22,6},{23,7},{24,8},{25... | collective-permute-start | bytes 1585160 | tf_op jit(solution)/shard_map/ppermute | solution.py:266
  17.2 19.7 %copy-start.4 = (bf16[2064,128]{1,0:T(8,128)(2,1)}, bf16[2064,128]{1,0:T(8,128)(2,1)S(1)}, u32[]{:S(2)}) copy-start(bf16[2064,128]{1,0:T(8,128)(2,1)S(1)} %collective-permute-done.refs_1_) | copy-start | bytes 1585156
  17.2 16.1 %collective-permute-start.2 = (bf16[2064,128]{1,0:T(8,128)(2,1)S(1)}, bf16[2064,128]{1,0:T(8,128)(2,1)S(1)}, u32[]{:S(2)}, u32[]{:S(2)}) collective-permute-start(bf16[2064,128]{1,0:T(8,128)(2,1)S(1)} %collective-permute-done.refs_1_), channel_id=1, source_target_pairs={{16,0},{17,1},{18,2},{19,3},{20,4},{21,5},{22,6},{23,7},{24,8},{25... | collective-permute-start | bytes 1585160 | tf_op jit(solution)/shard_map/ppermute | solution.py:266
  19.0 18.0 %collective-permute-start.3 = (bf16[2064,128]{1,0:T(8,128)(2,1)S(1)}, bf16[2064,128]{1,0:T(8,128)(2,1)}, u32[]{:S(2)}, u32[]{:S(2)}) collective-permute-start(bf16[2064,128]{1,0:T(8,128)(2,1)S(1)} %pad_maximum_fusion.refs_0_), channel_id=1, source_target_pairs={{8,0},{9,1},{10,2},{11,3},{12,4},{13,5},{14,6},{15,7},{0,8},{1,9},... | collective-permute-start | bytes 1585160 | tf_op jit(solution)/shard_map/ppermute | solution.py:266
  19.0 59.5 %copy-start.1 = (s32[264]{0:T(512)S(1)}, s32[264]{0:T(512)}, u32[]{:S(2)}) copy-start(s32[264]{0:T(512)} %constant.80.clone.table) | copy-start | bytes 3172
  31.4 15.3 %collective-permute-start.11 = (bf16[2064,128]{1,0:T(8,128)(2,1)}, bf16[2064,128]{1,0:T(8,128)(2,1)S(1)}, u32[]{:S(2)}, u32[]{:S(2)}) collective-permute-start(bf16[2064,128]{1,0:T(8,128)(2,1)} %collective-permute-done.8), channel_id=1, source_target_pairs={{0,2},{2,4},{4,6},{6,0},{1,3},{3,5},{5,7},{7,1},{8,10},{10,12},{12... | collective-permute-start | bytes 1585160 | tf_op jit(solution)/shard_map/ppermute | solution.py:257
  32.5 4.4 %copy-start.5 = (bf16[2064,128]{1,0:T(8,128)(2,1)}, bf16[2064,128]{1,0:T(8,128)(2,1)S(1)}, u32[]{:S(2)}) copy-start(bf16[2064,128]{1,0:T(8,128)(2,1)S(1)} %collective-permute-done.1.refs_2_) | copy-start | bytes 1585156
  33.3 13.4 %copy-start.6 = (bf16[2064,128]{1,0:T(8,128)(2,1)}, bf16[2064,128]{1,0:T(8,128)(2,1)S(1)}, u32[]{:S(2)}) copy-start(bf16[2064,128]{1,0:T(8,128)(2,1)S(1)} %collective-permute-done.2.refs_3_) | copy-start | bytes 1585156
  34.8 16.7 %copy-start.3 = (bf16[2064,128]{1,0:T(8,128)(2,1)}, bf16[2064,128]{1,0:T(8,128)(2,1)S(1)}, u32[]{:S(2)}) copy-start(bf16[2064,128]{1,0:T(8,128)(2,1)S(1)} %get-tuple-element.14.refs_8_) | copy-start | bytes 1585156
  34.8 13.1 %collective-permute-start.10 = (bf16[2064,128]{1,0:T(8,128)(2,1)S(1)}, bf16[2064,128]{1,0:T(8,128)(2,1)S(1)}, u32[]{:S(2)}, u32[]{:S(2)}) collective-permute-start(bf16[2064,128]{1,0:T(8,128)(2,1)S(1)} %get-tuple-element.13), channel_id=1, source_target_pairs={{16,0},{17,1},{18,2},{19,3},{20,4},{21,5},{22,6},{23,7},{24,8},{25... | collective-permute-start | bytes 1585160 | tf_op jit(solution)/shard_map/ppermute | solution.py:266
  36.4 12.9 %collective-permute-start.9 = (bf16[2064,128]{1,0:T(8,128)(2,1)S(1)}, bf16[2064,128]{1,0:T(8,128)(2,1)}, u32[]{:S(2)}, u32[]{:S(2)}) collective-permute-start(bf16[2064,128]{1,0:T(8,128)(2,1)S(1)} %get-tuple-element.14.refs_8_), channel_id=1, source_target_pairs={{1,0},{0,1},{3,2},{2,3},{5,4},{4,5},{7,6},{6,7},{9,8},{8,9},{11,10... | collective-permute-start | bytes 1585160 | tf_op jit(solution)/shard_map/ppermute | solution.py:266
  36.9 12.4 %collective-permute-start.5 = (bf16[2064,128]{1,0:T(8,128)(2,1)S(1)}, bf16[2064,128]{1,0:T(8,128)(2,1)S(1)}, u32[]{:S(2)}, u32[]{:S(2)}) collective-permute-start(bf16[2064,128]{1,0:T(8,128)(2,1)S(1)} %collective-permute-done.1.refs_2_), channel_id=1, source_target_pairs={{8,0},{9,1},{10,2},{11,3},{12,4},{13,5},{14,6},{15,7},{0,8},{1,9},... | collective-permute-start | bytes 1585160 | tf_op jit(solution)/shard_map/ppermute | solution.py:266
  37.0 13.0 %collective-permute-start.4 = (bf16[2064,128]{1,0:T(8,128)(2,1)S(1)}, bf16[2064,128]{1,0:T(8,128)(2,1)}, u32[]{:S(2)}, u32[]{:S(2)}) collective-permute-start(bf16[2064,128]{1,0:T(8,128)(2,1)S(1)} %collective-permute-done.refs_1_), channel_id=1, source_target_pairs={{8,0},{9,1},{10,2},{11,3},{12,4},{13,5},{14,6},{15,7},{0,8},{1,9},... | collective-permute-start | bytes 1585160 | tf_op jit(solution)/shard_map/ppermute | solution.py:266
  46.7 3.4 %collective-permute-start.6 = (bf16[2064,128]{1,0:T(8,128)(2,1)S(1)}, bf16[2064,128]{1,0:T(8,128)(2,1)S(1)}, u32[]{:S(2)}, u32[]{:S(2)}) collective-permute-start(bf16[2064,128]{1,0:T(8,128)(2,1)S(1)} %collective-permute-done.2.refs_3_), channel_id=1, source_target_pairs={{8,0},{9,1},{10,2},{11,3},{12,4},{13,5},{14,6},{15,7},{0,8},{1,9},... | collective-permute-start | bytes 1585160 | tf_op jit(solution)/shard_map/ppermute | solution.py:266
  47.9 27.7 %copy-start.7 = (bf16[2064,128]{1,0:T(8,128)(2,1)}, bf16[2064,128]{1,0:T(8,128)(2,1)S(1)}, u32[]{:S(2)}) copy-start(bf16[2064,128]{1,0:T(8,128)(2,1)S(1)} %collective-permute-done.10.refs_10_) | copy-start | bytes 1585156
  47.9 3.6 %collective-permute-start.13 = (bf16[2064,128]{1,0:T(8,128)(2,1)S(1)}, bf16[2064,128]{1,0:T(8,128)(2,1)S(1)}, u32[]{:S(2)}, u32[]{:S(2)}) collective-permute-start(bf16[2064,128]{1,0:T(8,128)(2,1)S(1)} %get-tuple-element.14.refs_8_), channel_id=1, source_target_pairs={{8,0},{9,1},{10,2},{11,3},{12,4},{13,5},{14,6},{15,7},{0,8},{1,9},... | collective-permute-start | bytes 1585160 | tf_op jit(solution)/shard_map/ppermute | solution.py:266
  49.3 2.9 %collective-permute-start.15 = (bf16[2064,128]{1,0:T(8,128)(2,1)S(1)}, bf16[2064,128]{1,0:T(8,128)(2,1)S(1)}, u32[]{:S(2)}, u32[]{:S(2)}) collective-permute-start(bf16[2064,128]{1,0:T(8,128)(2,1)S(1)} %collective-permute-done.10.refs_10_), channel_id=1, source_target_pairs={{8,0},{9,1},{10,2},{11,3},{12,4},{13,5},{14,6},{15,7},{0,8},{1,9},... | collective-permute-start | bytes 1585160 | tf_op jit(solution)/shard_map/ppermute | solution.py:266
  49.3 26.4 %copy-start.8 = (bf16[2064,128]{1,0:T(8,128)(2,1)}, bf16[2064,128]{1,0:T(8,128)(2,1)S(1)}, u32[]{:S(2)}) copy-start(bf16[2064,128]{1,0:T(8,128)(2,1)S(1)} %collective-permute-done.5.refs_6_) | copy-start | bytes 1585156
  49.3 15.0 %collective-permute-start.12 = (bf16[2064,128]{1,0:T(8,128)(2,1)S(1)}, bf16[2064,128]{1,0:T(8,128)(2,1)}, u32[]{:S(2)}, u32[]{:S(2)}) collective-permute-start(bf16[2064,128]{1,0:T(8,128)(2,1)S(1)} %collective-permute-done.10.refs_10_), channel_id=1, source_target_pairs={{1,0},{0,1},{3,2},{2,3},{5,4},{4,5},{7,6},{6,7},{9,8},{8,9},{11,10... | collective-permute-start | bytes 1585160 | tf_op jit(solution)/shard_map/ppermute | solution.py:266
  49.9 14.4 %collective-permute-start.20 = (bf16[2064,128]{1,0:T(8,128)(2,1)S(1)}, bf16[2064,128]{1,0:T(8,128)(2,1)S(1)}, u32[]{:S(2)}, u32[]{:S(2)}) collective-permute-start(bf16[2064,128]{1,0:T(8,128)(2,1)S(1)} %collective-permute-done.11.refs_16_), channel_id=1, source_target_pairs={{8,0},{9,1},{10,2},{11,3},{12,4},{13,5},{14,6},{15,7},{0,8},{1,9},... | collective-permute-start | bytes 1585160 | tf_op jit(solution)/shard_map/ppermute | solution.py:266
  50.1 25.6 %copy-start.9 = (bf16[2064,128]{1,0:T(8,128)(2,1)}, bf16[2064,128]{1,0:T(8,128)(2,1)S(1)}, u32[]{:S(2)}) copy-start(bf16[2064,128]{1,0:T(8,128)(2,1)S(1)} %collective-permute-done.6.refs_7_) | copy-start | bytes 1585156
  50.1 23.1 %collective-permute-start.19 = (bf16[2064,128]{1,0:T(8,128)(2,1)S(1)}, bf16[2064,128]{1,0:T(8,128)(2,1)S(1)}, u32[]{:S(2)}, u32[]{:S(2)}) collective-permute-start(bf16[2064,128]{1,0:T(8,128)(2,1)S(1)} %collective-permute-done.11.refs_16_), channel_id=1, source_target_pairs={{16,0},{17,1},{18,2},{19,3},{21,4},{20,5},{23,6},{22,7},{24,8},{25... | collective-permute-start | bytes 1585160 | tf_op jit(solution)/shard_map/ppermute | solution.py:266
  51.5 24.2 %copy-start.10 = (bf16[2064,128]{1,0:T(8,128)(2,1)}, bf16[2064,128]{1,0:T(8,128)(2,1)S(1)}, u32[]{:S(2)}) copy-start(bf16[2064,128]{1,0:T(8,128)(2,1)S(1)} %collective-permute-done.13.refs_12_) | copy-start | bytes 1585156
  51.5 24.1 %collective-permute-start.18 = (bf16[2064,128]{1,0:T(8,128)(2,1)S(1)}, bf16[2064,128]{1,0:T(8,128)(2,1)S(1)}, u32[]{:S(2)}, u32[]{:S(2)}) collective-permute-start(bf16[2064,128]{1,0:T(8,128)(2,1)S(1)} %collective-permute-done.11.refs_16_), channel_id=1, source_target_pairs={{16,0},{17,1},{18,2},{19,3},{20,4},{21,5},{22,6},{23,7},{24,8},{25... | collective-permute-start | bytes 1585160 | tf_op jit(solution)/shard_map/ppermute | solution.py:266
  52.2 23.5 %copy-start.11 = (bf16[2064,128]{1,0:T(8,128)(2,1)}, bf16[2064,128]{1,0:T(8,128)(2,1)S(1)}, u32[]{:S(2)}) copy-start(bf16[2064,128]{1,0:T(8,128)(2,1)S(1)} %collective-permute-done.15.refs_14_) | copy-start | bytes 1585156
  52.2 23.5 %collective-permute-start.17 = (bf16[2064,128]{1,0:T(8,128)(2,1)S(1)}, bf16[2064,128]{1,0:T(8,128)(2,1)S(1)}, u32[]{:S(2)}, u32[]{:S(2)}) collective-permute-start(bf16[2064,128]{1,0:T(8,128)(2,1)S(1)} %collective-permute-done.11.refs_16_), channel_id=1, source_target_pairs={{0,0},{1,1},{2,2},{3,3},{5,4},{4,5},{7,6},{6,7},{8,8},{9,9},{10,10... | collective-permute-start | bytes 1585160 | tf_op jit(solution)/shard_map/ppermute | solution.py:266
  64.3 13.1 %collective-permute-start.14 = (bf16[2064,128]{1,0:T(8,128)(2,1)}, bf16[2064,128]{1,0:T(8,128)(2,1)}, u32[]{:S(2)}, u32[]{:S(2)}) collective-permute-start(bf16[2064,128]{1,0:T(8,128)(2,1)} %collective-permute-done.9.refs_9_), channel_id=1, source_target_pairs={{8,0},{9,1},{10,2},{11,3},{12,4},{13,5},{14,6},{15,7},{0,8},{1,9},... | collective-permute-start | bytes 1585160 | tf_op jit(solution)/shard_map/ppermute | solution.py:266
  64.3 13.1 %collective-permute-start.16 = (bf16[2064,128]{1,0:T(8,128)(2,1)}, bf16[2064,128]{1,0:T(8,128)(2,1)}, u32[]{:S(2)}, u32[]{:S(2)}) collective-permute-start(bf16[2064,128]{1,0:T(8,128)(2,1)} %collective-permute-done.12.refs_11_), channel_id=1, source_target_pairs={{8,0},{9,1},{10,2},{11,3},{12,4},{13,5},{14,6},{15,7},{0,8},{1,9},... | collective-permute-start | bytes 1585160 | tf_op jit(solution)/shard_map/ppermute | solution.py:266
  73.1 4.2 %collective-permute-start.23 = (bf16[2064,128]{1,0:T(8,128)(2,1)S(1)}, bf16[2064,128]{1,0:T(8,128)(2,1)S(1)}, u32[]{:S(2)}, u32[]{:S(2)}) collective-permute-start(bf16[2064,128]{1,0:T(8,128)(2,1)S(1)} %collective-permute-done.19.refs_19_), channel_id=1, source_target_pairs={{8,0},{9,1},{10,2},{11,3},{12,4},{13,5},{14,6},{15,7},{0,8},{1,9},... | collective-permute-start | bytes 1585160 | tf_op jit(solution)/shard_map/ppermute | solution.py:266
  75.7 2.0 %collective-permute-start.22 = (bf16[2064,128]{1,0:T(8,128)(2,1)S(1)}, bf16[2064,128]{1,0:T(8,128)(2,1)}, u32[]{:S(2)}, u32[]{:S(2)}) collective-permute-start(bf16[2064,128]{1,0:T(8,128)(2,1)S(1)} %collective-permute-done.18.refs_18_), channel_id=1, source_target_pairs={{8,0},{9,1},{10,2},{11,3},{12,4},{13,5},{14,6},{15,7},{0,8},{1,9},... | collective-permute-start | bytes 1585160 | tf_op jit(solution)/shard_map/ppermute | solution.py:266
  75.7 2.8 %collective-permute-start.21 = (bf16[2064,128]{1,0:T(8,128)(2,1)S(1)}, bf16[2064,128]{1,0:T(8,128)(2,1)}, u32[]{:S(2)}, u32[]{:S(2)}) collective-permute-start(bf16[2064,128]{1,0:T(8,128)(2,1)S(1)} %collective-permute-done.17.refs_17_), channel_id=1, source_target_pairs={{8,0},{9,1},{10,2},{11,3},{12,4},{13,5},{14,6},{15,7},{0,8},{1,9},... | collective-permute-start | bytes 1585160 | tf_op jit(solution)/shard_map/ppermute | solution.py:266

commit v4 on v3

--- a/solution.py
+++ b/solution.py
@@ -9,8 +9,9 @@
 from jax.sharding import PartitionSpec as P
 
 KEY_ROWS = 16
-SLOTS = 48
+SLOTS = 32
 TOGETHER = 8
+FIRST = 4
 BITS = 8
 
 
@@ -47,13 +48,12 @@
             return known[part * rows_of_bits + slot // lanes, slot % lanes]
         return known[part * rows_of_bits + lax.div(slot, lanes), lax.rem(slot, lanes)]
 
-    def product(which, slot, j):
+    def product(which, slot, first, many):
         lefts, rights = [], []
         for part in which:
             code = table[known_of(part, slot)]
             n = lax.shift_right_logical(code, 3 * BITS)
-            for i in range(2):
-                at = 2 * j + i
+            for at in range(first, first + many):
                 which_one = part * BITS + (lax.shift_right_logical(code, 3 * at) & 7)
                 start = table[(1 << BITS) + which_one]
                 lefts.append(block_of(left, start + pos[2 * slot] * n_groups))
@@ -129,7 +129,7 @@
         lax.fori_loop(0, share + 1, clear, 0)
         copy.wait()
 
-        rounds = [(part, j) for part in range(parts) for j in range(1, BITS // 2)]
+        rounds = [(part, j) for part in range(parts) for j in range(FIRST // 2, BITS // 2)]
 
         totals = []
         for part in range(parts):
@@ -138,11 +138,11 @@
             for slot in range(share):
                 later[at * room + total] = jnp.int32(slot)
                 n = lax.shift_right_logical(table[known_of(part, slot)], 3 * BITS)
-                total = total + (n > 2).astype(jnp.int32)
+                total = total + (n > FIRST).astype(jnp.int32)
             totals.append(total)
-            for j in range(2, BITS // 2):
-
-                def more(k, total, at=at + j - 1, part=part, j=j):
+            for j in range(FIRST // 2 + 1, BITS // 2):
+
+                def more(k, total, at=at + j - FIRST // 2, part=part, j=j):
                     slot = later[(at - 1) * room + k]
                     later[at * room + total] = slot
                     n = lax.shift_right_logical(table[known_of(part, slot)], 3 * BITS)
@@ -167,7 +167,7 @@
 
             def some(k, _, i=i, part=part, j=j):
                 which = [later[i * room + k * TOGETHER + m] for m in range(TOGETHER)]
-                made = [product([part], slot, j) for slot in which]
+                made = [product([part], slot, 2 * j, 2) for slot in which]
                 added = [sums[slot] + value for slot, value in zip(which, made)]
                 for slot, value in zip(which, added):
                     sums[slot] = value
@@ -177,7 +177,7 @@
 
     for k in range(slots):
         slot = step * slots + k
-        value = product(range(parts), slot, 0) + sums[slot]
+        value = product(range(parts), slot, 0, FIRST) + sums[slot]
         out[k] = jnp.where(depth * share + slot < count, value, 0.0).astype(out.dtype)
 
 
@@ -194,7 +194,7 @@
     near = len(pieces) * rows * block * 2 <= 16 * 1024 * 1024
     args = [
         pltpu.with_memory_space_constraint(value, pltpu.VMEM if near and use == 2 else pltpu.HBM)
-        for value, _, use in pieces
+        for value, place, use in pieces
     ]
     starts = [k // n_groups * n_row * n_blocks + k % n_groups for k in range(possible)] + [0] * (parts * BITS - possible)
     table = jnp.asarray(np.concatenate([bit_table(), np.array(starts, np.int32)]))
@@ -212,12 +212,12 @@
             pltpu.VMEM((2, n_row * n_rows, parts * BITS, block), jnp.float32),
             pltpu.VMEM((parts * (share // block + 1), block), jnp.int32),
             pltpu.SMEM((parts * (share // block + 1), block), jnp.int32),
-            pltpu.SMEM((parts * (BITS // 2 - 1) * (share + TOGETHER),), jnp.int32),
+            pltpu.SMEM((parts * (BITS // 2) * (share + TOGETHER),), jnp.int32),
             pltpu.SemaphoreType.DMA((2,)),
             pltpu.SemaphoreType.DMA((2,)),
             pltpu.SemaphoreType.DMA,
         ],
-        compiler_params=pltpu.CompilerParams(vmem_limit_bytes=held + 4 * 1024 * 1024),
+        compiler_params=pltpu.CompilerParams(vmem_limit_bytes=held + 3 * 512 * 1024),
         cost_estimate=pl.CostEstimate(
             flops=2 * share * possible * block**3,
             bytes_accessed=2 * total * block * block * 2 + share * block * block * 2,
@@ -300,7 +300,7 @@
     for e in others:
         first[0, e] = move(first[0, 0], 0, e)
     for t in evens:
-        first[t, 0] = move(choose({**ring, 1: after(ring[1], *waited)}, t, 1), t, 0)
+        first[t, 0] = move(choose({**ring, 1: after(ring[1], *waited, first[0, 0])}, t, 1), t, 0)
     waited = [*[first[at] for at in first if at != (0, 0)], *ring.values()]
 
     for t in evens:
@@ -311,6 +311,9 @@
         value = choose({**ring, 2: after(ring[2], *waited)}, t, 0)
         for e in range(n_depth):
             second[t, e] = move(value, t, e, True) if t or e else value
+    for t in evens:
+        for e in others:
+            first[t, e] = after(first[t, e], *[second[at] for at in second if at != (0, 0)])
     for pieces in (right, first, second):
         between_cores(pieces)
     pieces = [(value, at, use) for use, part in enumerate((right, first, second)) for at, value in part.items()]

time: 88.5 us -> 87.2 us (0.985)
  other arithmetic: 3.62 us -> 2.27 us
    select_n x1 -> x2, other arithmetic: 1.47 us -> 0.11 us  [choose(): value = jnp.where(away == k, ring[k], value)]
    ppermute x3, waiting for transfers between devices: 21.7 us -> 22.6 us  [next_col(): lax.ppermute(value, 'col', [(i, (i + step) % n_col) for i in range(n_col)])]
  transfers between devices with their start and end apart: 24 -> 24, of which waited for: 12 -> 15; matrix products, arithmetic and copies ran while one was open for 2% -> 1% of each run, Pallas kernels for 0% -> 0%
where the time goes in v4:
time: 87.2 us; the launch traced here: 86.6 us
  waiting for transfers between devices  55.2 us (63%)
  starting transfers between devices  18.7 us (21%)
  Pallas kernels  9.1 us (10%)
  other arithmetic  2.27 us (3%)
    ppermute x21, waiting for transfers between devices, move(): return lax.ppermute(value, ('row', 'col', 'depth'), pairs)  32.6 us
    ppermute x3, waiting for transfers between devices, next_col(): lax.ppermute(value, 'col', [(i, (i + step) % n_col) for i in range(n_col)])  22.6 us
    ppermute x21, starting transfers between devices, move(): return lax.ppermute(value, ('row', 'col', 'depth'), pairs)  13.7 us
    pallas_call x1, Pallas kernels, products(): pl.pallas_call(functools.partial(product_kernel, plan, places, slots), gr...  9.1 us
    ppermute x3, starting transfers between devices, next_col(): lax.ppermute(value, 'col', [(i, (i + step) % n_col) for i in range(n_col)])  4.95 us
  transfers between devices with their start and end apart: 24, of which 15 were waited for; matrix products, arithmetic and copies ran while one was open for 1% of the time, Pallas kernels for 0%

profile of v4, /device:TPU:0, one launch (start us, length us, event | category | flops | bytes accessed | tf_op | source)
XLA Modules:
  0.0 86.6 jit_solution(4362046736952806205)
XLA Ops:
  0.0 0.0 copy-start
  0.0 0.7 convert_element_type.10
  0.7 0.1 reshape.17
  0.8 1.4 %pad_maximum_fusion.refs_0_ = bf16[2064,128]{1,0:T(8,128)(2,1)S(1)} fusion(bf16[2048,128]{1,0:T(8,128)(2,1)} %bitcast.9, bf16[2064]{0:T(1024)(128)(2,1)S(1)} %pad.6.clone), kind=kLoop, calls=%fused_computation | loop fusion | flops 1056768 | bytes 1056800 | tf_op jit(solution)/shard_map/concatenate | solution.py:237
  2.2 3.0 %collective-permute-start = (bf16[2064,128]{1,0:T(8,128)(2,1)S(1)}, bf16[2064,128]{1,0:T(8,128)(2,1)S(1)}, u32[]{:S(2)}, u32[]{:S(2)}) collective-permute-start(bf16[2064,128]{1,0:T(8,128)(2,1)S(1)} %pad_maximum_fusion.refs_0_), channel_id=1, source_target_pairs={{1,0},{0,1},{3,2},{2,3},{5,4},{4,5},{7,6},{6,7},{9,8},{8,9},{11,10... | collective-permute-start | bytes 1585160 | tf_op jit(solution)/shard_map/ppermute | solution.py:266
  5.2 1.6 %collective-permute-start.8 = (bf16[2064,128]{1,0:T(8,128)(2,1)S(1)}, bf16[2064,128]{1,0:T(8,128)(2,1)S(1)}, u32[]{:S(2)}, u32[]{:S(2)}) collective-permute-start(bf16[2064,128]{1,0:T(8,128)(2,1)S(1)} %pad_maximum_fusion.refs_0_), channel_id=1, source_target_pairs={{0,2},{2,4},{4,6},{6,0},{1,3},{3,5},{5,7},{7,1},{8,10},{10,12},{12... | collective-permute-start | bytes 1585160 | tf_op jit(solution)/shard_map/ppermute | solution.py:257
  6.8 2.2 %collective-permute-start.7 = (bf16[2064,128]{1,0:T(8,128)(2,1)S(1)}, bf16[2064,128]{1,0:T(8,128)(2,1)S(1)}, u32[]{:S(2)}, u32[]{:S(2)}) collective-permute-start(bf16[2064,128]{1,0:T(8,128)(2,1)S(1)} %pad_maximum_fusion.refs_0_), channel_id=1, source_target_pairs={{0,6},{2,0},{4,2},{6,4},{1,7},{3,1},{5,3},{7,5},{8,14},{10,8},{12,... | collective-permute-start | bytes 1585160 | tf_op jit(solution)/shard_map/ppermute | solution.py:257
  9.0 1.5 %collective-permute-start.1 = (bf16[2064,128]{1,0:T(8,128)(2,1)S(1)}, bf16[2064,128]{1,0:T(8,128)(2,1)S(1)}, u32[]{:S(2)}, u32[]{:S(2)}) collective-permute-start(bf16[2064,128]{1,0:T(8,128)(2,1)S(1)} %pad_maximum_fusion.refs_0_), channel_id=1, source_target_pairs={{16,0},{17,1},{18,2},{19,3},{20,4},{21,5},{22,6},{23,7},{24,8},{25... | collective-permute-start | bytes 1585160 | tf_op jit(solution)/shard_map/ppermute | solution.py:266
  10.5 6.7 %collective-permute-done.refs_1_ = bf16[2064,128]{1,0:T(8,128)(2,1)S(1)} collective-permute-done((bf16[2064,128]{1,0:T(8,128)(2,1)S(1)}, bf16[2064,128]{1,0:T(8,128)(2,1)S(1)}, u32[]{:S(2)}, u32[]{:S(2)}) %collective-permute-start) | collective-permute-done | bytes 528416 | tf_op jit(solution)/shard_map/ppermute | solution.py:266
  17.2 1.8 %collective-permute-start.2 = (bf16[2064,128]{1,0:T(8,128)(2,1)S(1)}, bf16[2064,128]{1,0:T(8,128)(2,1)}, u32[]{:S(2)}, u32[]{:S(2)}) collective-permute-start(bf16[2064,128]{1,0:T(8,128)(2,1)S(1)} %collective-permute-done.refs_1_), channel_id=1, source_target_pairs={{16,0},{17,1},{18,2},{19,3},{20,4},{21,5},{22,6},{23,7},{24,8},{25... | collective-permute-start | bytes 1585160 | tf_op jit(solution)/shard_map/ppermute | solution.py:266
  19.0 3.0 %collective-permute-done.8 = bf16[2064,128]{1,0:T(8,128)(2,1)S(1)} collective-permute-done((bf16[2064,128]{1,0:T(8,128)(2,1)S(1)}, bf16[2064,128]{1,0:T(8,128)(2,1)S(1)}, u32[]{:S(2)}, u32[]{:S(2)}) %collective-permute-start.8) | collective-permute-done | bytes 528416 | tf_op jit(solution)/shard_map/ppermute | solution.py:257
  22.0 9.3 %collective-permute-done.7 = bf16[2064,128]{1,0:T(8,128)(2,1)S(1)} collective-permute-done((bf16[2064,128]{1,0:T(8,128)(2,1)S(1)}, bf16[2064,128]{1,0:T(8,128)(2,1)S(1)}, u32[]{:S(2)}, u32[]{:S(2)}) %collective-permute-start.7) | collective-permute-done | bytes 528416 | tf_op jit(solution)/shard_map/ppermute | solution.py:257
  31.3 1.1 %collective-permute-start.11 = (bf16[2064,128]{1,0:T(8,128)(2,1)S(1)}, bf16[2064,128]{1,0:T(8,128)(2,1)S(1)}, u32[]{:S(2)}, u32[]{:S(2)}) collective-permute-start(bf16[2064,128]{1,0:T(8,128)(2,1)S(1)} %collective-permute-done.8), channel_id=1, source_target_pairs={{0,2},{2,4},{4,6},{6,0},{1,3},{3,5},{5,7},{7,1},{8,10},{10,12},{12... | collective-permute-start | bytes 1585160 | tf_op jit(solution)/shard_map/ppermute | solution.py:257
  32.4 0.0 collective-permute-done.1.refs_2_
  32.4 1.0 %collective-permute-done.2.refs_3_ = bf16[2064,128]{1,0:T(8,128)(2,1)} collective-permute-done((bf16[2064,128]{1,0:T(8,128)(2,1)S(1)}, bf16[2064,128]{1,0:T(8,128)(2,1)}, u32[]{:S(2)}, u32[]{:S(2)}) %collective-permute-start.2) | collective-permute-done | bytes 528416 | tf_op jit(solution)/shard_map/ppermute | solution.py:266
  33.4 0.1 broadcast_select_fusion.1.refs_8_
  33.5 0.0 copy-start.1
  33.5 0.1 broadcast_select_fusion
  33.6 1.6 %collective-permute-start.10 = (bf16[2064,128]{1,0:T(8,128)(2,1)S(1)}, bf16[2064,128]{1,0:T(8,128)(2,1)S(1)}, u32[]{:S(2)}, u32[]{:S(2)}) collective-permute-start(bf16[2064,128]{1,0:T(8,128)(2,1)S(1)} %broadcast_select_fusion), channel_id=1, source_target_pairs={{16,0},{17,1},{18,2},{19,3},{20,4},{21,5},{22,6},{23,7},{24,8},{25... | collective-permute-start | bytes 1585160 | tf_op jit(solution)/shard_map/ppermute | solution.py:266
  35.2 0.5 collective-permute-start.9
  35.7 0.0 collective-permute-start.3
  35.7 0.0 copy-done.5
  35.7 0.5 collective-permute-start.5
  36.2 10.3 %collective-permute-done.11.refs_16_ = bf16[2064,128]{1,0:T(8,128)(2,1)S(1)} collective-permute-done((bf16[2064,128]{1,0:T(8,128)(2,1)S(1)}, bf16[2064,128]{1,0:T(8,128)(2,1)S(1)}, u32[]{:S(2)}, u32[]{:S(2)}) %collective-permute-start.11) | collective-permute-done | bytes 528416 | tf_op jit(solution)/shard_map/ppermute | solution.py:257
  46.5 0.0 collective-permute-done.10.refs_10_
  46.5 1.3 %collective-permute-done.9.refs_9_ = bf16[2064,128]{1,0:T(8,128)(2,1)} collective-permute-done((bf16[2064,128]{1,0:T(8,128)(2,1)S(1)}, bf16[2064,128]{1,0:T(8,128)(2,1)}, u32[]{:S(2)}, u32[]{:S(2)}) %collective-permute-start.9) | collective-permute-done | bytes 528416 | tf_op jit(solution)/shard_map/ppermute | solution.py:266
  47.7 0.5 collective-permute-start.12
  48.3 1.4 %collective-permute-start.15 = (bf16[2064,128]{1,0:T(8,128)(2,1)S(1)}, bf16[2064,128]{1,0:T(8,128)(2,1)S(1)}, u32[]{:S(2)}, u32[]{:S(2)}) collective-permute-start(bf16[2064,128]{1,0:T(8,128)(2,1)S(1)} %collective-permute-done.11.refs_16_), channel_id=1, source_target_pairs={{16,0},{17,1},{18,2},{19,3},{21,4},{20,5},{23,6},{22,7},{24,8},{25... | collective-permute-start | bytes 1585160 | tf_op jit(solution)/shard_map/ppermute | solution.py:266
  49.7 0.6 collective-permute-start.14
  50.3 0.0 collective-permute-done.3.refs_4_
  50.3 0.7 collective-permute-start.13
  51.0 0.0 collective-permute-done.5.refs_6_
  51.0 0.0 copy-done.4
  51.0 0.0 copy-start.8
  51.0 0.1 collective-permute-start.4
  51.1 11.7 %collective-permute-done.12.refs_11_ = bf16[2064,128]{1,0:T(8,128)(2,1)} collective-permute-done((bf16[2064,128]{1,0:T(8,128)(2,1)S(1)}, bf16[2064,128]{1,0:T(8,128)(2,1)}, u32[]{:S(2)}, u32[]{:S(2)}) %collective-permute-start.12) | collective-permute-done | bytes 528416 | tf_op jit(solution)/shard_map/ppermute | solution.py:266
  62.8 0.0 collective-permute-start.16
  62.8 5.9 %collective-permute-done.15.refs_19_ = bf16[2064,128]{1,0:T(8,128)(2,1)S(1)} collective-permute-done((bf16[2064,128]{1,0:T(8,128)(2,1)S(1)}, bf16[2064,128]{1,0:T(8,128)(2,1)S(1)}, u32[]{:S(2)}, u32[]{:S(2)}) %collective-permute-start.15) | collective-permute-done | bytes 528416 | tf_op jit(solution)/shard_map/ppermute | solution.py:266
  68.7 0.0 collective-permute-start.6
  68.7 2.2 %collective-permute-done.14.refs_18_ = bf16[2064,128]{1,0:T(8,128)(2,1)S(1)} collective-permute-done((bf16[2064,128]{1,0:T(8,128)(2,1)S(1)}, bf16[2064,128]{1,0:T(8,128)(2,1)S(1)}, u32[]{:S(2)}, u32[]{:S(2)}) %collective-permute-start.14) | collective-permute-done | bytes 528416 | tf_op jit(solution)/shard_map/ppermute | solution.py:266
  70.9 0.0 collective-permute-start.18
  70.9 0.0 collective-permute-done.13.refs_17_
  70.9 0.5 collective-permute-start.20
  71.4 0.0 collective-permute-done.4.refs_5_
  71.4 0.1 collective-permute-start.17
  71.5 0.0 collective-permute-done.16.refs_12_
  71.5 0.4 collective-permute-start.19
  71.9 0.0 copy-done.3
  71.9 0.0 collective-permute-done.6.refs_7_
  71.9 0.1 collective-permute-start.23
  72.1 0.7 collective-permute-done.18.refs_14_
  72.8 0.1 collective-permute-start.22
  72.9 1.4 %collective-permute-done.20.refs_20_ = bf16[2064,128]{1,0:T(8,128)(2,1)S(1)} collective-permute-done((bf16[2064,128]{1,0:T(8,128)(2,1)S(1)}, bf16[2064,128]{1,0:T(8,128)(2,1)S(1)}, u32[]{:S(2)}, u32[]{:S(2)}) %collective-permute-start.20) | collective-permute-done | bytes 528416 | tf_op jit(solution)/shard_map/ppermute | solution.py:266
  74.4 0.2 collective-permute-start.21
  75.2 0.1 constant_dynamic-slice_fusion
  75.3 0.1 copy.6
  75.4 0.1 reshape.15
  75.6 0.1 pad_add_fusion.info
  75.6 0.0 collective-permute-done.17.refs_13_
  75.6 0.9 %collective-permute-done.23.refs_23_ = bf16[2064,128]{1,0:T(8,128)(2,1)S(1)} collective-permute-done((bf16[2064,128]{1,0:T(8,128)(2,1)S(1)}, bf16[2064,128]{1,0:T(8,128)(2,1)S(1)}, u32[]{:S(2)}, u32[]{:S(2)}) %collective-permute-start.23) | collective-permute-done | bytes 528416 | tf_op jit(solution)/shard_map/ppermute | solution.py:266
  76.6 0.1 collective-permute-done.22.refs_22_
  76.7 0.2 collective-permute-done.19.refs_15_
  76.9 0.5 collective-permute-done.21.refs_21_
  77.5 9.1 %shard_map.55 = bf16[96,128,128]{2,1,0:T(8,128)(2,1)} custom-call(s32[4]{0:T(128)S(1)} %pad_add_fusion.info, s32[194]{0:T(256)S(1)} %pad.4.pos, s32[264]{0:T(512)S(1)} %copy-done.1, bf16[2064,128]{1,0:T(8,128)(2,1)} %copy-done.2, bf16[2064,128]{1,0:T(8,128)(2,1)} %copy-done.4, bf16[2064,128]{1,0:T(8,128)(2,1)} %copy-done.5, ...), custom_call_target="tpu_custom_call" | custom-call | flops 3221225472 | bytes 11534336 | tf_op jit(solution)/shard_map/pallas_call | solution.py:202
  (22 shorter events, 0.1 us)
Async XLA Ops:
  0.0 75.2 %copy-start = (s32[1,1,192,2]{2,3,1,0:T(2,128)S(1)}, s32[1,1,192,2]{2,3,1,0:T(2,128)}, u32[]{:S(2)}) copy-start(s32[1,1,192,2]{2,3,1,0:T(2,128)} %param.7) | copy-start | bytes 4612
  2.2 33.5 %copy-start.2 = (bf16[2064,128]{1,0:T(8,128)(2,1)}, bf16[2064,128]{1,0:T(8,128)(2,1)S(1)}, u32[]{:S(2)}) copy-start(bf16[2064,128]{1,0:T(8,128)(2,1)S(1)} %pad_maximum_fusion.refs_0_) | copy-start | bytes 1585156
  2.2 15.0 %collective-permute-start = (bf16[2064,128]{1,0:T(8,128)(2,1)S(1)}, bf16[2064,128]{1,0:T(8,128)(2,1)S(1)}, u32[]{:S(2)}, u32[]{:S(2)}) collective-permute-start(bf16[2064,128]{1,0:T(8,128)(2,1)S(1)} %pad_maximum_fusion.refs_0_), channel_id=1, source_target_pairs={{1,0},{0,1},{3,2},{2,3},{5,4},{4,5},{7,6},{6,7},{9,8},{8,9},{11,10... | collective-permute-start | bytes 1585160 | tf_op jit(solution)/shard_map/ppermute | solution.py:266
  5.2 16.8 %collective-permute-start.8 = (bf16[2064,128]{1,0:T(8,128)(2,1)S(1)}, bf16[2064,128]{1,0:T(8,128)(2,1)S(1)}, u32[]{:S(2)}, u32[]{:S(2)}) collective-permute-start(bf16[2064,128]{1,0:T(8,128)(2,1)S(1)} %pad_maximum_fusion.refs_0_), channel_id=1, source_target_pairs={{0,2},{2,4},{4,6},{6,0},{1,3},{3,5},{5,7},{7,1},{8,10},{10,12},{12... | collective-permute-start | bytes 1585160 | tf_op jit(solution)/shard_map/ppermute | solution.py:257
  6.8 24.5 %collective-permute-start.7 = (bf16[2064,128]{1,0:T(8,128)(2,1)S(1)}, bf16[2064,128]{1,0:T(8,128)(2,1)S(1)}, u32[]{:S(2)}, u32[]{:S(2)}) collective-permute-start(bf16[2064,128]{1,0:T(8,128)(2,1)S(1)} %pad_maximum_fusion.refs_0_), channel_id=1, source_target_pairs={{0,6},{2,0},{4,2},{6,4},{1,7},{3,1},{5,3},{7,5},{8,14},{10,8},{12,... | collective-permute-start | bytes 1585160 | tf_op jit(solution)/shard_map/ppermute | solution.py:257
  9.0 23.4 %collective-permute-start.1 = (bf16[2064,128]{1,0:T(8,128)(2,1)S(1)}, bf16[2064,128]{1,0:T(8,128)(2,1)S(1)}, u32[]{:S(2)}, u32[]{:S(2)}) collective-permute-start(bf16[2064,128]{1,0:T(8,128)(2,1)S(1)} %pad_maximum_fusion.refs_0_), channel_id=1, source_target_pairs={{16,0},{17,1},{18,2},{19,3},{20,4},{21,5},{22,6},{23,7},{24,8},{25... | collective-permute-start | bytes 1585160 | tf_op jit(solution)/shard_map/ppermute | solution.py:266
  17.2 33.8 %copy-start.4 = (bf16[2064,128]{1,0:T(8,128)(2,1)}, bf16[2064,128]{1,0:T(8,128)(2,1)S(1)}, u32[]{:S(2)}) copy-start(bf16[2064,128]{1,0:T(8,128)(2,1)S(1)} %collective-permute-done.refs_1_) | copy-start | bytes 1585156
  17.2 16.2 %collective-permute-start.2 = (bf16[2064,128]{1,0:T(8,128)(2,1)S(1)}, bf16[2064,128]{1,0:T(8,128)(2,1)}, u32[]{:S(2)}, u32[]{:S(2)}) collective-permute-start(bf16[2064,128]{1,0:T(8,128)(2,1)S(1)} %collective-permute-done.refs_1_), channel_id=1, source_target_pairs={{16,0},{17,1},{18,2},{19,3},{20,4},{21,5},{22,6},{23,7},{24,8},{25... | collective-permute-start | bytes 1585160 | tf_op jit(solution)/shard_map/ppermute | solution.py:266
  31.3 15.2 %collective-permute-start.11 = (bf16[2064,128]{1,0:T(8,128)(2,1)S(1)}, bf16[2064,128]{1,0:T(8,128)(2,1)S(1)}, u32[]{:S(2)}, u32[]{:S(2)}) collective-permute-start(bf16[2064,128]{1,0:T(8,128)(2,1)S(1)} %collective-permute-done.8), channel_id=1, source_target_pairs={{0,2},{2,4},{4,6},{6,0},{1,3},{3,5},{5,7},{7,1},{8,10},{10,12},{12... | collective-permute-start | bytes 1585160 | tf_op jit(solution)/shard_map/ppermute | solution.py:257
  32.4 3.3 %copy-start.5 = (bf16[2064,128]{1,0:T(8,128)(2,1)}, bf16[2064,128]{1,0:T(8,128)(2,1)S(1)}, u32[]{:S(2)}) copy-start(bf16[2064,128]{1,0:T(8,128)(2,1)S(1)} %collective-permute-done.1.refs_2_) | copy-start | bytes 1585156
  33.5 38.4 %copy-start.3 = (bf16[2064,128]{1,0:T(8,128)(2,1)}, bf16[2064,128]{1,0:T(8,128)(2,1)S(1)}, u32[]{:S(2)}) copy-start(bf16[2064,128]{1,0:T(8,128)(2,1)S(1)} %broadcast_select_fusion.1.refs_8_) | copy-start | bytes 1585156
  33.5 44.0 %copy-start.1 = (s32[264]{0:T(512)S(1)}, s32[264]{0:T(512)}, u32[]{:S(2)}) copy-start(s32[264]{0:T(512)} %constant.80.clone.table) | copy-start | bytes 3172
  33.6 12.9 %collective-permute-start.10 = (bf16[2064,128]{1,0:T(8,128)(2,1)S(1)}, bf16[2064,128]{1,0:T(8,128)(2,1)S(1)}, u32[]{:S(2)}, u32[]{:S(2)}) collective-permute-start(bf16[2064,128]{1,0:T(8,128)(2,1)S(1)} %broadcast_select_fusion), channel_id=1, source_target_pairs={{16,0},{17,1},{18,2},{19,3},{20,4},{21,5},{22,6},{23,7},{24,8},{25... | collective-permute-start | bytes 1585160 | tf_op jit(solution)/shard_map/ppermute | solution.py:266
  35.2 12.6 %collective-permute-start.9 = (bf16[2064,128]{1,0:T(8,128)(2,1)S(1)}, bf16[2064,128]{1,0:T(8,128)(2,1)}, u32[]{:S(2)}, u32[]{:S(2)}) collective-permute-start(bf16[2064,128]{1,0:T(8,128)(2,1)S(1)} %broadcast_select_fusion.1.refs_8_), channel_id=1, source_target_pairs={{1,0},{0,1},{3,2},{2,3},{5,4},{4,5},{7,6},{6,7},{9,8},{8,9},{11,10... | collective-permute-start | bytes 1585160 | tf_op jit(solution)/shard_map/ppermute | solution.py:266
  35.7 14.6 %collective-permute-start.3 = (bf16[2064,128]{1,0:T(8,128)(2,1)S(1)}, bf16[2064,128]{1,0:T(8,128)(2,1)S(1)}, u32[]{:S(2)}, u32[]{:S(2)}) collective-permute-start(bf16[2064,128]{1,0:T(8,128)(2,1)S(1)} %pad_maximum_fusion.refs_0_), channel_id=1, source_target_pairs={{8,0},{9,1},{10,2},{11,3},{12,4},{13,5},{14,6},{15,7},{0,8},{1,9},... | collective-permute-start | bytes 1585160 | tf_op jit(solution)/shard_map/ppermute | solution.py:266
  35.7 15.3 %collective-permute-start.5 = (bf16[2064,128]{1,0:T(8,128)(2,1)S(1)}, bf16[2064,128]{1,0:T(8,128)(2,1)S(1)}, u32[]{:S(2)}, u32[]{:S(2)}) collective-permute-start(bf16[2064,128]{1,0:T(8,128)(2,1)S(1)} %collective-permute-done.1.refs_2_), channel_id=1, source_target_pairs={{8,0},{9,1},{10,2},{11,3},{12,4},{13,5},{14,6},{15,7},{0,8},{1,9},... | collective-permute-start | bytes 1585160 | tf_op jit(solution)/shard_map/ppermute | solution.py:266
  46.5 27.8 %copy-start.6 = (bf16[2064,128]{1,0:T(8,128)(2,1)}, bf16[2064,128]{1,0:T(8,128)(2,1)S(1)}, u32[]{:S(2)}) copy-start(bf16[2064,128]{1,0:T(8,128)(2,1)S(1)} %collective-permute-done.10.refs_10_) | copy-start | bytes 1585156
  47.7 15.1 %collective-permute-start.12 = (bf16[2064,128]{1,0:T(8,128)(2,1)S(1)}, bf16[2064,128]{1,0:T(8,128)(2,1)}, u32[]{:S(2)}, u32[]{:S(2)}) collective-permute-start(bf16[2064,128]{1,0:T(8,128)(2,1)S(1)} %collective-permute-done.10.refs_10_), channel_id=1, source_target_pairs={{1,0},{0,1},{3,2},{2,3},{5,4},{4,5},{7,6},{6,7},{9,8},{8,9},{11,10... | collective-permute-start | bytes 1585160 | tf_op jit(solution)/shard_map/ppermute | solution.py:266
  48.3 20.5 %collective-permute-start.15 = (bf16[2064,128]{1,0:T(8,128)(2,1)S(1)}, bf16[2064,128]{1,0:T(8,128)(2,1)S(1)}, u32[]{:S(2)}, u32[]{:S(2)}) collective-permute-start(bf16[2064,128]{1,0:T(8,128)(2,1)S(1)} %collective-permute-done.11.refs_16_), channel_id=1, source_target_pairs={{16,0},{17,1},{18,2},{19,3},{21,4},{20,5},{23,6},{22,7},{24,8},{25... | collective-permute-start | bytes 1585160 | tf_op jit(solution)/shard_map/ppermute | solution.py:266
  49.7 21.2 %collective-permute-start.14 = (bf16[2064,128]{1,0:T(8,128)(2,1)S(1)}, bf16[2064,128]{1,0:T(8,128)(2,1)S(1)}, u32[]{:S(2)}, u32[]{:S(2)}) collective-permute-start(bf16[2064,128]{1,0:T(8,128)(2,1)S(1)} %collective-permute-done.11.refs_16_), channel_id=1, source_target_pairs={{16,0},{17,1},{18,2},{19,3},{20,4},{21,5},{22,6},{23,7},{24,8},{25... | collective-permute-start | bytes 1585160 | tf_op jit(solution)/shard_map/ppermute | solution.py:266
  50.3 24.0 %copy-start.7 = (bf16[2064,128]{1,0:T(8,128)(2,1)}, bf16[2064,128]{1,0:T(8,128)(2,1)S(1)}, u32[]{:S(2)}) copy-start(bf16[2064,128]{1,0:T(8,128)(2,1)S(1)} %collective-permute-done.3.refs_4_) | copy-start | bytes 1585156
  50.3 20.6 %collective-permute-start.13 = (bf16[2064,128]{1,0:T(8,128)(2,1)S(1)}, bf16[2064,128]{1,0:T(8,128)(2,1)S(1)}, u32[]{:S(2)}, u32[]{:S(2)}) collective-permute-start(bf16[2064,128]{1,0:T(8,128)(2,1)S(1)} %collective-permute-done.11.refs_16_), channel_id=1, source_target_pairs={{0,0},{1,1},{2,2},{3,3},{5,4},{4,5},{7,6},{6,7},{8,8},{9,9},{10,10... | collective-permute-start | bytes 1585160 | tf_op jit(solution)/shard_map/ppermute | solution.py:266
  51.0 23.3 %copy-start.8 = (bf16[2064,128]{1,0:T(8,128)(2,1)}, bf16[2064,128]{1,0:T(8,128)(2,1)S(1)}, u32[]{:S(2)}) copy-start(bf16[2064,128]{1,0:T(8,128)(2,1)S(1)} %collective-permute-done.5.refs_6_) | copy-start | bytes 1585156
  51.0 20.4 %collective-permute-start.4 = (bf16[2064,128]{1,0:T(8,128)(2,1)S(1)}, bf16[2064,128]{1,0:T(8,128)(2,1)S(1)}, u32[]{:S(2)}, u32[]{:S(2)}) collective-permute-start(bf16[2064,128]{1,0:T(8,128)(2,1)S(1)} %collective-permute-done.refs_1_), channel_id=1, source_target_pairs={{8,0},{9,1},{10,2},{11,3},{12,4},{13,5},{14,6},{15,7},{0,8},{1,9},... | collective-permute-start | bytes 1585160 | tf_op jit(solution)/shard_map/ppermute | solution.py:266
  62.8 8.7 %collective-permute-start.16 = (bf16[2064,128]{1,0:T(8,128)(2,1)S(1)}, bf16[2064,128]{1,0:T(8,128)(2,1)S(1)}, u32[]{:S(2)}, u32[]{:S(2)}) collective-permute-start(bf16[2064,128]{1,0:T(8,128)(2,1)S(1)} %broadcast_select_fusion.1.refs_8_), channel_id=1, source_target_pairs={{8,0},{9,1},{10,2},{11,3},{12,4},{13,5},{14,6},{15,7},{0,8},{1,9},... | collective-permute-start | bytes 1585160 | tf_op jit(solution)/shard_map/ppermute | solution.py:266
  68.7 3.2 %collective-permute-start.6 = (bf16[2064,128]{1,0:T(8,128)(2,1)}, bf16[2064,128]{1,0:T(8,128)(2,1)S(1)}, u32[]{:S(2)}, u32[]{:S(2)}) collective-permute-start(bf16[2064,128]{1,0:T(8,128)(2,1)} %collective-permute-done.2.refs_3_), channel_id=1, source_target_pairs={{8,0},{9,1},{10,2},{11,3},{12,4},{13,5},{14,6},{15,7},{0,8},{1,9},... | collective-permute-start | bytes 1585160 | tf_op jit(solution)/shard_map/ppermute | solution.py:266
  70.9 1.9 %collective-permute-start.18 = (bf16[2064,128]{1,0:T(8,128)(2,1)S(1)}, bf16[2064,128]{1,0:T(8,128)(2,1)S(1)}, u32[]{:S(2)}, u32[]{:S(2)}) collective-permute-start(bf16[2064,128]{1,0:T(8,128)(2,1)S(1)} %collective-permute-done.10.refs_10_), channel_id=1, source_target_pairs={{8,0},{9,1},{10,2},{11,3},{12,4},{13,5},{14,6},{15,7},{0,8},{1,9},... | collective-permute-start | bytes 1585160 | tf_op jit(solution)/shard_map/ppermute | solution.py:266
  70.9 3.4 %collective-permute-start.20 = (bf16[2064,128]{1,0:T(8,128)(2,1)S(1)}, bf16[2064,128]{1,0:T(8,128)(2,1)S(1)}, u32[]{:S(2)}, u32[]{:S(2)}) collective-permute-start(bf16[2064,128]{1,0:T(8,128)(2,1)S(1)} %collective-permute-done.11.refs_16_), channel_id=1, source_target_pairs={{8,0},{9,1},{10,2},{11,3},{12,4},{13,5},{14,6},{15,7},{0,8},{1,9},... | collective-permute-start | bytes 1585160 | tf_op jit(solution)/shard_map/ppermute | solution.py:266
  71.4 2.9 %copy-start.9 = (bf16[2064,128]{1,0:T(8,128)(2,1)}, bf16[2064,128]{1,0:T(8,128)(2,1)S(1)}, u32[]{:S(2)}) copy-start(bf16[2064,128]{1,0:T(8,128)(2,1)S(1)} %collective-permute-done.4.refs_5_) | copy-start | bytes 1585156
  71.4 4.2 %collective-permute-start.17 = (bf16[2064,128]{1,0:T(8,128)(2,1)}, bf16[2064,128]{1,0:T(8,128)(2,1)}, u32[]{:S(2)}, u32[]{:S(2)}) collective-permute-start(bf16[2064,128]{1,0:T(8,128)(2,1)} %collective-permute-done.9.refs_9_), channel_id=1, source_target_pairs={{8,0},{9,1},{10,2},{11,3},{12,4},{13,5},{14,6},{15,7},{0,8},{1,9},... | collective-permute-start | bytes 1585160 | tf_op jit(solution)/shard_map/ppermute | solution.py:266
  71.5 2.8 %copy-start.10 = (bf16[2064,128]{1,0:T(8,128)(2,1)}, bf16[2064,128]{1,0:T(8,128)(2,1)S(1)}, u32[]{:S(2)}) copy-start(bf16[2064,128]{1,0:T(8,128)(2,1)S(1)} %collective-permute-done.16.refs_12_) | copy-start | bytes 1585156
  71.5 5.4 %collective-permute-start.19 = (bf16[2064,128]{1,0:T(8,128)(2,1)}, bf16[2064,128]{1,0:T(8,128)(2,1)}, u32[]{:S(2)}, u32[]{:S(2)}) collective-permute-start(bf16[2064,128]{1,0:T(8,128)(2,1)} %collective-permute-done.12.refs_11_), channel_id=1, source_target_pairs={{8,0},{9,1},{10,2},{11,3},{12,4},{13,5},{14,6},{15,7},{0,8},{1,9},... | collective-permute-start | bytes 1585160 | tf_op jit(solution)/shard_map/ppermute | solution.py:266
  71.9 2.4 %copy-start.11 = (bf16[2064,128]{1,0:T(8,128)(2,1)}, bf16[2064,128]{1,0:T(8,128)(2,1)S(1)}, u32[]{:S(2)}) copy-start(bf16[2064,128]{1,0:T(8,128)(2,1)S(1)} %collective-permute-done.6.refs_7_) | copy-start | bytes 1585156
  71.9 4.6 %collective-permute-start.23 = (bf16[2064,128]{1,0:T(8,128)(2,1)S(1)}, bf16[2064,128]{1,0:T(8,128)(2,1)S(1)}, u32[]{:S(2)}, u32[]{:S(2)}) collective-permute-start(bf16[2064,128]{1,0:T(8,128)(2,1)S(1)} %collective-permute-done.15.refs_19_), channel_id=1, source_target_pairs={{8,0},{9,1},{10,2},{11,3},{12,4},{13,5},{14,6},{15,7},{0,8},{1,9},... | collective-permute-start | bytes 1585160 | tf_op jit(solution)/shard_map/ppermute | solution.py:266
  72.8 1.6 %copy-start.12 = (bf16[2064,128]{1,0:T(8,128)(2,1)}, bf16[2064,128]{1,0:T(8,128)(2,1)S(1)}, u32[]{:S(2)}) copy-start(bf16[2064,128]{1,0:T(8,128)(2,1)S(1)} %collective-permute-done.18.refs_14_) | copy-start | bytes 1585156
  72.8 3.9 %collective-permute-start.22 = (bf16[2064,128]{1,0:T(8,128)(2,1)S(1)}, bf16[2064,128]{1,0:T(8,128)(2,1)}, u32[]{:S(2)}, u32[]{:S(2)}) collective-permute-start(bf16[2064,128]{1,0:T(8,128)(2,1)S(1)} %collective-permute-done.14.refs_18_), channel_id=1, source_target_pairs={{8,0},{9,1},{10,2},{11,3},{12,4},{13,5},{14,6},{15,7},{0,8},{1,9},... | collective-permute-start | bytes 1585160 | tf_op jit(solution)/shard_map/ppermute | solution.py:266
  74.4 3.1 %collective-permute-start.21 = (bf16[2064,128]{1,0:T(8,128)(2,1)S(1)}, bf16[2064,128]{1,0:T(8,128)(2,1)}, u32[]{:S(2)}, u32[]{:S(2)}) collective-permute-start(bf16[2064,128]{1,0:T(8,128)(2,1)S(1)} %collective-permute-done.13.refs_17_), channel_id=1, source_target_pairs={{8,0},{9,1},{10,2},{11,3},{12,4},{13,5},{14,6},{15,7},{0,8},{1,9},... | collective-permute-start | bytes 1585160 | tf_op jit(solution)/shard_map/ppermute | solution.py:266

commit v5 on v4

--- a/solution.py
+++ b/solution.py
@@ -193,7 +193,7 @@
     places = [(place, use) for _, place, use in pieces]
     near = len(pieces) * rows * block * 2 <= 16 * 1024 * 1024
     args = [
-        pltpu.with_memory_space_constraint(value, pltpu.VMEM if near and use == 2 else pltpu.HBM)
+        pltpu.with_memory_space_constraint(value, pltpu.VMEM if near and (use == 2 or use and place == (3, 1)) else pltpu.HBM)
         for value, place, use in pieces
     ]
     starts = [k // n_groups * n_row * n_blocks + k % n_groups for k in range(possible)] + [0] * (parts * BITS - possible)
@@ -232,9 +232,9 @@
 
 def payload(x_blocks, col_slot):
     block = x_blocks.shape[-1]
-    keys = col_slot.reshape(-1).astype(x_blocks.dtype)
-    keys = jnp.pad(keys, (0, -keys.shape[0] % KEY_ROWS))
-    return jnp.concatenate([x_blocks.reshape(-1, block), jnp.broadcast_to(keys[:, None], (keys.shape[0], block))])
+    keys = jnp.broadcast_to(col_slot[:, :, None], (*col_slot.shape, block)).reshape(-1, block)
+    keys = jnp.pad(keys, ((0, -keys.shape[0] % KEY_ROWS), (0, 0)))
+    return jnp.concatenate([x_blocks.reshape(-1, block), keys.astype(x_blocks.dtype)])
 
 
 def body(sizes, x_blocks, col_slot, out_pos, out_count):
@@ -317,6 +317,7 @@
     for pieces in (right, first, second):
         between_cores(pieces)
     pieces = [(value, at, use) for use, part in enumerate((right, first, second)) for at, value in part.items()]
+    pieces.sort(key=lambda piece: [1, 0, 2][piece[2]])
     plan = (n_row, n_depth, n_rows, n_groups, share)
     return products(plan, info, pos, pieces)[None, None]
 

time: 87.2 us -> 87.1 us (level)
  local copies, waits for them, and re-layouts: 0.47 us -> 2 us
  waiting for transfers between devices: 55.2 us -> 53.7 us
    unnamed x26 -> x30, local copies, waits for them, and re-layouts: 0.05 us -> 1.58 us
    ppermute x21, waiting for transfers between devices: 32.6 us -> 31.1 us  [move(): return lax.ppermute(value, ('row', 'col', 'depth'), pairs)]
where the time goes in v5:
time: 87.1 us; the launch traced here: 86.5 us
  waiting for transfers between devices  53.7 us (62%)
  starting transfers between devices  18.5 us (21%)
  Pallas kernels  9.1 us (10%)
  other arithmetic  2.27 us (3%)
  local copies, waits for them, and re-layouts  2 us (2%)
    ppermute x21, waiting for transfers between devices, move(): return lax.ppermute(value, ('row', 'col', 'depth'), pairs)  31.1 us
    ppermute x3, waiting for transfers between devices, next_col(): lax.ppermute(value, 'col', [(i, (i + step) % n_col) for i in range(n_col)])  22.6 us
    ppermute x21, starting transfers between devices, move(): return lax.ppermute(value, ('row', 'col', 'depth'), pairs)  13.6 us
    pallas_call x1, Pallas kernels, products(): pl.pallas_call(functools.partial(product_kernel, plan, places, slots), gr...  9.1 us
    ppermute x3, starting transfers between devices, next_col(): lax.ppermute(value, 'col', [(i, (i + step) % n_col) for i in range(n_col)])  4.95 us
  transfers between devices with their start and end apart: 24, of which 15 were waited for; matrix products, arithmetic and copies ran while one was open for 1% of the time, Pallas kernels for 0%

profile of v5, /device:TPU:0, one launch (start us, length us, event | category | flops | bytes accessed | tf_op | source)
XLA Modules:
  0.0 86.5 jit_solution(16359814002117629648)
XLA Ops:
  0.0 0.0 copy-start
  0.0 0.7 convert_element_type.7
  0.7 0.1 reshape.15
  0.8 1.4 %pad_maximum_fusion.refs_8_ = bf16[2064,128]{1,0:T(8,128)(2,1)S(1)} fusion(bf16[2048,128]{1,0:T(8,128)(2,1)} %bitcast.9, bf16[2064]{0:T(1024)(128)(2,1)S(1)} %pad.6.clone), kind=kLoop, calls=%fused_computation | loop fusion | flops 1056768 | bytes 1056800 | tf_op jit(solution)/shard_map/concatenate | solution.py:237
  2.2 0.0 copy-start.2
  2.2 3.0 %collective-permute-start.2 = (bf16[2064,128]{1,0:T(8,128)(2,1)S(1)}, bf16[2064,128]{1,0:T(8,128)(2,1)S(1)}, u32[]{:S(2)}, u32[]{:S(2)}) collective-permute-start(bf16[2064,128]{1,0:T(8,128)(2,1)S(1)} %pad_maximum_fusion.refs_8_), channel_id=1, source_target_pairs={{1,0},{0,1},{3,2},{2,3},{5,4},{4,5},{7,6},{6,7},{9,8},{8,9},{11,10... | collective-permute-start | bytes 1585160 | tf_op jit(solution)/shard_map/ppermute | solution.py:266
  5.2 1.6 %collective-permute-start.1 = (bf16[2064,128]{1,0:T(8,128)(2,1)S(1)}, bf16[2064,128]{1,0:T(8,128)(2,1)S(1)}, u32[]{:S(2)}, u32[]{:S(2)}) collective-permute-start(bf16[2064,128]{1,0:T(8,128)(2,1)S(1)} %pad_maximum_fusion.refs_8_), channel_id=1, source_target_pairs={{0,2},{2,4},{4,6},{6,0},{1,3},{3,5},{5,7},{7,1},{8,10},{10,12},{12... | collective-permute-start | bytes 1585160 | tf_op jit(solution)/shard_map/ppermute | solution.py:257
  6.8 2.2 %collective-permute-start = (bf16[2064,128]{1,0:T(8,128)(2,1)S(1)}, bf16[2064,128]{1,0:T(8,128)(2,1)S(1)}, u32[]{:S(2)}, u32[]{:S(2)}) collective-permute-start(bf16[2064,128]{1,0:T(8,128)(2,1)S(1)} %pad_maximum_fusion.refs_8_), channel_id=1, source_target_pairs={{0,6},{2,0},{4,2},{6,4},{1,7},{3,1},{5,3},{7,5},{8,14},{10,8},{12,... | collective-permute-start | bytes 1585160 | tf_op jit(solution)/shard_map/ppermute | solution.py:257
  9.0 1.5 %collective-permute-start.3 = (bf16[2064,128]{1,0:T(8,128)(2,1)S(1)}, bf16[2064,128]{1,0:T(8,128)(2,1)S(1)}, u32[]{:S(2)}, u32[]{:S(2)}) collective-permute-start(bf16[2064,128]{1,0:T(8,128)(2,1)S(1)} %pad_maximum_fusion.refs_8_), channel_id=1, source_target_pairs={{16,0},{17,1},{18,2},{19,3},{20,4},{21,5},{22,6},{23,7},{24,8},{25... | collective-permute-start | bytes 1585160 | tf_op jit(solution)/shard_map/ppermute | solution.py:266
  10.5 6.7 %collective-permute-done.2.refs_9_ = bf16[2064,128]{1,0:T(8,128)(2,1)S(1)} collective-permute-done((bf16[2064,128]{1,0:T(8,128)(2,1)S(1)}, bf16[2064,128]{1,0:T(8,128)(2,1)S(1)}, u32[]{:S(2)}, u32[]{:S(2)}) %collective-permute-start.2) | collective-permute-done | bytes 528416 | tf_op jit(solution)/shard_map/ppermute | solution.py:266
  17.2 1.8 %collective-permute-start.4 = (bf16[2064,128]{1,0:T(8,128)(2,1)S(1)}, bf16[2064,128]{1,0:T(8,128)(2,1)}, u32[]{:S(2)}, u32[]{:S(2)}) collective-permute-start(bf16[2064,128]{1,0:T(8,128)(2,1)S(1)} %collective-permute-done.2.refs_9_), channel_id=1, source_target_pairs={{16,0},{17,1},{18,2},{19,3},{20,4},{21,5},{22,6},{23,7},{24,8},{25... | collective-permute-start | bytes 1585160 | tf_op jit(solution)/shard_map/ppermute | solution.py:266
  19.0 3.0 %collective-permute-done.1 = bf16[2064,128]{1,0:T(8,128)(2,1)S(1)} collective-permute-done((bf16[2064,128]{1,0:T(8,128)(2,1)S(1)}, bf16[2064,128]{1,0:T(8,128)(2,1)S(1)}, u32[]{:S(2)}, u32[]{:S(2)}) %collective-permute-start.1) | collective-permute-done | bytes 528416 | tf_op jit(solution)/shard_map/ppermute | solution.py:257
  22.0 9.3 %collective-permute-done = bf16[2064,128]{1,0:T(8,128)(2,1)S(1)} collective-permute-done((bf16[2064,128]{1,0:T(8,128)(2,1)S(1)}, bf16[2064,128]{1,0:T(8,128)(2,1)S(1)}, u32[]{:S(2)}, u32[]{:S(2)}) %collective-permute-start) | collective-permute-done | bytes 528416 | tf_op jit(solution)/shard_map/ppermute | solution.py:257
  31.3 1.1 %collective-permute-start.7 = (bf16[2064,128]{1,0:T(8,128)(2,1)S(1)}, bf16[2064,128]{1,0:T(8,128)(2,1)S(1)}, u32[]{:S(2)}, u32[]{:S(2)}) collective-permute-start(bf16[2064,128]{1,0:T(8,128)(2,1)S(1)} %collective-permute-done.1), channel_id=1, source_target_pairs={{0,2},{2,4},{4,6},{6,0},{1,3},{3,5},{5,7},{7,1},{8,10},{10,12},{12... | collective-permute-start | bytes 1585160 | tf_op jit(solution)/shard_map/ppermute | solution.py:257
  32.4 0.0 collective-permute-done.3.refs_10_
  32.4 1.0 %collective-permute-done.4.refs_11_ = bf16[2064,128]{1,0:T(8,128)(2,1)} collective-permute-done((bf16[2064,128]{1,0:T(8,128)(2,1)S(1)}, bf16[2064,128]{1,0:T(8,128)(2,1)}, u32[]{:S(2)}, u32[]{:S(2)}) %collective-permute-start.4) | collective-permute-done | bytes 528416 | tf_op jit(solution)/shard_map/ppermute | solution.py:266
  33.4 0.1 broadcast_select_fusion.1.refs_0_
  33.5 0.0 copy-start.1
  33.5 0.1 broadcast_select_fusion
  33.6 1.6 %collective-permute-start.6 = (bf16[2064,128]{1,0:T(8,128)(2,1)S(1)}, bf16[2064,128]{1,0:T(8,128)(2,1)S(1)}, u32[]{:S(2)}, u32[]{:S(2)}) collective-permute-start(bf16[2064,128]{1,0:T(8,128)(2,1)S(1)} %broadcast_select_fusion), channel_id=1, source_target_pairs={{16,0},{17,1},{18,2},{19,3},{20,4},{21,5},{22,6},{23,7},{24,8},{25... | collective-permute-start | bytes 1585160 | tf_op jit(solution)/shard_map/ppermute | solution.py:266
  35.2 0.5 collective-permute-start.5
  35.7 0.0 collective-permute-start.16
  35.7 0.5 collective-permute-start.18
  36.2 10.3 %collective-permute-done.7.refs_16_ = bf16[2064,128]{1,0:T(8,128)(2,1)S(1)} collective-permute-done((bf16[2064,128]{1,0:T(8,128)(2,1)S(1)}, bf16[2064,128]{1,0:T(8,128)(2,1)S(1)}, u32[]{:S(2)}, u32[]{:S(2)}) %collective-permute-start.7) | collective-permute-done | bytes 528416 | tf_op jit(solution)/shard_map/ppermute | solution.py:257
  46.5 0.0 collective-permute-done.6.refs_2_
  46.5 1.2 %collective-permute-done.5.refs_1_ = bf16[2064,128]{1,0:T(8,128)(2,1)S(1)} collective-permute-done((bf16[2064,128]{1,0:T(8,128)(2,1)S(1)}, bf16[2064,128]{1,0:T(8,128)(2,1)S(1)}, u32[]{:S(2)}, u32[]{:S(2)}) %collective-permute-start.5) | collective-permute-done | bytes 528416 | tf_op jit(solution)/shard_map/ppermute | solution.py:266
  47.6 0.5 collective-permute-start.8
  48.2 1.4 %collective-permute-start.11 = (bf16[2064,128]{1,0:T(8,128)(2,1)S(1)}, bf16[2064,128]{1,0:T(8,128)(2,1)S(1)}, u32[]{:S(2)}, u32[]{:S(2)}) collective-permute-start(bf16[2064,128]{1,0:T(8,128)(2,1)S(1)} %collective-permute-done.7.refs_16_), channel_id=1, source_target_pairs={{16,0},{17,1},{18,2},{19,3},{21,4},{20,5},{23,6},{22,7},{24,8},{25... | collective-permute-start | bytes 1585160 | tf_op jit(solution)/shard_map/ppermute | solution.py:266
  49.6 0.6 collective-permute-start.10
  50.2 0.0 collective-permute-done.16.refs_12_
  50.2 0.7 collective-permute-start.9
  50.9 0.0 collective-permute-done.18.refs_14_
  50.9 0.1 collective-permute-start.17
  51.0 11.7 %collective-permute-done.8.refs_3_ = bf16[2064,128]{1,0:T(8,128)(2,1)} collective-permute-done((bf16[2064,128]{1,0:T(8,128)(2,1)S(1)}, bf16[2064,128]{1,0:T(8,128)(2,1)}, u32[]{:S(2)}, u32[]{:S(2)}) %collective-permute-start.8) | collective-permute-done | bytes 528416 | tf_op jit(solution)/shard_map/ppermute | solution.py:266
  62.7 0.0 collective-permute-start.19
  62.7 5.9 %collective-permute-done.11.refs_19_ = bf16[2064,128]{1,0:T(8,128)(2,1)S(1)} collective-permute-done((bf16[2064,128]{1,0:T(8,128)(2,1)S(1)}, bf16[2064,128]{1,0:T(8,128)(2,1)S(1)}, u32[]{:S(2)}, u32[]{:S(2)}) %collective-permute-start.11) | collective-permute-done | bytes 528416 | tf_op jit(solution)/shard_map/ppermute | solution.py:266
  68.6 0.0 collective-permute-start.12
  68.6 2.2 %collective-permute-done.10.refs_18_ = bf16[2064,128]{1,0:T(8,128)(2,1)S(1)} collective-permute-done((bf16[2064,128]{1,0:T(8,128)(2,1)S(1)}, bf16[2064,128]{1,0:T(8,128)(2,1)S(1)}, u32[]{:S(2)}, u32[]{:S(2)}) %collective-permute-start.10) | collective-permute-done | bytes 528416 | tf_op jit(solution)/shard_map/ppermute | solution.py:266
  70.8 0.0 collective-permute-start.14
  70.8 0.0 collective-permute-done.9.refs_17_
  70.8 0.5 collective-permute-start.13
  71.3 0.0 collective-permute-done.17.refs_13_
  71.3 0.1 collective-permute-start.20
  71.4 0.7 copy-done.10
  72.1 0.0 collective-permute-done.19.refs_15_
  72.1 0.0 collective-permute-start.15
  72.1 0.0 collective-permute-done.12.refs_4_
  72.1 0.5 collective-permute-start.23
  72.6 0.1 collective-permute-done.14.refs_6_
  72.7 0.1 collective-permute-start.22
  72.8 0.6 collective-permute-done.13.refs_5_
  73.5 0.0 copy-done.7
  73.5 0.8 copy-done.14
  74.3 0.1 collective-permute-start.21
  75.1 0.1 constant_dynamic-slice_fusion
  75.2 0.1 copy.6
  75.3 0.1 reshape.13
  75.5 0.1 pad_add_fusion.info
  75.5 0.2 collective-permute-done.20.refs_20_
  75.7 0.1 collective-permute-done.23.refs_23_
  75.9 0.8 collective-permute-done.22.refs_22_
  76.6 0.0 collective-permute-done.15.refs_7_
  76.6 0.8 collective-permute-done.21.refs_21_
  77.4 9.1 %shard_map.55 = bf16[96,128,128]{2,1,0:T(8,128)(2,1)} custom-call(s32[4]{0:T(128)S(1)} %pad_add_fusion.info, s32[194]{0:T(256)S(1)} %pad.4.pos, s32[264]{0:T(512)S(1)} %copy-done.1, bf16[2064,128]{1,0:T(8,128)(2,1)} %copy-done.3, bf16[2064,128]{1,0:T(8,128)(2,1)} %copy-done.7, bf16[2064,128]{1,0:T(8,128)(2,1)} %copy-done.6, ...), custom_call_target="tpu_custom_call" | custom-call | flops 3221225472 | bytes 11534336 | tf_op jit(solution)/shard_map/pallas_call | solution.py:202
  (26 shorter events, 0.1 us)
Async XLA Ops:
  0.0 75.1 %copy-start = (s32[1,1,192,2]{2,3,1,0:T(2,128)S(1)}, s32[1,1,192,2]{2,3,1,0:T(2,128)}, u32[]{:S(2)}) copy-start(s32[1,1,192,2]{2,3,1,0:T(2,128)} %param.7) | copy-start | bytes 4612
  2.2 33.5 %copy-start.2 = (bf16[2064,128]{1,0:T(8,128)(2,1)}, bf16[2064,128]{1,0:T(8,128)(2,1)S(1)}, u32[]{:S(2)}) copy-start(bf16[2064,128]{1,0:T(8,128)(2,1)S(1)} %pad_maximum_fusion.refs_8_) | copy-start | bytes 1585156
  2.2 15.0 %collective-permute-start.2 = (bf16[2064,128]{1,0:T(8,128)(2,1)S(1)}, bf16[2064,128]{1,0:T(8,128)(2,1)S(1)}, u32[]{:S(2)}, u32[]{:S(2)}) collective-permute-start(bf16[2064,128]{1,0:T(8,128)(2,1)S(1)} %pad_maximum_fusion.refs_8_), channel_id=1, source_target_pairs={{1,0},{0,1},{3,2},{2,3},{5,4},{4,5},{7,6},{6,7},{9,8},{8,9},{11,10... | collective-permute-start | bytes 1585160 | tf_op jit(solution)/shard_map/ppermute | solution.py:266
  5.2 16.8 %collective-permute-start.1 = (bf16[2064,128]{1,0:T(8,128)(2,1)S(1)}, bf16[2064,128]{1,0:T(8,128)(2,1)S(1)}, u32[]{:S(2)}, u32[]{:S(2)}) collective-permute-start(bf16[2064,128]{1,0:T(8,128)(2,1)S(1)} %pad_maximum_fusion.refs_8_), channel_id=1, source_target_pairs={{0,2},{2,4},{4,6},{6,0},{1,3},{3,5},{5,7},{7,1},{8,10},{10,12},{12... | collective-permute-start | bytes 1585160 | tf_op jit(solution)/shard_map/ppermute | solution.py:257
  6.8 24.5 %collective-permute-start = (bf16[2064,128]{1,0:T(8,128)(2,1)S(1)}, bf16[2064,128]{1,0:T(8,128)(2,1)S(1)}, u32[]{:S(2)}, u32[]{:S(2)}) collective-permute-start(bf16[2064,128]{1,0:T(8,128)(2,1)S(1)} %pad_maximum_fusion.refs_8_), channel_id=1, source_target_pairs={{0,6},{2,0},{4,2},{6,4},{1,7},{3,1},{5,3},{7,5},{8,14},{10,8},{12,... | collective-permute-start | bytes 1585160 | tf_op jit(solution)/shard_map/ppermute | solution.py:257
  9.0 23.4 %collective-permute-start.3 = (bf16[2064,128]{1,0:T(8,128)(2,1)S(1)}, bf16[2064,128]{1,0:T(8,128)(2,1)S(1)}, u32[]{:S(2)}, u32[]{:S(2)}) collective-permute-start(bf16[2064,128]{1,0:T(8,128)(2,1)S(1)} %pad_maximum_fusion.refs_8_), channel_id=1, source_target_pairs={{16,0},{17,1},{18,2},{19,3},{20,4},{21,5},{22,6},{23,7},{24,8},{25... | collective-permute-start | bytes 1585160 | tf_op jit(solution)/shard_map/ppermute | solution.py:266
  17.2 33.7 %copy-start.4 = (bf16[2064,128]{1,0:T(8,128)(2,1)}, bf16[2064,128]{1,0:T(8,128)(2,1)S(1)}, u32[]{:S(2)}) copy-start(bf16[2064,128]{1,0:T(8,128)(2,1)S(1)} %collective-permute-done.2.refs_9_) | copy-start | bytes 1585156
  17.2 16.2 %collective-permute-start.4 = (bf16[2064,128]{1,0:T(8,128)(2,1)S(1)}, bf16[2064,128]{1,0:T(8,128)(2,1)}, u32[]{:S(2)}, u32[]{:S(2)}) collective-permute-start(bf16[2064,128]{1,0:T(8,128)(2,1)S(1)} %collective-permute-done.2.refs_9_), channel_id=1, source_target_pairs={{16,0},{17,1},{18,2},{19,3},{20,4},{21,5},{22,6},{23,7},{24,8},{25... | collective-permute-start | bytes 1585160 | tf_op jit(solution)/shard_map/ppermute | solution.py:266
  31.3 15.2 %collective-permute-start.7 = (bf16[2064,128]{1,0:T(8,128)(2,1)S(1)}, bf16[2064,128]{1,0:T(8,128)(2,1)S(1)}, u32[]{:S(2)}, u32[]{:S(2)}) collective-permute-start(bf16[2064,128]{1,0:T(8,128)(2,1)S(1)} %collective-permute-done.1), channel_id=1, source_target_pairs={{0,2},{2,4},{4,6},{6,0},{1,3},{3,5},{5,7},{7,1},{8,10},{10,12},{12... | collective-permute-start | bytes 1585160 | tf_op jit(solution)/shard_map/ppermute | solution.py:257
  32.4 3.3 %copy-start.5 = (bf16[2064,128]{1,0:T(8,128)(2,1)}, bf16[2064,128]{1,0:T(8,128)(2,1)S(1)}, u32[]{:S(2)}) copy-start(bf16[2064,128]{1,0:T(8,128)(2,1)S(1)} %collective-permute-done.3.refs_10_) | copy-start | bytes 1585156
  33.5 39.4 %copy-start.3 = (bf16[2064,128]{1,0:T(8,128)(2,1)}, bf16[2064,128]{1,0:T(8,128)(2,1)S(1)}, u32[]{:S(2)}) copy-start(bf16[2064,128]{1,0:T(8,128)(2,1)S(1)} %broadcast_select_fusion.1.refs_0_) | copy-start | bytes 1585156
  33.5 43.9 %copy-start.1 = (s32[264]{0:T(512)S(1)}, s32[264]{0:T(512)}, u32[]{:S(2)}) copy-start(s32[264]{0:T(512)} %constant.80.clone.table) | copy-start | bytes 3172
  33.6 12.9 %collective-permute-start.6 = (bf16[2064,128]{1,0:T(8,128)(2,1)S(1)}, bf16[2064,128]{1,0:T(8,128)(2,1)S(1)}, u32[]{:S(2)}, u32[]{:S(2)}) collective-permute-start(bf16[2064,128]{1,0:T(8,128)(2,1)S(1)} %broadcast_select_fusion), channel_id=1, source_target_pairs={{16,0},{17,1},{18,2},{19,3},{20,4},{21,5},{22,6},{23,7},{24,8},{25... | collective-permute-start | bytes 1585160 | tf_op jit(solution)/shard_map/ppermute | solution.py:266
  35.2 12.5 %collective-permute-start.5 = (bf16[2064,128]{1,0:T(8,128)(2,1)S(1)}, bf16[2064,128]{1,0:T(8,128)(2,1)S(1)}, u32[]{:S(2)}, u32[]{:S(2)}) collective-permute-start(bf16[2064,128]{1,0:T(8,128)(2,1)S(1)} %broadcast_select_fusion.1.refs_0_), channel_id=1, source_target_pairs={{1,0},{0,1},{3,2},{2,3},{5,4},{4,5},{7,6},{6,7},{9,8},{8,9},{11,10... | collective-permute-start | bytes 1585160 | tf_op jit(solution)/shard_map/ppermute | solution.py:266
  35.7 14.5 %collective-permute-start.16 = (bf16[2064,128]{1,0:T(8,128)(2,1)S(1)}, bf16[2064,128]{1,0:T(8,128)(2,1)S(1)}, u32[]{:S(2)}, u32[]{:S(2)}) collective-permute-start(bf16[2064,128]{1,0:T(8,128)(2,1)S(1)} %pad_maximum_fusion.refs_8_), channel_id=1, source_target_pairs={{8,0},{9,1},{10,2},{11,3},{12,4},{13,5},{14,6},{15,7},{0,8},{1,9},... | collective-permute-start | bytes 1585160 | tf_op jit(solution)/shard_map/ppermute | solution.py:266
  35.7 15.2 %collective-permute-start.18 = (bf16[2064,128]{1,0:T(8,128)(2,1)S(1)}, bf16[2064,128]{1,0:T(8,128)(2,1)S(1)}, u32[]{:S(2)}, u32[]{:S(2)}) collective-permute-start(bf16[2064,128]{1,0:T(8,128)(2,1)S(1)} %collective-permute-done.3.refs_10_), channel_id=1, source_target_pairs={{8,0},{9,1},{10,2},{11,3},{12,4},{13,5},{14,6},{15,7},{0,8},{1,9},... | collective-permute-start | bytes 1585160 | tf_op jit(solution)/shard_map/ppermute | solution.py:266
  46.5 27.0 %copy-start.6 = (bf16[2064,128]{1,0:T(8,128)(2,1)}, bf16[2064,128]{1,0:T(8,128)(2,1)S(1)}, u32[]{:S(2)}) copy-start(bf16[2064,128]{1,0:T(8,128)(2,1)S(1)} %collective-permute-done.6.refs_2_) | copy-start | bytes 1585156
  47.6 25.8 %copy-start.7 = (bf16[2064,128]{1,0:T(8,128)(2,1)}, bf16[2064,128]{1,0:T(8,128)(2,1)S(1)}, u32[]{:S(2)}) copy-start(bf16[2064,128]{1,0:T(8,128)(2,1)S(1)} %collective-permute-done.5.refs_1_) | copy-start | bytes 1585156
  47.6 15.1 %collective-permute-start.8 = (bf16[2064,128]{1,0:T(8,128)(2,1)S(1)}, bf16[2064,128]{1,0:T(8,128)(2,1)}, u32[]{:S(2)}, u32[]{:S(2)}) collective-permute-start(bf16[2064,128]{1,0:T(8,128)(2,1)S(1)} %collective-permute-done.6.refs_2_), channel_id=1, source_target_pairs={{1,0},{0,1},{3,2},{2,3},{5,4},{4,5},{7,6},{6,7},{9,8},{8,9},{11,10... | collective-permute-start | bytes 1585160 | tf_op jit(solution)/shard_map/ppermute | solution.py:266
  48.2 20.5 %collective-permute-start.11 = (bf16[2064,128]{1,0:T(8,128)(2,1)S(1)}, bf16[2064,128]{1,0:T(8,128)(2,1)S(1)}, u32[]{:S(2)}, u32[]{:S(2)}) collective-permute-start(bf16[2064,128]{1,0:T(8,128)(2,1)S(1)} %collective-permute-done.7.refs_16_), channel_id=1, source_target_pairs={{16,0},{17,1},{18,2},{19,3},{21,4},{20,5},{23,6},{22,7},{24,8},{25... | collective-permute-start | bytes 1585160 | tf_op jit(solution)/shard_map/ppermute | solution.py:266
  49.6 21.2 %collective-permute-start.10 = (bf16[2064,128]{1,0:T(8,128)(2,1)S(1)}, bf16[2064,128]{1,0:T(8,128)(2,1)S(1)}, u32[]{:S(2)}, u32[]{:S(2)}) collective-permute-start(bf16[2064,128]{1,0:T(8,128)(2,1)S(1)} %collective-permute-done.7.refs_16_), channel_id=1, source_target_pairs={{16,0},{17,1},{18,2},{19,3},{20,4},{21,5},{22,6},{23,7},{24,8},{25... | collective-permute-start | bytes 1585160 | tf_op jit(solution)/shard_map/ppermute | solution.py:266
  50.2 23.3 %copy-start.8 = (bf16[2064,128]{1,0:T(8,128)(2,1)}, bf16[2064,128]{1,0:T(8,128)(2,1)S(1)}, u32[]{:S(2)}) copy-start(bf16[2064,128]{1,0:T(8,128)(2,1)S(1)} %collective-permute-done.16.refs_12_) | copy-start | bytes 1585156
  50.2 20.6 %collective-permute-start.9 = (bf16[2064,128]{1,0:T(8,128)(2,1)S(1)}, bf16[2064,128]{1,0:T(8,128)(2,1)S(1)}, u32[]{:S(2)}, u32[]{:S(2)}) collective-permute-start(bf16[2064,128]{1,0:T(8,128)(2,1)S(1)} %collective-permute-done.7.refs_16_), channel_id=1, source_target_pairs={{0,0},{1,1},{2,2},{3,3},{5,4},{4,5},{7,6},{6,7},{8,8},{9,9},{10,10... | collective-permute-start | bytes 1585160 | tf_op jit(solution)/shard_map/ppermute | solution.py:266
  50.9 22.5 %copy-start.9 = (bf16[2064,128]{1,0:T(8,128)(2,1)}, bf16[2064,128]{1,0:T(8,128)(2,1)S(1)}, u32[]{:S(2)}) copy-start(bf16[2064,128]{1,0:T(8,128)(2,1)S(1)} %collective-permute-done.18.refs_14_) | copy-start | bytes 1585156
  50.9 20.4 %collective-permute-start.17 = (bf16[2064,128]{1,0:T(8,128)(2,1)S(1)}, bf16[2064,128]{1,0:T(8,128)(2,1)S(1)}, u32[]{:S(2)}, u32[]{:S(2)}) collective-permute-start(bf16[2064,128]{1,0:T(8,128)(2,1)S(1)} %collective-permute-done.2.refs_9_), channel_id=1, source_target_pairs={{8,0},{9,1},{10,2},{11,3},{12,4},{13,5},{14,6},{15,7},{0,8},{1,9},... | collective-permute-start | bytes 1585160 | tf_op jit(solution)/shard_map/ppermute | solution.py:266
  62.7 9.4 %collective-permute-start.19 = (bf16[2064,128]{1,0:T(8,128)(2,1)}, bf16[2064,128]{1,0:T(8,128)(2,1)S(1)}, u32[]{:S(2)}, u32[]{:S(2)}) collective-permute-start(bf16[2064,128]{1,0:T(8,128)(2,1)} %collective-permute-done.4.refs_11_), channel_id=1, source_target_pairs={{8,0},{9,1},{10,2},{11,3},{12,4},{13,5},{14,6},{15,7},{0,8},{1,9},... | collective-permute-start | bytes 1585160 | tf_op jit(solution)/shard_map/ppermute | solution.py:266
  68.6 3.5 %collective-permute-start.12 = (bf16[2064,128]{1,0:T(8,128)(2,1)S(1)}, bf16[2064,128]{1,0:T(8,128)(2,1)S(1)}, u32[]{:S(2)}, u32[]{:S(2)}) collective-permute-start(bf16[2064,128]{1,0:T(8,128)(2,1)S(1)} %broadcast_select_fusion.1.refs_0_), channel_id=1, source_target_pairs={{8,0},{9,1},{10,2},{11,3},{12,4},{13,5},{14,6},{15,7},{0,8},{1,9},... | collective-permute-start | bytes 1585160 | tf_op jit(solution)/shard_map/ppermute | solution.py:266
  70.8 1.9 %collective-permute-start.14 = (bf16[2064,128]{1,0:T(8,128)(2,1)S(1)}, bf16[2064,128]{1,0:T(8,128)(2,1)S(1)}, u32[]{:S(2)}, u32[]{:S(2)}) collective-permute-start(bf16[2064,128]{1,0:T(8,128)(2,1)S(1)} %collective-permute-done.6.refs_2_), channel_id=1, source_target_pairs={{8,0},{9,1},{10,2},{11,3},{12,4},{13,5},{14,6},{15,7},{0,8},{1,9},... | collective-permute-start | bytes 1585160 | tf_op jit(solution)/shard_map/ppermute | solution.py:266
  70.8 2.7 %collective-permute-start.13 = (bf16[2064,128]{1,0:T(8,128)(2,1)S(1)}, bf16[2064,128]{1,0:T(8,128)(2,1)S(1)}, u32[]{:S(2)}, u32[]{:S(2)}) collective-permute-start(bf16[2064,128]{1,0:T(8,128)(2,1)S(1)} %collective-permute-done.5.refs_1_), channel_id=1, source_target_pairs={{8,0},{9,1},{10,2},{11,3},{12,4},{13,5},{14,6},{15,7},{0,8},{1,9},... | collective-permute-start | bytes 1585160 | tf_op jit(solution)/shard_map/ppermute | solution.py:266
  71.3 0.8 copy-start.10
  71.3 4.4 %collective-permute-start.20 = (bf16[2064,128]{1,0:T(8,128)(2,1)S(1)}, bf16[2064,128]{1,0:T(8,128)(2,1)S(1)}, u32[]{:S(2)}, u32[]{:S(2)}) collective-permute-start(bf16[2064,128]{1,0:T(8,128)(2,1)S(1)} %collective-permute-done.7.refs_16_), channel_id=1, source_target_pairs={{8,0},{9,1},{10,2},{11,3},{12,4},{13,5},{14,6},{15,7},{0,8},{1,9},... | collective-permute-start | bytes 1585160 | tf_op jit(solution)/shard_map/ppermute | solution.py:266
  72.1 1.4 %copy-start.11 = (bf16[2064,128]{1,0:T(8,128)(2,1)}, bf16[2064,128]{1,0:T(8,128)(2,1)S(1)}, u32[]{:S(2)}) copy-start(bf16[2064,128]{1,0:T(8,128)(2,1)S(1)} %collective-permute-done.19.refs_15_) | copy-start | bytes 1585156
  72.1 4.5 %collective-permute-start.15 = (bf16[2064,128]{1,0:T(8,128)(2,1)}, bf16[2064,128]{1,0:T(8,128)(2,1)S(1)}, u32[]{:S(2)}, u32[]{:S(2)}) collective-permute-start(bf16[2064,128]{1,0:T(8,128)(2,1)} %collective-permute-done.8.refs_3_), channel_id=1, source_target_pairs={{8,0},{9,1},{10,2},{11,3},{12,4},{13,5},{14,6},{15,7},{0,8},{1,9},... | collective-permute-start | bytes 1585160 | tf_op jit(solution)/shard_map/ppermute | solution.py:266
  72.1 1.4 %copy-start.12 = (bf16[2064,128]{1,0:T(8,128)(2,1)}, bf16[2064,128]{1,0:T(8,128)(2,1)S(1)}, u32[]{:S(2)}) copy-start(bf16[2064,128]{1,0:T(8,128)(2,1)S(1)} %collective-permute-done.12.refs_4_) | copy-start | bytes 1585156
  72.1 3.7 %collective-permute-start.23 = (bf16[2064,128]{1,0:T(8,128)(2,1)S(1)}, bf16[2064,128]{1,0:T(8,128)(2,1)}, u32[]{:S(2)}, u32[]{:S(2)}) collective-permute-start(bf16[2064,128]{1,0:T(8,128)(2,1)S(1)} %collective-permute-done.11.refs_19_), channel_id=1, source_target_pairs={{8,0},{9,1},{10,2},{11,3},{12,4},{13,5},{14,6},{15,7},{0,8},{1,9},... | collective-permute-start | bytes 1585160 | tf_op jit(solution)/shard_map/ppermute | solution.py:266
  72.7 0.8 copy-start.13
  72.7 3.9 %collective-permute-start.22 = (bf16[2064,128]{1,0:T(8,128)(2,1)S(1)}, bf16[2064,128]{1,0:T(8,128)(2,1)}, u32[]{:S(2)}, u32[]{:S(2)}) collective-permute-start(bf16[2064,128]{1,0:T(8,128)(2,1)S(1)} %collective-permute-done.10.refs_18_), channel_id=1, source_target_pairs={{8,0},{9,1},{10,2},{11,3},{12,4},{13,5},{14,6},{15,7},{0,8},{1,9},... | collective-permute-start | bytes 1585160 | tf_op jit(solution)/shard_map/ppermute | solution.py:266
  73.5 0.8 copy-start.14
  74.3 3.0 %collective-permute-start.21 = (bf16[2064,128]{1,0:T(8,128)(2,1)S(1)}, bf16[2064,128]{1,0:T(8,128)(2,1)}, u32[]{:S(2)}, u32[]{:S(2)}) collective-permute-start(bf16[2064,128]{1,0:T(8,128)(2,1)S(1)} %collective-permute-done.9.refs_17_), channel_id=1, source_target_pairs={{8,0},{9,1},{10,2},{11,3},{12,4},{13,5},{14,6},{15,7},{0,8},{1,9},... | collective-permute-start | bytes 1585160 | tf_op jit(solution)/shard_map/ppermute | solution.py:266

commit v6 on v5

--- a/solution.py
+++ b/solution.py
@@ -9,7 +9,7 @@
 from jax.sharding import PartitionSpec as P
 
 KEY_ROWS = 16
-SLOTS = 32
+SLOTS = 48
 TOGETHER = 8
 FIRST = 4
 BITS = 8

time: 87.1 us -> 87 us (level)
  no operation moved by 1% of the time
where the time goes in v6:
time: 87 us; the launch traced here: 86.1 us
  waiting for transfers between devices  53.7 us (62%)
  starting transfers between devices  18.5 us (21%)
  Pallas kernels  8.76 us (10%)
  other arithmetic  2.27 us (3%)
  local copies, waits for them, and re-layouts  2 us (2%)
    ppermute x21, waiting for transfers between devices, move(): return lax.ppermute(value, ('row', 'col', 'depth'), pairs)  31.1 us
    ppermute x3, waiting for transfers between devices, next_col(): lax.ppermute(value, 'col', [(i, (i + step) % n_col) for i in range(n_col)])  22.6 us
    ppermute x21, starting transfers between devices, move(): return lax.ppermute(value, ('row', 'col', 'depth'), pairs)  13.6 us
    pallas_call x1, Pallas kernels, products(): pl.pallas_call(functools.partial(product_kernel, plan, places, slots), gr...  8.76 us
    ppermute x3, starting transfers between devices, next_col(): lax.ppermute(value, 'col', [(i, (i + step) % n_col) for i in range(n_col)])  4.95 us
  transfers between devices with their start and end apart: 24, of which 15 were waited for; matrix products, arithmetic and copies ran while one was open for 1% of the time, Pallas kernels for 0%

profile of v6, /device:TPU:0, one launch (start us, length us, event | category | flops | bytes accessed | tf_op | source)
XLA Modules:
  0.0 86.1 jit_solution(4091267933683568144)
XLA Ops:
  0.0 0.7 convert_element_type.7
  0.7 0.1 reshape.15
  0.8 1.4 %pad_maximum_fusion.refs_8_ = bf16[2064,128]{1,0:T(8,128)(2,1)S(1)} fusion(bf16[2048,128]{1,0:T(8,128)(2,1)} %bitcast.9, bf16[2064]{0:T(1024)(128)(2,1)S(1)} %pad.6.clone), kind=kLoop, calls=%fused_computation | loop fusion | flops 1056768 | bytes 1056800 | tf_op jit(solution)/shard_map/concatenate | solution.py:237
  2.2 0.0 copy-start.2
  2.2 3.0 %collective-permute-start.2 = (bf16[2064,128]{1,0:T(8,128)(2,1)S(1)}, bf16[2064,128]{1,0:T(8,128)(2,1)S(1)}, u32[]{:S(2)}, u32[]{:S(2)}) collective-permute-start(bf16[2064,128]{1,0:T(8,128)(2,1)S(1)} %pad_maximum_fusion.refs_8_), channel_id=1, source_target_pairs={{1,0},{0,1},{3,2},{2,3},{5,4},{4,5},{7,6},{6,7},{9,8},{8,9},{11,10... | collective-permute-start | bytes 1585160 | tf_op jit(solution)/shard_map/ppermute | solution.py:266
  5.2 1.6 %collective-permute-start.1 = (bf16[2064,128]{1,0:T(8,128)(2,1)S(1)}, bf16[2064,128]{1,0:T(8,128)(2,1)S(1)}, u32[]{:S(2)}, u32[]{:S(2)}) collective-permute-start(bf16[2064,128]{1,0:T(8,128)(2,1)S(1)} %pad_maximum_fusion.refs_8_), channel_id=1, source_target_pairs={{0,2},{2,4},{4,6},{6,0},{1,3},{3,5},{5,7},{7,1},{8,10},{10,12},{12... | collective-permute-start | bytes 1585160 | tf_op jit(solution)/shard_map/ppermute | solution.py:257
  6.8 2.2 %collective-permute-start = (bf16[2064,128]{1,0:T(8,128)(2,1)S(1)}, bf16[2064,128]{1,0:T(8,128)(2,1)S(1)}, u32[]{:S(2)}, u32[]{:S(2)}) collective-permute-start(bf16[2064,128]{1,0:T(8,128)(2,1)S(1)} %pad_maximum_fusion.refs_8_), channel_id=1, source_target_pairs={{0,6},{2,0},{4,2},{6,4},{1,7},{3,1},{5,3},{7,5},{8,14},{10,8},{12,... | collective-permute-start | bytes 1585160 | tf_op jit(solution)/shard_map/ppermute | solution.py:257
  9.0 1.5 %collective-permute-start.3 = (bf16[2064,128]{1,0:T(8,128)(2,1)S(1)}, bf16[2064,128]{1,0:T(8,128)(2,1)S(1)}, u32[]{:S(2)}, u32[]{:S(2)}) collective-permute-start(bf16[2064,128]{1,0:T(8,128)(2,1)S(1)} %pad_maximum_fusion.refs_8_), channel_id=1, source_target_pairs={{16,0},{17,1},{18,2},{19,3},{20,4},{21,5},{22,6},{23,7},{24,8},{25... | collective-permute-start | bytes 1585160 | tf_op jit(solution)/shard_map/ppermute | solution.py:266
  10.5 6.7 %collective-permute-done.2.refs_9_ = bf16[2064,128]{1,0:T(8,128)(2,1)S(1)} collective-permute-done((bf16[2064,128]{1,0:T(8,128)(2,1)S(1)}, bf16[2064,128]{1,0:T(8,128)(2,1)S(1)}, u32[]{:S(2)}, u32[]{:S(2)}) %collective-permute-start.2) | collective-permute-done | bytes 528416 | tf_op jit(solution)/shard_map/ppermute | solution.py:266
  17.2 1.8 %collective-permute-start.4 = (bf16[2064,128]{1,0:T(8,128)(2,1)S(1)}, bf16[2064,128]{1,0:T(8,128)(2,1)}, u32[]{:S(2)}, u32[]{:S(2)}) collective-permute-start(bf16[2064,128]{1,0:T(8,128)(2,1)S(1)} %collective-permute-done.2.refs_9_), channel_id=1, source_target_pairs={{16,0},{17,1},{18,2},{19,3},{20,4},{21,5},{22,6},{23,7},{24,8},{25... | collective-permute-start | bytes 1585160 | tf_op jit(solution)/shard_map/ppermute | solution.py:266
  19.0 3.0 %collective-permute-done.1 = bf16[2064,128]{1,0:T(8,128)(2,1)S(1)} collective-permute-done((bf16[2064,128]{1,0:T(8,128)(2,1)S(1)}, bf16[2064,128]{1,0:T(8,128)(2,1)S(1)}, u32[]{:S(2)}, u32[]{:S(2)}) %collective-permute-start.1) | collective-permute-done | bytes 528416 | tf_op jit(solution)/shard_map/ppermute | solution.py:257
  22.0 9.3 %collective-permute-done = bf16[2064,128]{1,0:T(8,128)(2,1)S(1)} collective-permute-done((bf16[2064,128]{1,0:T(8,128)(2,1)S(1)}, bf16[2064,128]{1,0:T(8,128)(2,1)S(1)}, u32[]{:S(2)}, u32[]{:S(2)}) %collective-permute-start) | collective-permute-done | bytes 528416 | tf_op jit(solution)/shard_map/ppermute | solution.py:257
  31.3 1.1 %collective-permute-start.7 = (bf16[2064,128]{1,0:T(8,128)(2,1)S(1)}, bf16[2064,128]{1,0:T(8,128)(2,1)S(1)}, u32[]{:S(2)}, u32[]{:S(2)}) collective-permute-start(bf16[2064,128]{1,0:T(8,128)(2,1)S(1)} %collective-permute-done.1), channel_id=1, source_target_pairs={{0,2},{2,4},{4,6},{6,0},{1,3},{3,5},{5,7},{7,1},{8,10},{10,12},{12... | collective-permute-start | bytes 1585160 | tf_op jit(solution)/shard_map/ppermute | solution.py:257
  32.4 0.0 collective-permute-done.3.refs_10_
  32.4 1.0 %collective-permute-done.4.refs_11_ = bf16[2064,128]{1,0:T(8,128)(2,1)} collective-permute-done((bf16[2064,128]{1,0:T(8,128)(2,1)S(1)}, bf16[2064,128]{1,0:T(8,128)(2,1)}, u32[]{:S(2)}, u32[]{:S(2)}) %collective-permute-start.4) | collective-permute-done | bytes 528416 | tf_op jit(solution)/shard_map/ppermute | solution.py:266
  33.4 0.1 broadcast_select_fusion.1.refs_0_
  33.5 0.0 copy-start.3
  33.5 0.0 copy-start.1
  33.5 0.1 broadcast_select_fusion
  33.6 1.6 %collective-permute-start.6 = (bf16[2064,128]{1,0:T(8,128)(2,1)S(1)}, bf16[2064,128]{1,0:T(8,128)(2,1)S(1)}, u32[]{:S(2)}, u32[]{:S(2)}) collective-permute-start(bf16[2064,128]{1,0:T(8,128)(2,1)S(1)} %broadcast_select_fusion), channel_id=1, source_target_pairs={{16,0},{17,1},{18,2},{19,3},{20,4},{21,5},{22,6},{23,7},{24,8},{25... | collective-permute-start | bytes 1585160 | tf_op jit(solution)/shard_map/ppermute | solution.py:266
  35.2 0.5 collective-permute-start.5
  35.7 0.0 collective-permute-start.16
  35.7 0.0 copy-done.5
  35.7 0.5 collective-permute-start.18
  36.2 10.3 %collective-permute-done.7.refs_16_ = bf16[2064,128]{1,0:T(8,128)(2,1)S(1)} collective-permute-done((bf16[2064,128]{1,0:T(8,128)(2,1)S(1)}, bf16[2064,128]{1,0:T(8,128)(2,1)S(1)}, u32[]{:S(2)}, u32[]{:S(2)}) %collective-permute-start.7) | collective-permute-done | bytes 528416 | tf_op jit(solution)/shard_map/ppermute | solution.py:257
  46.5 0.0 collective-permute-done.6.refs_2_
  46.5 1.2 %collective-permute-done.5.refs_1_ = bf16[2064,128]{1,0:T(8,128)(2,1)S(1)} collective-permute-done((bf16[2064,128]{1,0:T(8,128)(2,1)S(1)}, bf16[2064,128]{1,0:T(8,128)(2,1)S(1)}, u32[]{:S(2)}, u32[]{:S(2)}) %collective-permute-start.5) | collective-permute-done | bytes 528416 | tf_op jit(solution)/shard_map/ppermute | solution.py:266
  47.6 0.5 collective-permute-start.8
  48.2 1.4 %collective-permute-start.11 = (bf16[2064,128]{1,0:T(8,128)(2,1)S(1)}, bf16[2064,128]{1,0:T(8,128)(2,1)S(1)}, u32[]{:S(2)}, u32[]{:S(2)}) collective-permute-start(bf16[2064,128]{1,0:T(8,128)(2,1)S(1)} %collective-permute-done.7.refs_16_), channel_id=1, source_target_pairs={{16,0},{17,1},{18,2},{19,3},{21,4},{20,5},{23,6},{22,7},{24,8},{25... | collective-permute-start | bytes 1585160 | tf_op jit(solution)/shard_map/ppermute | solution.py:266
  49.6 0.6 collective-permute-start.10
  50.2 0.0 collective-permute-done.16.refs_12_
  50.2 0.7 collective-permute-start.9
  50.9 0.0 collective-permute-done.18.refs_14_
  50.9 0.1 collective-permute-start.17
  51.0 11.7 %collective-permute-done.8.refs_3_ = bf16[2064,128]{1,0:T(8,128)(2,1)} collective-permute-done((bf16[2064,128]{1,0:T(8,128)(2,1)S(1)}, bf16[2064,128]{1,0:T(8,128)(2,1)}, u32[]{:S(2)}, u32[]{:S(2)}) %collective-permute-start.8) | collective-permute-done | bytes 528416 | tf_op jit(solution)/shard_map/ppermute | solution.py:266
  62.7 0.0 collective-permute-start.19
  62.7 5.9 %collective-permute-done.11.refs_19_ = bf16[2064,128]{1,0:T(8,128)(2,1)S(1)} collective-permute-done((bf16[2064,128]{1,0:T(8,128)(2,1)S(1)}, bf16[2064,128]{1,0:T(8,128)(2,1)S(1)}, u32[]{:S(2)}, u32[]{:S(2)}) %collective-permute-start.11) | collective-permute-done | bytes 528416 | tf_op jit(solution)/shard_map/ppermute | solution.py:266
  68.6 0.0 collective-permute-start.12
  68.6 2.2 %collective-permute-done.10.refs_18_ = bf16[2064,128]{1,0:T(8,128)(2,1)S(1)} collective-permute-done((bf16[2064,128]{1,0:T(8,128)(2,1)S(1)}, bf16[2064,128]{1,0:T(8,128)(2,1)S(1)}, u32[]{:S(2)}, u32[]{:S(2)}) %collective-permute-start.10) | collective-permute-done | bytes 528416 | tf_op jit(solution)/shard_map/ppermute | solution.py:266
  70.8 0.0 collective-permute-start.14
  70.8 0.0 collective-permute-done.9.refs_17_
  70.8 0.5 collective-permute-start.13
  71.3 0.0 collective-permute-done.17.refs_13_
  71.3 0.1 collective-permute-start.20
  71.4 0.7 copy-done.10
  72.1 0.0 collective-permute-done.19.refs_15_
  72.1 0.0 collective-permute-start.15
  72.1 0.0 collective-permute-done.12.refs_4_
  72.1 0.5 collective-permute-start.23
  72.6 0.1 collective-permute-done.14.refs_6_
  72.7 0.1 collective-permute-start.22
  72.8 0.6 collective-permute-done.13.refs_5_
  73.5 0.8 copy-done.14
  74.3 0.1 collective-permute-start.21
  75.1 0.1 constant_dynamic-slice_fusion
  75.2 0.1 copy.6
  75.3 0.1 reshape.13
  75.5 0.1 pad_add_fusion.info
  75.5 0.2 collective-permute-done.20.refs_20_
  75.7 0.1 collective-permute-done.23.refs_23_
  75.9 0.8 collective-permute-done.22.refs_22_
  76.6 0.0 collective-permute-done.15.refs_7_
  76.6 0.8 collective-permute-done.21.refs_21_
  77.4 8.8 %shard_map.55 = bf16[96,128,128]{2,1,0:T(8,128)(2,1)} custom-call(s32[4]{0:T(128)S(1)} %pad_add_fusion.info, s32[194]{0:T(256)S(1)} %pad.4.pos, s32[264]{0:T(512)S(1)} %copy-done.1, bf16[2064,128]{1,0:T(8,128)(2,1)} %copy-done.3, bf16[2064,128]{1,0:T(8,128)(2,1)} %copy-done.7, bf16[2064,128]{1,0:T(8,128)(2,1)} %copy-done.6, ...), custom_call_target="tpu_custom_call" | custom-call | flops 3221225472 | bytes 11534336 | tf_op jit(solution)/shard_map/pallas_call | solution.py:202
  (26 shorter events, 0.1 us)
Async XLA Ops:
  0.0 75.1 %copy-start = (s32[1,1,192,2]{2,3,1,0:T(2,128)S(1)}, s32[1,1,192,2]{2,3,1,0:T(2,128)}, u32[]{:S(2)}) copy-start(s32[1,1,192,2]{2,3,1,0:T(2,128)} %param.7) | copy-start | bytes 4612
  2.2 33.5 %copy-start.2 = (bf16[2064,128]{1,0:T(8,128)(2,1)}, bf16[2064,128]{1,0:T(8,128)(2,1)S(1)}, u32[]{:S(2)}) copy-start(bf16[2064,128]{1,0:T(8,128)(2,1)S(1)} %pad_maximum_fusion.refs_8_) | copy-start | bytes 1585156
  2.2 15.0 %collective-permute-start.2 = (bf16[2064,128]{1,0:T(8,128)(2,1)S(1)}, bf16[2064,128]{1,0:T(8,128)(2,1)S(1)}, u32[]{:S(2)}, u32[]{:S(2)}) collective-permute-start(bf16[2064,128]{1,0:T(8,128)(2,1)S(1)} %pad_maximum_fusion.refs_8_), channel_id=1, source_target_pairs={{1,0},{0,1},{3,2},{2,3},{5,4},{4,5},{7,6},{6,7},{9,8},{8,9},{11,10... | collective-permute-start | bytes 1585160 | tf_op jit(solution)/shard_map/ppermute | solution.py:266
  5.2 16.8 %collective-permute-start.1 = (bf16[2064,128]{1,0:T(8,128)(2,1)S(1)}, bf16[2064,128]{1,0:T(8,128)(2,1)S(1)}, u32[]{:S(2)}, u32[]{:S(2)}) collective-permute-start(bf16[2064,128]{1,0:T(8,128)(2,1)S(1)} %pad_maximum_fusion.refs_8_), channel_id=1, source_target_pairs={{0,2},{2,4},{4,6},{6,0},{1,3},{3,5},{5,7},{7,1},{8,10},{10,12},{12... | collective-permute-start | bytes 1585160 | tf_op jit(solution)/shard_map/ppermute | solution.py:257
  6.8 24.5 %collective-permute-start = (bf16[2064,128]{1,0:T(8,128)(2,1)S(1)}, bf16[2064,128]{1,0:T(8,128)(2,1)S(1)}, u32[]{:S(2)}, u32[]{:S(2)}) collective-permute-start(bf16[2064,128]{1,0:T(8,128)(2,1)S(1)} %pad_maximum_fusion.refs_8_), channel_id=1, source_target_pairs={{0,6},{2,0},{4,2},{6,4},{1,7},{3,1},{5,3},{7,5},{8,14},{10,8},{12,... | collective-permute-start | bytes 1585160 | tf_op jit(solution)/shard_map/ppermute | solution.py:257
  9.0 23.4 %collective-permute-start.3 = (bf16[2064,128]{1,0:T(8,128)(2,1)S(1)}, bf16[2064,128]{1,0:T(8,128)(2,1)S(1)}, u32[]{:S(2)}, u32[]{:S(2)}) collective-permute-start(bf16[2064,128]{1,0:T(8,128)(2,1)S(1)} %pad_maximum_fusion.refs_8_), channel_id=1, source_target_pairs={{16,0},{17,1},{18,2},{19,3},{20,4},{21,5},{22,6},{23,7},{24,8},{25... | collective-permute-start | bytes 1585160 | tf_op jit(solution)/shard_map/ppermute | solution.py:266
  17.2 33.7 %copy-start.4 = (bf16[2064,128]{1,0:T(8,128)(2,1)}, bf16[2064,128]{1,0:T(8,128)(2,1)S(1)}, u32[]{:S(2)}) copy-start(bf16[2064,128]{1,0:T(8,128)(2,1)S(1)} %collective-permute-done.2.refs_9_) | copy-start | bytes 1585156
  17.2 16.2 %collective-permute-start.4 = (bf16[2064,128]{1,0:T(8,128)(2,1)S(1)}, bf16[2064,128]{1,0:T(8,128)(2,1)}, u32[]{:S(2)}, u32[]{:S(2)}) collective-permute-start(bf16[2064,128]{1,0:T(8,128)(2,1)S(1)} %collective-permute-done.2.refs_9_), channel_id=1, source_target_pairs={{16,0},{17,1},{18,2},{19,3},{20,4},{21,5},{22,6},{23,7},{24,8},{25... | collective-permute-start | bytes 1585160 | tf_op jit(solution)/shard_map/ppermute | solution.py:266
  31.3 15.2 %collective-permute-start.7 = (bf16[2064,128]{1,0:T(8,128)(2,1)S(1)}, bf16[2064,128]{1,0:T(8,128)(2,1)S(1)}, u32[]{:S(2)}, u32[]{:S(2)}) collective-permute-start(bf16[2064,128]{1,0:T(8,128)(2,1)S(1)} %collective-permute-done.1), channel_id=1, source_target_pairs={{0,2},{2,4},{4,6},{6,0},{1,3},{3,5},{5,7},{7,1},{8,10},{10,12},{12... | collective-permute-start | bytes 1585160 | tf_op jit(solution)/shard_map/ppermute | solution.py:257
  32.4 3.3 %copy-start.5 = (bf16[2064,128]{1,0:T(8,128)(2,1)}, bf16[2064,128]{1,0:T(8,128)(2,1)S(1)}, u32[]{:S(2)}) copy-start(bf16[2064,128]{1,0:T(8,128)(2,1)S(1)} %collective-permute-done.3.refs_10_) | copy-start | bytes 1585156
  33.5 39.4 %copy-start.3 = (bf16[2064,128]{1,0:T(8,128)(2,1)}, bf16[2064,128]{1,0:T(8,128)(2,1)S(1)}, u32[]{:S(2)}) copy-start(bf16[2064,128]{1,0:T(8,128)(2,1)S(1)} %broadcast_select_fusion.1.refs_0_) | copy-start | bytes 1585156
  33.5 43.9 %copy-start.1 = (s32[264]{0:T(512)S(1)}, s32[264]{0:T(512)}, u32[]{:S(2)}) copy-start(s32[264]{0:T(512)} %constant.80.clone.table) | copy-start | bytes 3172
  33.6 12.9 %collective-permute-start.6 = (bf16[2064,128]{1,0:T(8,128)(2,1)S(1)}, bf16[2064,128]{1,0:T(8,128)(2,1)S(1)}, u32[]{:S(2)}, u32[]{:S(2)}) collective-permute-start(bf16[2064,128]{1,0:T(8,128)(2,1)S(1)} %broadcast_select_fusion), channel_id=1, source_target_pairs={{16,0},{17,1},{18,2},{19,3},{20,4},{21,5},{22,6},{23,7},{24,8},{25... | collective-permute-start | bytes 1585160 | tf_op jit(solution)/shard_map/ppermute | solution.py:266
  35.2 12.5 %collective-permute-start.5 = (bf16[2064,128]{1,0:T(8,128)(2,1)S(1)}, bf16[2064,128]{1,0:T(8,128)(2,1)S(1)}, u32[]{:S(2)}, u32[]{:S(2)}) collective-permute-start(bf16[2064,128]{1,0:T(8,128)(2,1)S(1)} %broadcast_select_fusion.1.refs_0_), channel_id=1, source_target_pairs={{1,0},{0,1},{3,2},{2,3},{5,4},{4,5},{7,6},{6,7},{9,8},{8,9},{11,10... | collective-permute-start | bytes 1585160 | tf_op jit(solution)/shard_map/ppermute | solution.py:266
  35.7 14.5 %collective-permute-start.16 = (bf16[2064,128]{1,0:T(8,128)(2,1)S(1)}, bf16[2064,128]{1,0:T(8,128)(2,1)S(1)}, u32[]{:S(2)}, u32[]{:S(2)}) collective-permute-start(bf16[2064,128]{1,0:T(8,128)(2,1)S(1)} %pad_maximum_fusion.refs_8_), channel_id=1, source_target_pairs={{8,0},{9,1},{10,2},{11,3},{12,4},{13,5},{14,6},{15,7},{0,8},{1,9},... | collective-permute-start | bytes 1585160 | tf_op jit(solution)/shard_map/ppermute | solution.py:266
  35.7 15.2 %collective-permute-start.18 = (bf16[2064,128]{1,0:T(8,128)(2,1)S(1)}, bf16[2064,128]{1,0:T(8,128)(2,1)S(1)}, u32[]{:S(2)}, u32[]{:S(2)}) collective-permute-start(bf16[2064,128]{1,0:T(8,128)(2,1)S(1)} %collective-permute-done.3.refs_10_), channel_id=1, source_target_pairs={{8,0},{9,1},{10,2},{11,3},{12,4},{13,5},{14,6},{15,7},{0,8},{1,9},... | collective-permute-start | bytes 1585160 | tf_op jit(solution)/shard_map/ppermute | solution.py:266
  46.5 27.0 %copy-start.6 = (bf16[2064,128]{1,0:T(8,128)(2,1)}, bf16[2064,128]{1,0:T(8,128)(2,1)S(1)}, u32[]{:S(2)}) copy-start(bf16[2064,128]{1,0:T(8,128)(2,1)S(1)} %collective-permute-done.6.refs_2_) | copy-start | bytes 1585156
  47.6 25.8 %copy-start.7 = (bf16[2064,128]{1,0:T(8,128)(2,1)}, bf16[2064,128]{1,0:T(8,128)(2,1)S(1)}, u32[]{:S(2)}) copy-start(bf16[2064,128]{1,0:T(8,128)(2,1)S(1)} %collective-permute-done.5.refs_1_) | copy-start | bytes 1585156
  47.6 15.1 %collective-permute-start.8 = (bf16[2064,128]{1,0:T(8,128)(2,1)S(1)}, bf16[2064,128]{1,0:T(8,128)(2,1)}, u32[]{:S(2)}, u32[]{:S(2)}) collective-permute-start(bf16[2064,128]{1,0:T(8,128)(2,1)S(1)} %collective-permute-done.6.refs_2_), channel_id=1, source_target_pairs={{1,0},{0,1},{3,2},{2,3},{5,4},{4,5},{7,6},{6,7},{9,8},{8,9},{11,10... | collective-permute-start | bytes 1585160 | tf_op jit(solution)/shard_map/ppermute | solution.py:266
  48.2 20.5 %collective-permute-start.11 = (bf16[2064,128]{1,0:T(8,128)(2,1)S(1)}, bf16[2064,128]{1,0:T(8,128)(2,1)S(1)}, u32[]{:S(2)}, u32[]{:S(2)}) collective-permute-start(bf16[2064,128]{1,0:T(8,128)(2,1)S(1)} %collective-permute-done.7.refs_16_), channel_id=1, source_target_pairs={{16,0},{17,1},{18,2},{19,3},{21,4},{20,5},{23,6},{22,7},{24,8},{25... | collective-permute-start | bytes 1585160 | tf_op jit(solution)/shard_map/ppermute | solution.py:266
  49.6 21.2 %collective-permute-start.10 = (bf16[2064,128]{1,0:T(8,128)(2,1)S(1)}, bf16[2064,128]{1,0:T(8,128)(2,1)S(1)}, u32[]{:S(2)}, u32[]{:S(2)}) collective-permute-start(bf16[2064,128]{1,0:T(8,128)(2,1)S(1)} %collective-permute-done.7.refs_16_), channel_id=1, source_target_pairs={{16,0},{17,1},{18,2},{19,3},{20,4},{21,5},{22,6},{23,7},{24,8},{25... | collective-permute-start | bytes 1585160 | tf_op jit(solution)/shard_map/ppermute | solution.py:266
  50.2 23.3 %copy-start.8 = (bf16[2064,128]{1,0:T(8,128)(2,1)}, bf16[2064,128]{1,0:T(8,128)(2,1)S(1)}, u32[]{:S(2)}) copy-start(bf16[2064,128]{1,0:T(8,128)(2,1)S(1)} %collective-permute-done.16.refs_12_) | copy-start | bytes 1585156
  50.2 20.6 %collective-permute-start.9 = (bf16[2064,128]{1,0:T(8,128)(2,1)S(1)}, bf16[2064,128]{1,0:T(8,128)(2,1)S(1)}, u32[]{:S(2)}, u32[]{:S(2)}) collective-permute-start(bf16[2064,128]{1,0:T(8,128)(2,1)S(1)} %collective-permute-done.7.refs_16_), channel_id=1, source_target_pairs={{0,0},{1,1},{2,2},{3,3},{5,4},{4,5},{7,6},{6,7},{8,8},{9,9},{10,10... | collective-permute-start | bytes 1585160 | tf_op jit(solution)/shard_map/ppermute | solution.py:266
  50.9 22.5 %copy-start.9 = (bf16[2064,128]{1,0:T(8,128)(2,1)}, bf16[2064,128]{1,0:T(8,128)(2,1)S(1)}, u32[]{:S(2)}) copy-start(bf16[2064,128]{1,0:T(8,128)(2,1)S(1)} %collective-permute-done.18.refs_14_) | copy-start | bytes 1585156
  50.9 20.4 %collective-permute-start.17 = (bf16[2064,128]{1,0:T(8,128)(2,1)S(1)}, bf16[2064,128]{1,0:T(8,128)(2,1)S(1)}, u32[]{:S(2)}, u32[]{:S(2)}) collective-permute-start(bf16[2064,128]{1,0:T(8,128)(2,1)S(1)} %collective-permute-done.2.refs_9_), channel_id=1, source_target_pairs={{8,0},{9,1},{10,2},{11,3},{12,4},{13,5},{14,6},{15,7},{0,8},{1,9},... | collective-permute-start | bytes 1585160 | tf_op jit(solution)/shard_map/ppermute | solution.py:266
  62.7 9.4 %collective-permute-start.19 = (bf16[2064,128]{1,0:T(8,128)(2,1)}, bf16[2064,128]{1,0:T(8,128)(2,1)S(1)}, u32[]{:S(2)}, u32[]{:S(2)}) collective-permute-start(bf16[2064,128]{1,0:T(8,128)(2,1)} %collective-permute-done.4.refs_11_), channel_id=1, source_target_pairs={{8,0},{9,1},{10,2},{11,3},{12,4},{13,5},{14,6},{15,7},{0,8},{1,9},... | collective-permute-start | bytes 1585160 | tf_op jit(solution)/shard_map/ppermute | solution.py:266
  68.6 3.5 %collective-permute-start.12 = (bf16[2064,128]{1,0:T(8,128)(2,1)S(1)}, bf16[2064,128]{1,0:T(8,128)(2,1)S(1)}, u32[]{:S(2)}, u32[]{:S(2)}) collective-permute-start(bf16[2064,128]{1,0:T(8,128)(2,1)S(1)} %broadcast_select_fusion.1.refs_0_), channel_id=1, source_target_pairs={{8,0},{9,1},{10,2},{11,3},{12,4},{13,5},{14,6},{15,7},{0,8},{1,9},... | collective-permute-start | bytes 1585160 | tf_op jit(solution)/shard_map/ppermute | solution.py:266
  70.8 1.9 %collective-permute-start.14 = (bf16[2064,128]{1,0:T(8,128)(2,1)S(1)}, bf16[2064,128]{1,0:T(8,128)(2,1)S(1)}, u32[]{:S(2)}, u32[]{:S(2)}) collective-permute-start(bf16[2064,128]{1,0:T(8,128)(2,1)S(1)} %collective-permute-done.6.refs_2_), channel_id=1, source_target_pairs={{8,0},{9,1},{10,2},{11,3},{12,4},{13,5},{14,6},{15,7},{0,8},{1,9},... | collective-permute-start | bytes 1585160 | tf_op jit(solution)/shard_map/ppermute | solution.py:266
  70.8 2.7 %collective-permute-start.13 = (bf16[2064,128]{1,0:T(8,128)(2,1)S(1)}, bf16[2064,128]{1,0:T(8,128)(2,1)S(1)}, u32[]{:S(2)}, u32[]{:S(2)}) collective-permute-start(bf16[2064,128]{1,0:T(8,128)(2,1)S(1)} %collective-permute-done.5.refs_1_), channel_id=1, source_target_pairs={{8,0},{9,1},{10,2},{11,3},{12,4},{13,5},{14,6},{15,7},{0,8},{1,9},... | collective-permute-start | bytes 1585160 | tf_op jit(solution)/shard_map/ppermute | solution.py:266
  71.3 0.8 copy-start.10
  71.3 4.4 %collective-permute-start.20 = (bf16[2064,128]{1,0:T(8,128)(2,1)S(1)}, bf16[2064,128]{1,0:T(8,128)(2,1)S(1)}, u32[]{:S(2)}, u32[]{:S(2)}) collective-permute-start(bf16[2064,128]{1,0:T(8,128)(2,1)S(1)} %collective-permute-done.7.refs_16_), channel_id=1, source_target_pairs={{8,0},{9,1},{10,2},{11,3},{12,4},{13,5},{14,6},{15,7},{0,8},{1,9},... | collective-permute-start | bytes 1585160 | tf_op jit(solution)/shard_map/ppermute | solution.py:266
  72.1 1.4 %copy-start.11 = (bf16[2064,128]{1,0:T(8,128)(2,1)}, bf16[2064,128]{1,0:T(8,128)(2,1)S(1)}, u32[]{:S(2)}) copy-start(bf16[2064,128]{1,0:T(8,128)(2,1)S(1)} %collective-permute-done.19.refs_15_) | copy-start | bytes 1585156
  72.1 4.5 %collective-permute-start.15 = (bf16[2064,128]{1,0:T(8,128)(2,1)}, bf16[2064,128]{1,0:T(8,128)(2,1)S(1)}, u32[]{:S(2)}, u32[]{:S(2)}) collective-permute-start(bf16[2064,128]{1,0:T(8,128)(2,1)} %collective-permute-done.8.refs_3_), channel_id=1, source_target_pairs={{8,0},{9,1},{10,2},{11,3},{12,4},{13,5},{14,6},{15,7},{0,8},{1,9},... | collective-permute-start | bytes 1585160 | tf_op jit(solution)/shard_map/ppermute | solution.py:266
  72.1 1.4 %copy-start.12 = (bf16[2064,128]{1,0:T(8,128)(2,1)}, bf16[2064,128]{1,0:T(8,128)(2,1)S(1)}, u32[]{:S(2)}) copy-start(bf16[2064,128]{1,0:T(8,128)(2,1)S(1)} %collective-permute-done.12.refs_4_) | copy-start | bytes 1585156
  72.1 3.7 %collective-permute-start.23 = (bf16[2064,128]{1,0:T(8,128)(2,1)S(1)}, bf16[2064,128]{1,0:T(8,128)(2,1)}, u32[]{:S(2)}, u32[]{:S(2)}) collective-permute-start(bf16[2064,128]{1,0:T(8,128)(2,1)S(1)} %collective-permute-done.11.refs_19_), channel_id=1, source_target_pairs={{8,0},{9,1},{10,2},{11,3},{12,4},{13,5},{14,6},{15,7},{0,8},{1,9},... | collective-permute-start | bytes 1585160 | tf_op jit(solution)/shard_map/ppermute | solution.py:266
  72.7 0.8 copy-start.13
  72.7 3.9 %collective-permute-start.22 = (bf16[2064,128]{1,0:T(8,128)(2,1)S(1)}, bf16[2064,128]{1,0:T(8,128)(2,1)}, u32[]{:S(2)}, u32[]{:S(2)}) collective-permute-start(bf16[2064,128]{1,0:T(8,128)(2,1)S(1)} %collective-permute-done.10.refs_18_), channel_id=1, source_target_pairs={{8,0},{9,1},{10,2},{11,3},{12,4},{13,5},{14,6},{15,7},{0,8},{1,9},... | collective-permute-start | bytes 1585160 | tf_op jit(solution)/shard_map/ppermute | solution.py:266
  73.5 0.8 copy-start.14
  74.3 3.0 %collective-permute-start.21 = (bf16[2064,128]{1,0:T(8,128)(2,1)S(1)}, bf16[2064,128]{1,0:T(8,128)(2,1)}, u32[]{:S(2)}, u32[]{:S(2)}) collective-permute-start(bf16[2064,128]{1,0:T(8,128)(2,1)S(1)} %collective-permute-done.9.refs_17_), channel_id=1, source_target_pairs={{8,0},{9,1},{10,2},{11,3},{12,4},{13,5},{14,6},{15,7},{0,8},{1,9},... | collective-permute-start | bytes 1585160 | tf_op jit(solution)/shard_map/ppermute | solution.py:266
